TPU v7x, 32 devices: a whole 2x2x4 slice. The times are simulated.
32 devices in a mesh: expert: 8 (over y, x, core), shard: 4 (over z).
Axes of the slice: x: 2, y: 2, z: 4, core: 2. Of those that a mesh axis runs over, the one named last changes fastest.
Arguments:
- hidden_in: bfloat16 [4096, 2048], P(('expert', 'shard')), may hold values from -6 to 6
- segments: int32 [4096], P(('expert', 'shard')), may hold values from 0 to 7, never falling along the last dimension, each value on 1 to 1024 neighbouring positions
- routes: int32 [4096, 8], P(('expert', 'shard')), may hold values from 0 to 15, all different within a row; in each aligned block of 128 rows (0 to 127, 128 to 255, ...) at most 96 rows name the same one
- norm_gains: bfloat16 [1, 2, 2048], P(None, None, 'shard'), may hold values from 0.099609375 to 1.8984375
- qk_gains: bfloat16 [1, 2, 128], P(None, None, 'shard'), may hold values from 0.099609375 to 1.8984375
- w_qkv: bfloat16 [1, 2048, 5120], P(None, 'shard'), may hold values from -0.125 to 0.125
- w_attn_out: bfloat16 [1, 4096, 2048], P(None, 'shard'), may hold values from -0.375 to 0.375
- w_router: bfloat16 [1, 2048, 16], P(None, 'shard'), may hold values from -0.0625 to 0.0625
- w_gate_up: bfloat16 [1, 16, 2048, 1536], P(None, 'expert', 'shard'), may hold values from -0.125 to 0.125
- w_down: bfloat16 [1, 16, 768, 2048], P(None, 'expert', None, 'shard'), may hold values from -0.875 to 0.875
- cotangent: bfloat16 [4096, 2048], P(('expert', 'shard')), may hold values from -6 to 6
Outputs:
- hidden_out: bfloat16 [4096, 2048], P(('expert', 'shard'))
- grad_hidden: float32 [4096, 2048], P(('expert', 'shard'))
- grad_norm_gains: float32 [1, 2, 2048], P(None, None, 'shard')
- grad_qk_gains: float32 [1, 2, 128], P(None, None, 'shard')
- grad_w_qkv: float32 [1, 2048, 5120], P(None, 'shard')
- grad_w_attn_out: float32 [1, 4096, 2048], P(None, 'shard')
- grad_w_router: float32 [1, 2048, 16], P(None, 'shard')
- grad_w_gate_up: float32 [1, 16, 2048, 1536], P(None, 'expert', 'shard')
- grad_w_down: float32 [1, 16, 768, 2048], P(None, 'expert', None, 'shard')
Inputs may be any that keep to these rules, and one draw needn't show every extreme that they name: `segments`: segment numbers never fall along the tokens; a document has at most 1024 tokens, and one has exactly that many. `routes`: A row names 8 different experts. Tokens of one device are the aligned blocks of 128 rows; within such a block no expert is named more than 96 times, and in some blocks an expert is named exactly 96 times.
All inputs are finite; a program needn't handle non-finite values.
Results may differ from a plain program's by a relative error of at most 0.024.
Values may be sent and summed in bfloat16 or wider, within the bound.
A program may use at most 320 MiB of HBM per device.

v0:
```python
import jax
import jax.numpy as jnp
from jax import lax
from jax.sharding import PartitionSpec as P

HEADS = 32
KV_HEADS = 4
HEAD_DIM = 128
TOP = 8


highest = lax.Precision.HIGHEST
eps_norm = 1e-06
rope_base = 1000000.0
neg_fill = -1e30


def rms_scale(value, gain_vec):
    return value * lax.rsqrt(jnp.mean(value * value, axis=-1, keepdims=True) + eps_norm) * gain_vec


def rotary_tables(position, head_width):
    half_width = head_width // 2
    frequency = rope_base ** (-(jnp.arange(half_width, dtype=jnp.float32) * 2.0) / head_width)
    angles = position[:, None] * frequency[None, :]
    return (jnp.cos(angles), jnp.sin(angles))


def apply_rotary(value, cos_table, sin_table):
    half_width = value.shape[-1] // 2
    lower_half = value[..., :half_width]
    upper_half = value[..., half_width:]
    cos_rows = cos_table[:, None, :]
    sin_rows = sin_table[:, None, :]
    return jnp.concatenate(
        [
            lower_half * cos_rows - upper_half * sin_rows,
            upper_half * cos_rows + lower_half * sin_rows,
        ],
        axis=-1,
    )


def post_qkv(qkv_out, qk_gain, cos_table, sin_table):
    length = qkv_out.shape[0]
    q_width = HEADS * HEAD_DIM
    kv_width = KV_HEADS * HEAD_DIM
    queries = qkv_out[:, :q_width].reshape(length, HEADS, HEAD_DIM)
    key_rows = qkv_out[:, q_width : q_width + kv_width].reshape(length, KV_HEADS, HEAD_DIM)
    values = qkv_out[:, q_width + kv_width :].reshape(length, KV_HEADS, HEAD_DIM)
    queries = apply_rotary(rms_scale(queries, qk_gain[0]), cos_table, sin_table)
    key_rows = apply_rotary(rms_scale(key_rows, qk_gain[1]), cos_table, sin_table)
    return (queries, key_rows, values)


def masked_scores(query_group, key_all, allowed, score_scale):
    scores = (
        jnp.einsum("tkgd,skd->kgts", query_group, key_all, preferred_element_type=jnp.float32)
        * score_scale
    )
    return jnp.where(allowed[None, None], scores, neg_fill)


def shards(
    hidden_in,
    segments,
    routes,
    norm_gains,
    qk_gains,
    w_qkv,
    w_attn_out,
    w_router,
    w_gate_up,
    w_down,
    cotangent,
):
    n_expert = lax.axis_size("expert")
    tok_count = hidden_in.shape[0]
    model_width = hidden_in.shape[1]
    experts_all = w_router.shape[2]
    exp_dev = w_gate_up.shape[1]
    layer_count = w_qkv.shape[0]
    capacity = 3 * tok_count * TOP // (2 * experts_all)
    head_group = HEADS // KV_HEADS
    score_scale = HEAD_DIM ** (-0.5)
    flat_routes = routes.reshape(-1)
    expert_ids = jnp.arange(experts_all, dtype=jnp.int32)
    one_hot = (flat_routes[:, None] == expert_ids[None, :]).astype(jnp.int32)
    slot_ranks = jnp.sum((jnp.cumsum(one_hot, axis=0) - one_hot) * one_hot, axis=1)
    slot_index = flat_routes * capacity + slot_ranks
    route_mask = (routes[:, :, None] == expert_ids[None, None, :]).astype(jnp.float32)
    query_index = lax.axis_index("shard") * tok_count + jnp.arange(tok_count, dtype=jnp.int32)
    cos_table, sin_table = rotary_tables(query_index.astype(jnp.float32), HEAD_DIM)
    residual = hidden_in.astype(jnp.float32)
    layer_index = 0
    gains_full = lax.all_gather(norm_gains[layer_index], "shard", axis=1, tiled=True)
    qk_full = lax.all_gather(qk_gains[layer_index], "shard", axis=1, tiled=True)
    qkv_weight = lax.all_gather(w_qkv[layer_index], "shard", axis=0, tiled=True)
    out_weight = lax.all_gather(w_attn_out[layer_index], "shard", axis=0, tiled=True)
    router_weight = lax.all_gather(w_router[layer_index], "shard", axis=0, tiled=True)
    gate_up_full = lax.all_gather(w_gate_up[layer_index], "shard", axis=1, tiled=True)
    down_full = lax.all_gather(w_down[layer_index], "shard", axis=2, tiled=True)
    norm_gain = gains_full.astype(jnp.float32)
    qk_gain = qk_full.astype(jnp.float32)
    expert_width = down_full.shape[1]
    attn_in = rms_scale(residual, norm_gain[0]).astype(jnp.bfloat16)
    qkv_out = jnp.dot(attn_in, qkv_weight, preferred_element_type=jnp.float32)
    queries, key_rows, values = post_qkv(qkv_out, qk_gain, cos_table, sin_table)
    query_group = queries.astype(jnp.bfloat16).reshape(tok_count, KV_HEADS, head_group, HEAD_DIM)
    key_all = lax.all_gather(key_rows.astype(jnp.bfloat16), "shard", axis=0, tiled=True)
    value_all = lax.all_gather(values.astype(jnp.bfloat16), "shard", axis=0, tiled=True)
    segment_all = lax.all_gather(segments, "shard", axis=0, tiled=True)
    key_index = jnp.arange(key_all.shape[0], dtype=jnp.int32)
    allowed = (key_index[None, :] <= query_index[:, None]) & (
        segment_all[None, :] == segments[:, None]
    )
    masked = masked_scores(query_group, key_all, allowed, score_scale)
    row_max = jnp.max(masked, axis=-1, keepdims=True)
    exp_scores = jnp.exp(masked - row_max)
    row_total = jnp.sum(exp_scores, axis=-1, keepdims=True)
    log_total = row_max + jnp.log(row_total)
    soft_low = (exp_scores / row_total).astype(jnp.bfloat16)
    attn_mix = (
        jnp.einsum("kgts,skd->tkgd", soft_low, value_all, preferred_element_type=jnp.float32)
        .reshape(tok_count, HEADS * HEAD_DIM)
        .astype(jnp.bfloat16)
    )
    middle = residual + jnp.dot(attn_mix, out_weight, preferred_element_type=jnp.float32)
    ffn_in = rms_scale(middle, norm_gain[1]).astype(jnp.bfloat16)
    router_logits = jnp.dot(ffn_in, router_weight, preferred_element_type=jnp.float32)
    chosen = jnp.take_along_axis(router_logits, routes, axis=1)
    chosen_exp = jnp.exp(chosen - jnp.max(chosen, axis=1, keepdims=True))
    route_weight = chosen_exp / jnp.sum(chosen_exp, axis=1, keepdims=True)
    send_rows = (
        jnp.zeros((experts_all * capacity, model_width), jnp.bfloat16)
        .at[slot_index]
        .set(jnp.repeat(ffn_in, TOP, axis=0))
        .reshape(n_expert, exp_dev, capacity, model_width)
    )
    received = lax.all_to_all(send_rows, "expert", split_axis=0, concat_axis=0, tiled=True)
    pre_gu = jnp.einsum(
        "necd,edf->necf", received, gate_up_full, preferred_element_type=jnp.float32
    )
    expert_pre_gate = pre_gu[..., :expert_width]
    expert_pre_up = pre_gu[..., expert_width:]
    expert_hidden = (expert_pre_gate * jax.nn.sigmoid(expert_pre_gate) * expert_pre_up).astype(
        jnp.bfloat16
    )
    result = jnp.einsum(
        "necf,efd->necd", expert_hidden, down_full, preferred_element_type=jnp.float32
    ).astype(jnp.bfloat16)
    pre_keep = pre_gu
    rows_keep = received
    returned = lax.all_to_all(result, "expert", split_axis=0, concat_axis=0, tiled=True).reshape(
        experts_all * capacity, model_width
    )
    picked = returned[slot_index].reshape(tok_count, TOP, model_width)
    kept_state = [
        (
            residual,
            norm_gain,
            qk_gain,
            qkv_weight,
            out_weight,
            router_weight,
            gate_up_full,
            down_full,
            attn_in,
            qkv_out,
            query_group,
            key_all,
            value_all,
            allowed,
            log_total,
            attn_mix,
            middle,
            ffn_in,
            route_weight,
            picked,
            pre_keep,
            rows_keep,
        )
    ]
    residual = middle + jnp.sum(route_weight[:, :, None] * picked.astype(jnp.float32), axis=1)
    hidden_out = residual.astype(jnp.bfloat16)
    upstream = cotangent.astype(jnp.float32)
    list_gains, list_qk, list_qkv, list_attn_out, list_router, list_gate_up, list_down = (
        [],
        [],
        [],
        [],
        [],
        [],
        [],
    )
    for layer_index in reversed(range(layer_count)):
        (
            layer_in,
            norm_gain,
            qk_gain,
            qkv_weight,
            out_weight,
            router_weight,
            gate_up_full,
            down_full,
            attn_in,
            qkv_out,
            query_group,
            key_all,
            value_all,
            allowed,
            log_total,
            attn_mix,
            middle,
            ffn_in,
            route_weight,
            picked,
            pre_keep,
            rows_keep,
        ) = kept_state[layer_index]
        expert_width = down_full.shape[1]
        weight_grad = jnp.sum(upstream[:, None, :] * picked.astype(jnp.float32), axis=-1)
        chosen_grad = route_weight * (
            weight_grad - jnp.sum(route_weight * weight_grad, axis=1, keepdims=True)
        )
        logit_grad = jnp.sum(chosen_grad[:, :, None] * route_mask, axis=1)
        grad_router = jnp.dot(
            ffn_in.astype(jnp.float32).T,
            logit_grad,
            precision=highest,
            preferred_element_type=jnp.float32,
        )
        router_back = jnp.dot(
            logit_grad,
            router_weight.astype(jnp.float32).T,
            precision=highest,
            preferred_element_type=jnp.float32,
        )
        out_grad = (
            (route_weight[:, :, None] * upstream[:, None, :])
            .astype(jnp.bfloat16)
            .reshape(tok_count * TOP, model_width)
        )
        send_grad = (
            jnp.zeros((experts_all * capacity, model_width), jnp.bfloat16)
            .at[slot_index]
            .set(out_grad)
            .reshape(n_expert, exp_dev, capacity, model_width)
        )
        recv_grad = lax.all_to_all(send_grad, "expert", split_axis=0, concat_axis=0, tiled=True)
        pre_gate = pre_keep[..., :expert_width]
        pre_up = pre_keep[..., expert_width:]
        sigmoid_gate = jax.nn.sigmoid(pre_gate)
        act_gate = pre_gate * sigmoid_gate
        hidden = (act_gate * pre_up).astype(jnp.bfloat16)
        grad_down = jnp.einsum(
            "necf,necd->efd", hidden, recv_grad, preferred_element_type=jnp.float32
        )
        hidden_grad = jnp.einsum(
            "necd,efd->necf", recv_grad, down_full, preferred_element_type=jnp.float32
        )
        gate_grad = hidden_grad * pre_up * sigmoid_gate * (1.0 + pre_gate * (1.0 - sigmoid_gate))
        up_grad = hidden_grad * act_gate
        gu_grad = jnp.concatenate([gate_grad, up_grad], axis=-1).astype(jnp.bfloat16)
        grad_gate_up = jnp.einsum(
            "necd,necf->edf", rows_keep, gu_grad, preferred_element_type=jnp.float32
        )
        rows_grad = jnp.einsum(
            "necf,edf->necd", gu_grad, gate_up_full, preferred_element_type=jnp.float32
        ).astype(jnp.bfloat16)
        back_grad = lax.all_to_all(
            rows_grad, "expert", split_axis=0, concat_axis=0, tiled=True
        ).reshape(experts_all * capacity, model_width)
        ffn_grad = (
            jnp.sum(
                back_grad[slot_index].reshape(tok_count, TOP, model_width).astype(jnp.float32),
                axis=1,
            )
            + router_back
        )
        gate_up_part, down_part = (
            lax.psum_scatter(
                grad_gate_up.astype(jnp.bfloat16), "shard", scatter_dimension=1, tiled=True
            ).astype(jnp.float32),
            lax.psum_scatter(
                grad_down.astype(jnp.bfloat16), "shard", scatter_dimension=2, tiled=True
            ).astype(jnp.float32),
        )
        list_gate_up.append(gate_up_part)
        list_down.append(down_part)
        _, norm_two_pull = jax.vjp(rms_scale, middle, norm_gain[1])
        middle_norm_grad, gain_two_grad = norm_two_pull(ffn_grad)
        middle_grad = upstream + middle_norm_grad
        branch_grad = middle_grad.astype(jnp.bfloat16)
        grad_attn_out = jnp.dot(attn_mix.T, branch_grad, preferred_element_type=jnp.float32)
        mix_grad = (
            jnp.dot(branch_grad, out_weight.T, preferred_element_type=jnp.float32)
            .astype(jnp.bfloat16)
            .reshape(tok_count, KV_HEADS, head_group, HEAD_DIM)
        )
        masked = masked_scores(query_group, key_all, allowed, score_scale)
        soft_full = jnp.exp(masked - log_total)
        soft_low = soft_full.astype(jnp.bfloat16)
        soft_grad = jnp.einsum(
            "tkgd,skd->kgts", mix_grad, value_all, preferred_element_type=jnp.float32
        )
        row_delta = jnp.sum(soft_full * soft_grad, axis=-1, keepdims=True)
        score_grad = (soft_full * (soft_grad - row_delta)).astype(jnp.bfloat16)
        query_grad = (
            jnp.einsum("kgts,skd->tkgd", score_grad, key_all, preferred_element_type=jnp.float32)
            * score_scale
        )
        key_part = (
            jnp.einsum(
                "kgts,tkgd->skd", score_grad, query_group, preferred_element_type=jnp.float32
            )
            * score_scale
        )
        value_part = jnp.einsum(
            "kgts,tkgd->skd", soft_low, mix_grad, preferred_element_type=jnp.float32
        )
        key_grad, value_grad = (
            lax.psum_scatter(
                key_part.astype(jnp.bfloat16), "shard", scatter_dimension=0, tiled=True
            ).astype(jnp.float32),
            lax.psum_scatter(
                value_part.astype(jnp.bfloat16), "shard", scatter_dimension=0, tiled=True
            ).astype(jnp.float32),
        )
        _, post_pull = jax.vjp(
            lambda qkv_value, gain_value: post_qkv(qkv_value, gain_value, cos_table, sin_table),
            qkv_out,
            qk_gain,
        )
        qkv_grad, qk_gain_grad = post_pull(
            (query_grad.reshape(tok_count, HEADS, HEAD_DIM), key_grad, value_grad)
        )
        qkv_low = qkv_grad.astype(jnp.bfloat16)
        grad_qkv = jnp.dot(attn_in.T, qkv_low, preferred_element_type=jnp.float32)
        attn_in_grad = jnp.dot(qkv_low, qkv_weight.T, preferred_element_type=jnp.float32)
        _, norm_one_pull = jax.vjp(rms_scale, layer_in, norm_gain[0])
        input_norm_grad, gain_one_grad = norm_one_pull(attn_in_grad)
        upstream = middle_grad + input_norm_grad
        gains_grad = jnp.stack([gain_one_grad, gain_two_grad])
        gains_part, qk_part, qkv_part, attn_out_part, router_part = (
            lax.psum_scatter(
                gains_grad.astype(jnp.bfloat16), "shard", scatter_dimension=1, tiled=True
            ).astype(jnp.float32),
            lax.psum_scatter(
                qk_gain_grad.astype(jnp.bfloat16), "shard", scatter_dimension=1, tiled=True
            ).astype(jnp.float32),
            lax.psum_scatter(
                grad_qkv.astype(jnp.bfloat16), "shard", scatter_dimension=0, tiled=True
            ).astype(jnp.float32),
            lax.psum_scatter(
                grad_attn_out.astype(jnp.bfloat16), "shard", scatter_dimension=0, tiled=True
            ).astype(jnp.float32),
            lax.psum_scatter(
                grad_router.astype(jnp.bfloat16), "shard", scatter_dimension=0, tiled=True
            ).astype(jnp.float32),
        )
        gains_part, qk_part, qkv_part, attn_out_part, router_part = (
            lax.psum(gains_part.astype(jnp.bfloat16), "expert").astype(jnp.float32),
            lax.psum(qk_part.astype(jnp.bfloat16), "expert").astype(jnp.float32),
            lax.psum(qkv_part.astype(jnp.bfloat16), "expert").astype(jnp.float32),
            lax.psum(attn_out_part.astype(jnp.bfloat16), "expert").astype(jnp.float32),
            lax.psum(router_part.astype(jnp.bfloat16), "expert").astype(jnp.float32),
        )
        list_gains.append(gains_part)
        list_qk.append(qk_part)
        list_qkv.append(qkv_part)
        list_attn_out.append(attn_out_part)
        list_router.append(router_part)
    return (
        hidden_out,
        upstream,
        jnp.stack(list_gains[::-1]),
        jnp.stack(list_qk[::-1]),
        jnp.stack(list_qkv[::-1]),
        jnp.stack(list_attn_out[::-1]),
        jnp.stack(list_router[::-1]),
        jnp.stack(list_gate_up[::-1]),
        jnp.stack(list_down[::-1]),
    )


def solution(mesh):
    in_specs = (
        P(("expert", "shard"), None),
        P(("expert", "shard")),
        P(("expert", "shard"), None),
        P(None, None, "shard"),
        P(None, None, "shard"),
        P(None, "shard", None),
        P(None, "shard", None),
        P(None, "shard", None),
        P(None, "expert", "shard", None),
        P(None, "expert", None, "shard"),
        P(("expert", "shard"), None),
    )
    out_specs = (
        P(("expert", "shard"), None),
        P(("expert", "shard"), None),
        P(None, None, "shard"),
        P(None, None, "shard"),
        P(None, "shard", None),
        P(None, "shard", None),
        P(None, "shard", None),
        P(None, "expert", "shard", None),
        P(None, "expert", None, "shard"),
    )
    return jax.shard_map(shards, mesh=mesh, in_specs=in_specs, out_specs=out_specs, check_vma=False)
```

profile of v0, /device:TPU:0, one launch (start us, length us, event | category | flops | bytes accessed | tf_op | source)
XLA Modules:
  0.0 2457.6 jit_solution(939479008603668972)
XLA Ops:
  9.9 14.9 all-gather.2
  29.9 11.1 all-gather.7
  41.0 23.5 all-gather
  67.9 301.5 %all-gather.13.cloned.1.call-done = bf16[1,2048,5120]{2,1,0:T(8,128)(2,1)} async-done(((bf16[1,512,5120]{2,1,0:T(8,128)(2,1)}), bf16[1,2048,5120]{2,1,0:T(8,128)(2,1)}) %all-gather.13.cloned.1.call-update) | async-done | bytes 20971536 | tf_op jit(solution)/shard_map/all_gather | solution.py:98
  369.3 8.8 fusion.2
  389.5 27.9 %all_gather.32 = bf16[512,4,128]{0,2,1:T(8,128)(2,1)S(1)} all-gather(bf16[128,4,128]{0,2,1:T(8,128)(2,1)S(1)} %bitcast.281), channel_id=1, replica_groups=mesh['expert'=8,'shard'=4] {'shard'}, dimensions={0}, use_global_device_ids=true | all-gather | bytes 655360 | tf_op jit(solution)/shard_map/all_gather | solution.py:111
  417.5 32.1 %all_gather.35 = bf16[512,4,128]{2,0,1:T(8,128)(2,1)S(1)} all-gather(bf16[128,4,128]{2,0,1:T(8,128)(2,1)S(1)} %pad_maximum_fusion.4), channel_id=1, replica_groups=mesh['expert'=8,'shard'=4] {'shard'}, dimensions={0}, use_global_device_ids=true | all-gather | bytes 655360 | tf_op jit(solution)/shard_map/all_gather | solution.py:110
  458.2 214.8 %all-gather.15.cloned.1.call-done = bf16[1,4096,2048]{2,1,0:T(8,128)(2,1)} async-done(((bf16[1,1024,2048]{2,1,0:T(8,128)(2,1)}), bf16[1,4096,2048]{2,1,0:T(8,128)(2,1)}) %all-gather.15.cloned.1.call-update) | async-done | bytes 16777232 | tf_op jit(solution)/shard_map/all_gather | solution.py:99
  673.0 8.5 multiply_reduce_fusion.5
  681.8 10.6 scatter_custom_fusion
  698.3 24.6 all-gather.4
  723.0 7.0 gather_fusion.2
  730.5 10.6 scatter_custom_fusion.1
  741.1 27.8 %all-to-all-done = bf16[8,2,96,2048]{3,2,1,0:T(8,128)(2,1)} async-done(((bf16[8,2,96,2048]{3,2,1,0:T(8,128)(2,1)}), bf16[8,2,96,2048]{3,2,1,0:T(8,128)(2,1)}, u32[]{:S(2)}, u32[]{:S(2)}) %all-to-all-start) | async-done | bytes 6291488 | tf_op jit(solution)/shard_map/all_to_all | solution.py:140
  773.9 118.3 %all-gather.17.cloned.1.call-done = bf16[1,2,2048,1536]{3,2,1,0:T(8,128)(2,1)} async-done(((bf16[1,2,512,1536]{3,2,1,0:T(8,128)(2,1)}), bf16[1,2,2048,1536]{3,2,1,0:T(8,128)(2,1)}) %all-gather.17.cloned.1.call-update) | async-done | bytes 12582928 | tf_op jit(solution)/shard_map/all_gather | solution.py:101
  892.1 16.9 fusion.28
  909.0 98.1 %all-gather.19.cloned.1.call-done = bf16[1,2,768,2048]{3,2,1,0:T(8,128)(2,1)} async-done(((bf16[1,2,768,512]{3,2,1,0:T(8,128)(2,1)}), bf16[1,2,768,2048]{3,2,1,0:T(8,128)(2,1)}) %all-gather.19.cloned.1.call-update) | async-done | bytes 6291472 | tf_op jit(solution)/shard_map/all_gather | solution.py:102
  1007.1 13.9 fusion.38
  1021.1 6.9 convert_bitcast_fusion.1
  1031.2 5.0 all-to-all-start.1
  1036.3 16.0 convert_bitcast_fusion
  1052.3 6.6 copy.298
  1058.9 49.0 %all-to-all-done.1 = bf16[8,2,96,2048]{3,2,1,0:T(8,128)(2,1)} async-done(((bf16[8,2,96,2048]{3,2,1,0:T(8,128)(2,1)}), bf16[8,2,96,2048]{3,2,1,0:T(8,128)(2,1)}, u32[]{:S(2)}, u32[]{:S(2)}) %all-to-all-start.1) | async-done | bytes 6291488 | tf_op jit(solution)/shard_map/all_to_all | solution.py:154
  1112.7 12.4 gather_fusion
  1125.1 6.0 fusion.13
  1131.2 53.0 %all-to-all-done.3 = bf16[8,2,96,2048]{3,2,1,0:T(8,128)(2,1)} async-done(((bf16[8,2,96,2048]{3,2,1,0:T(8,128)(2,1)}), bf16[8,2,96,2048]{3,2,1,0:T(8,128)(2,1)}, u32[]{:S(2)}, u32[]{:S(2)}) %all-to-all-start.3) | async-done | bytes 6291488 | tf_op jit(solution)/shard_map/all_to_all | solution.py:271
  1184.2 12.8 gather_fusion.1
  1197.0 5.2 convert_reduce_fusion
  1204.5 11.4 fusion.63
  1216.2 5.6 fusion.14
  1231.1 7.9 copy.301
  1245.0 8.1 convolution_convert_fusion.1
  1270.0 5.1 add_add_fusion
  1281.1 11.7 convolution_convert_fusion
  1293.6 12.7 fusion.73
  1308.6 9.9 bitcast_convert_fusion.1
  1318.5 16.2 bitcast_convert_fusion
  1334.8 217.5 %reduce-scatter.20.cloned.1.call-done = bf16[1024,2048]{1,0:T(8,128)(2,1)} async-done(((bf16[4096,2048]{1,0:T(8,128)(2,1)}), bf16[1024,2048]{1,0:T(8,128)(2,1)}) %reduce-scatter.20.cloned.1.call-update) | async-done | bytes 4194320 | tf_op jit(solution)/shard_map/reduce_scatter | solution.py:355
  1552.3 350.5 %reduce-scatter.18.cloned.1.call-done = bf16[512,5120]{1,0:T(8,128)(2,1)} async-done(((bf16[2048,5120]{1,0:T(8,128)(2,1)}), bf16[512,5120]{1,0:T(8,128)(2,1)}) %reduce-scatter.18.cloned.1.call-update) | async-done | bytes 5242896 | tf_op jit(solution)/shard_map/reduce_scatter | solution.py:352
  1905.3 20.7 reduce-scatter.32.cloned.1.call-done
  1926.7 21.9 reduce-scatter.30.cloned.1.call-done
  1949.6 19.1 reduce-scatter.22.cloned.1.call-done
  1968.7 23.7 all-reduce.9
  1994.2 86.2 %reduce-scatter.26.cloned.1.call-done = bf16[2,768,512]{2,1,0:T(8,128)(2,1)} async-done(((bf16[2,768,2048]{2,1,0:T(8,128)(2,1)}), bf16[2,768,512]{2,1,0:T(8,128)(2,1)}) %reduce-scatter.26.cloned.1.call-update) | async-done | bytes 1572880 | tf_op jit(solution)/shard_map/reduce_scatter | solution.py:285
  2084.0 211.2 %reduce-scatter.24.cloned.1.call-done = bf16[2,512,1536]{2,1,0:T(8,128)(2,1)} async-done(((bf16[2,2048,1536]{2,1,0:T(8,128)(2,1)}), bf16[2,512,1536]{2,1,0:T(8,128)(2,1)}) %reduce-scatter.24.cloned.1.call-update) | async-done | bytes 3145744 | tf_op jit(solution)/shard_map/reduce_scatter | solution.py:282
  2295.2 5.5 bitcast_convert_fusion.2
  2300.7 137.4 %all-reduce.13.cloned.1.call-done = (bf16[1,512,5120]{2,1,0:T(8,128)(2,1)}, bf16[1,1024,2048]{2,1,0:T(8,128)(2,1)}) async-done(((bf16[1,512,5120]{2,1,0:T(8,128)(2,1)}, bf16[1,1024,2048]{2,1,0:T(8,128)(2,1)}), (bf16[1,512,5120]{2,1,0:T(8,128)(2,1)}, bf16[1,1024,2048]{2,1,0:T(8,128)(2,1)})) %all-reduce.13.cloned.1.call-update) | async-done | bytes 9437200 | tf_op jit(solution)/shard_map/psum | solution.py:365
  2438.1 8.1 stack.56
  (263 shorter events, 108.0 us)
Async XLA Ops:
  7.2 362.2 %all-gather.13.cloned.1.call-start = ((), (), s32[]{:S(2)}) async-start(), calls=%async_computation.19 | async-start | bytes 26214400 | tf_op jit(solution)/shard_map/all_gather | solution.py:98
  7.9 22.0 copy-start.50
  7.9 33.0 %copy-start.51 = (bf16[1,2,512]{2,1,0:T(2,128)(2,1)S(1)}, bf16[1,2,512]{2,1,0:T(2,128)(2,1)}, u32[]{:S(2)}) copy-start(bf16[1,2,512]{2,1,0:T(2,128)(2,1)} %param.14) | copy-start | bytes 6148
  8.0 58.8 %copy-start.6 = (bf16[128,2048]{1,0:T(8,128)(2,1)S(1)}, bf16[128,2048]{1,0:T(8,128)(2,1)}, u32[]{:S(2)}) copy-start(bf16[128,2048]{1,0:T(8,128)(2,1)} %param.11) | copy-start | bytes 1572868
  8.0 665.1 %all-gather.15.cloned.1.call-start = ((), (), s32[]{:S(2)}) async-start(), calls=%async_computation.20 | async-start | bytes 20971520 | tf_op jit(solution)/shard_map/all_gather | solution.py:99
  8.7 883.4 %all-gather.17.cloned.1.call-start = ((), (), s32[]{:S(2)}) async-start(), calls=%async_computation.21 | async-start | bytes 15728640 | tf_op jit(solution)/shard_map/all_gather | solution.py:101
  66.7 319.7 %copy-start.48 = (f32[128]{0:T(128)}, f32[128]{0:T(128)S(1)}, u32[]{:S(2)}) copy-start(f32[128]{0:T(128)S(1)} %get-tuple-element.19) | copy-start | bytes 1540
  66.8 322.3 %copy-start.46 = (f32[128]{0:T(128)}, f32[128]{0:T(128)S(1)}, u32[]{:S(2)}) copy-start(f32[128]{0:T(128)S(1)} %get-tuple-element.20) | copy-start | bytes 1540
  67.0 302.4 %copy-start.41 = (f32[128]{0:T(128)}, f32[128]{0:T(128)S(1)}, u32[]{:S(2)}) copy-start(f32[128]{0:T(128)S(1)} %fusion.103) | copy-start | bytes 1540
  67.5 385.9 %copy-start.22 = (pred[128,512]{0,1:T(8,128)(4,1)}, pred[128,512]{0,1:T(8,128)(4,1)S(1)}, u32[]{:S(2)}) copy-start(pred[128,512]{0,1:T(8,128)(4,1)S(1)} %fusion.88) | copy-start | bytes 196612
  67.8 321.4 %copy-start.27 = (f32[128,64]{1,0:T(8,128)}, f32[128,64]{1,0:T(8,128)S(1)}, u32[]{:S(2)}) copy-start(f32[128,64]{1,0:T(8,128)S(1)} %get-tuple-element.47) | copy-start | bytes 98308
  67.8 321.4 %copy-start.29 = (f32[128,64]{1,0:T(8,128)}, f32[128,64]{1,0:T(8,128)S(1)}, u32[]{:S(2)}) copy-start(f32[128,64]{1,0:T(8,128)S(1)} %get-tuple-element.48) | copy-start | bytes 98308
  67.9 301.5 %copy-start.34 = (f32[1,1,2048]{2,1,0:T(1,128)}, f32[1,1,2048]{2,1,0:T(1,128)S(1)}, u32[]{:S(2)}) copy-start(f32[1,1,2048]{2,1,0:T(1,128)S(1)} %get-tuple-element.46) | copy-start | bytes 24580
  388.6 62.9 %copy-start.9 = (bf16[128,32,64]{2,0,1:T(8,128)(2,1)}, bf16[128,32,64]{2,0,1:T(8,128)(2,1)S(1)}, u32[]{:S(2)}) copy-start(bf16[128,32,64]{2,0,1:T(8,128)(2,1)S(1)} %copy.283) | copy-start | bytes 1572868
  389.0 62.4 %copy-start.11 = (bf16[128,32,64]{2,0,1:T(8,128)(2,1)}, bf16[128,32,64]{2,0,1:T(8,128)(2,1)S(1)}, u32[]{:S(2)}) copy-start(bf16[128,32,64]{2,0,1:T(8,128)(2,1)S(1)} %copy.284) | copy-start | bytes 1572868
  389.1 62.4 %copy-start.39 = (f32[128,4]{0,1:T(4,128)}, f32[128,4]{0,1:T(4,128)S(1)}, u32[]{:S(2)}) copy-start(f32[128,4]{0,1:T(4,128)S(1)} %fusion.102) | copy-start | bytes 6148
  417.5 36.0 %copy-start.26 = (bf16[512,4,128]{0,2,1:T(8,128)(2,1)}, bf16[512,4,128]{0,2,1:T(8,128)(2,1)S(1)}, u32[]{:S(2)}) copy-start(bf16[512,4,128]{0,2,1:T(8,128)(2,1)S(1)} %all_gather.32) | copy-start | bytes 1572868
  681.8 41.1 %copy-start.13 = (bf16[128,2048]{1,0:T(8,128)(2,1)}, bf16[128,2048]{1,0:T(8,128)(2,1)S(1)}, u32[]{:S(2)}) copy-start(bf16[128,2048]{1,0:T(8,128)(2,1)S(1)} %multiply_convert_fusion.1) | copy-start | bytes 1572868
  692.4 76.5 %all-to-all-start = ((bf16[8,2,96,2048]{3,2,1,0:T(8,128)(2,1)}), bf16[8,2,96,2048]{3,2,1,0:T(8,128)(2,1)}, u32[]{:S(2)}, u32[]{:S(2)}) async-start(bf16[8,2,96,2048]{3,2,1,0:T(8,128)(2,1)} %bitcast.262), calls=%async_computation | async-start | bytes 12582912 | tf_op jit(solution)/shard_map/all_to_all | solution.py:140
  697.3 309.8 %all-gather.19.cloned.1.call-start = ((), (), s32[]{:S(2)}) async-start(), calls=%async_computation.22 | async-start | bytes 7864320 | tf_op jit(solution)/shard_map/all_gather | solution.py:102
  768.9 238.2 %all-to-all-start.2 = ((bf16[8,2,96,2048]{3,2,1,0:T(8,128)(2,1)}), bf16[8,2,96,2048]{3,2,1,0:T(8,128)(2,1)}, u32[]{:S(2)}, u32[]{:S(2)}) async-start(bf16[8,2,96,2048]{3,2,1,0:T(8,128)(2,1)} %bitcast.263), calls=%async_computation.2 | async-start | bytes 12582912 | tf_op jit(solution)/shard_map/all_to_all | solution.py:250
  1007.1 13.9 copy-start.55
  1031.2 76.6 %all-to-all-start.1 = ((bf16[8,2,96,2048]{3,2,1,0:T(8,128)(2,1)}), bf16[8,2,96,2048]{3,2,1,0:T(8,128)(2,1)}, u32[]{:S(2)}, u32[]{:S(2)}) async-start(bf16[8,2,96,2048]{3,2,1,0:T(8,128)(2,1)} %copy.295), calls=%async_computation.1 | async-start | bytes 12582912 | tf_op jit(solution)/shard_map/all_to_all | solution.py:154
  1107.9 76.3 %all-to-all-start.3 = ((bf16[8,2,96,2048]{3,2,1,0:T(8,128)(2,1)}), bf16[8,2,96,2048]{3,2,1,0:T(8,128)(2,1)}, u32[]{:S(2)}, u32[]{:S(2)}) async-start(bf16[8,2,96,2048]{3,2,1,0:T(8,128)(2,1)} %copy.298), calls=%async_computation.3 | async-start | bytes 12582912 | tf_op jit(solution)/shard_map/all_to_all | solution.py:271
  1112.6 165.5 %reduce-scatter.16.cloned.1.call-start = ((), (), s32[]{:S(2)}) async-start(), calls=%async_computation.13 | async-start | bytes 655360 | tf_op jit(solution)/shard_map/reduce_scatter | solution.py:323
  1197.0 6.2 copy-start.19
  1197.0 6.2 copy-start.25
  1204.5 11.7 copy-start.23
  1216.2 6.1 slice-start.1
  1222.3 6.6 copy-start.10
  1222.3 6.6 copy-start.12
  1231.0 49.0 %reduce-scatter.28.cloned.1.call-start = ((), (), s32[]{:S(2)}) async-start(), calls=%async_computation.23 | async-start | bytes 655360
  1238.9 6.0 copy-start.15
  1244.9 307.4 %reduce-scatter.20.cloned.1.call-start = ((), (), s32[]{:S(2)}) async-start(), calls=%async_computation.15 | async-start | bytes 20971520 | tf_op jit(solution)/shard_map/reduce_scatter | solution.py:355
  1253.1 649.7 %reduce-scatter.18.cloned.1.call-start = ((), (), s32[]{:S(2)}) async-start(), calls=%async_computation.14 | async-start | bytes 26214400 | tf_op jit(solution)/shard_map/reduce_scatter | solution.py:352
  1257.2 5.9 copy-start.28
  1257.2 5.9 copy-start.30
  1275.0 6.0 copy-start.7
  1275.0 6.0 copy-start.35
  1275.1 6.0 copy-start.42
  1292.8 633.2 %reduce-scatter.32.cloned.1.call-start = ((), (), s32[]{:S(2)}) async-start(), calls=%async_computation.25 | async-start | bytes 40960
  1293.6 14.0 copy-start.14
  1306.3 642.3 %reduce-scatter.30.cloned.1.call-start = ((), (), s32[]{:S(2)}) async-start(), calls=%async_computation.24 | async-start | bytes 655360
  1307.5 661.2 %reduce-scatter.22.cloned.1.call-start = ((), (), s32[]{:S(2)}) async-start(), calls=%async_computation.16 | async-start | bytes 81920 | tf_op jit(solution)/shard_map/reduce_scatter | solution.py:358
  1308.5 771.9 %reduce-scatter.26.cloned.1.call-start = ((), (), s32[]{:S(2)}) async-start(), calls=%async_computation.18 | async-start | bytes 7864320 | tf_op jit(solution)/shard_map/reduce_scatter | solution.py:285
  1318.5 976.8 %reduce-scatter.24.cloned.1.call-start = ((), (), s32[]{:S(2)}) async-start(), calls=%async_computation.17 | async-start | bytes 15728640 | tf_op jit(solution)/shard_map/reduce_scatter | solution.py:282
  1334.8 1103.3 %all-reduce.13.cloned.1.call-start = ((), (), s32[]{:S(2)}) async-start(), calls=%async_computation.26 | async-start | bytes 18874368 | tf_op jit(solution)/shard_map/psum | solution.py:365
  2438.1 8.1 copy-start.18
  (28 other events, 90.3 us)
Sparse Core Ops, SparseCore 0:
  9.6 359.6 all-gather.12
  370.9 302.0 all-gather.14
  674.6 217.4 all-gather.16
  893.6 113.5 all-gather.18
  1231.2 18.0 reduce-scatter.15
  1251.4 19.9 reduce-scatter.27
  1273.7 278.5 reduce-scatter.19
  1554.8 347.9 reduce-scatter.17
  1905.6 20.3 reduce-scatter.31
  1928.7 19.8 reduce-scatter.29
  1951.5 17.1 reduce-scatter.21
  1971.5 108.9 reduce-scatter.25
  2082.8 212.3 reduce-scatter.23
  2298.7 139.3 all-reduce.12
where the time goes:
time: 2470 us; the launch traced here: 2460 us
  waiting for transfers between devices  1930 us (78%)
  matrix products  163 us (7%)
  blocking collectives  158 us (6%)
  local copies, waits for them, and re-layouts  95.4 us (4%)
  other arithmetic  75.8 us (3%)
    reduce_scatter x1, waiting for transfers between devices, shards(): lax.psum_scatter(grad_qkv.astype(jnp.bfloat16), 'shard', scatter_dimensio...  350 us
    all_gather x1, waiting for transfers between devices, shards(): qkv_weight = lax.all_gather(w_qkv[layer_index], 'shard', axis=0, tiled=True)  301 us
    reduce_scatter x1, waiting for transfers between devices, shards(): lax.psum_scatter(grad_attn_out.astype(jnp.bfloat16), 'shard', scatter_dim...  218 us
    all_gather x1, waiting for transfers between devices, shards(): lax.all_gather(w_attn_out[layer_index], 'shard', axis=0, tiled=True)  215 us
    reduce_scatter x1, waiting for transfers between devices, shards(): lax.psum_scatter(grad_gate_up.astype(jnp.bfloat16), 'shard', scatter_dime...  211 us
    psum x1, waiting for transfers between devices, shards(): lax.psum(qkv_part.astype(jnp.bfloat16), 'expert').astype(jnp.float32)  137 us
    all_gather x1, waiting for transfers between devices, shards(): lax.all_gather(w_gate_up[layer_index], 'shard', axis=1, tiled=True)  118 us
    all_gather x1, waiting for transfers between devices, shards(): down_full = lax.all_gather(w_down[layer_index], 'shard', axis=2, tiled=True)  98.1 us
  transfers between devices with their start and end apart: 18, of which 15 were waited for; matrix products, arithmetic and copies ran while one was open for 10% of the time, Pallas kernels for 0%

commit v1 on v0

v1 whole, which is shorter than its diff:
```python
import functools

import jax
import jax.numpy as jnp
from jax import lax
from jax.experimental import pallas as pl
from jax.experimental.pallas import tpu as pltpu
from jax.sharding import PartitionSpec as P

HEADS = 32
KV_HEADS = 4
HEAD_DIM = 128
TOP = 8

bf16 = jnp.bfloat16
f32 = jnp.float32
highest = lax.Precision.HIGHEST
eps_norm = 1e-06
rope_base = 1000000.0
neg_fill = -1e30


def dot(left, right, dims, out=f32):
    return lax.dot_general(left, right, (dims, ((), ())), preferred_element_type=out)


def mm(left, right):
    return dot(left, right, ((1,), (0,)))


def mm_nt(left, right):
    return dot(left, right, ((1,), (1,)))


def mm_tn(left, right):
    return dot(left, right, ((0,), (0,)))


def inv_rms(value):
    return lax.rsqrt(jnp.mean(value * value, axis=-1, keepdims=True) + eps_norm)


def rms_back(value, gain, grad):
    r = inv_rms(value)
    c = grad * gain
    back = r * c - value * (r * r * r) * jnp.mean(c * value, axis=-1, keepdims=True)
    return back, grad * value * r


def rotary_tables(length):
    half = HEAD_DIM // 2
    frequency = rope_base ** (-(jnp.arange(half, dtype=f32) * 2.0) / HEAD_DIM)
    angles = jnp.arange(length, dtype=f32)[:, None] * frequency[None, :]
    cos, sin = jnp.cos(angles), jnp.sin(angles)
    return jnp.concatenate([cos, cos], axis=1), jnp.concatenate([-sin, sin], axis=1)


MESH = pl.DeviceIdType.MESH


class Place:
    def __init__(self, n_expert, n_shard, group):
        self.e = lax.axis_index("expert")
        self.z = lax.axis_index("shard")
        self.n_expert, self.n_shard, self.group = n_expert, n_shard, group
        self.chip, self.core = self.e // 2, self.e % 2
        self.chips = n_expert // 2

    def z_dev(self, t):
        return (self.e, self.z ^ t)

    def slot(self, t, other=0):
        return (self.chip ^ t) * 2 + (self.core ^ other)

    def chip_dev(self, t):
        return (self.slot(t), self.z)

    def mate(self):
        return (self.e ^ 1, self.z)


class Net:
    def __init__(self, send, recv, local):
        self.send, self.recv, self.local = send, recv, local
        self.n, self.m, self.open = 0, 0, []

    def push(self, src, dst, dev):
        i = self.n
        self.n += 1
        copy = pltpu.make_async_remote_copy(
            src_ref=src, dst_ref=dst, send_sem=self.send.at[i], recv_sem=self.recv.at[i],
            device_id=dev, device_id_type=MESH,
        )
        copy.start()
        self.open.append(copy)
        return copy

    def copy(self, src, dst):
        i = self.m
        self.m += 1
        copy = pltpu.make_async_copy(src, dst, self.local.at[i])
        copy.start()
        return copy

    def sent(self):
        for copy in self.open:
            copy.wait_send()
        self.open = []


def greet(devices):
    barrier = pltpu.get_barrier_semaphore()
    for dev in devices:
        pl.semaphore_signal(barrier, inc=1, device_id=dev, device_id_type=MESH)
    pl.semaphore_wait(barrier, len(devices))


def everyone(at):
    return (
        [at.z_dev(t) for t in range(1, at.n_shard)]
        + [at.chip_dev(t) for t in range(1, at.chips)]
        + [at.mate()]
    )


def arrive(copies):
    for copy in copies:
        copy.wait_recv()


def spread(net, at, pieces):
    own = [p(at.e) for p in pieces]
    mate = [net.push(o, o, at.mate()) for o in own]
    out = [(t, [net.push(o, o, at.chip_dev(t)) for o in own]) for t in range(1, at.chips)]
    return mate, out


def pass_on(net, at, pieces, state):
    mate, out = state
    for t, copies in out:
        for p, copy in zip(pieces, copies):
            copy.wait_recv()
            got = p(at.slot(t))
            mate.append(net.push(got, got, at.mate()))
    return mate


def comm_call(kernel, cid, n_remote, n_local, scratch, outs, vmem_mb, in_specs=None, out_specs=None, cost=None):
    any_spec = pl.BlockSpec(memory_space=pl.ANY)

    def call(*args):
        return pl.pallas_call(
            kernel,
            out_shape=outs,
            in_specs=in_specs or [any_spec] * len(args),
            out_specs=out_specs or [any_spec] * len(outs),
            scratch_shapes=list(scratch)
            + [
                pltpu.SemaphoreType.DMA((n_remote,)),
                pltpu.SemaphoreType.DMA((n_remote,)),
                pltpu.SemaphoreType.DMA((n_local,)),
            ],
            compiler_params=pltpu.CompilerParams(
                collective_id=cid, has_side_effects=True, vmem_limit_bytes=vmem_mb << 20
            ),
            cost_estimate=cost,
        )(*args)

    return call


def tiled(size, most):
    while size % most:
        most //= 2
    return most


def halves(at):
    return list(range(1, at.chips)) + [0]


def norm_kernel(
    dims, db, ex, ggu, gdn, x1, b, cot, rw, router_t, gains,
    gx1, do_all, gain_two, g_router, land_gu, land_dn,
    own, own_x, core_in, core_x, chip_in, chip_x, half_out, half_x, swap_in, swap_x, logit, d_out,
    send, recv, local,
):
    at = Place(*dims)
    net = Net(send, recv, local)
    z, e, group = at.z, at.e, at.group
    tok = x1.shape[0]
    loads = {}
    for t in halves(at):
        loads[t] = (net.copy(db.at[at.slot(t)], own.at[t]), net.copy(ex.at[at.slot(t)], own_x.at[t]))
    greet(everyone(at))
    mates = {}
    for t in halves(at):
        mates[t] = (
            net.push(db.at[at.slot(t, 1)], core_in.at[t], at.mate()),
            net.push(ex.at[at.slot(t, 1)], core_x.at[t], at.mate()),
        )
    d_slice = ggu.shape[1]
    landed = []
    for t in range(1, group):
        j = z ^ t ^ group
        landed.append(net.push(gdn.at[:, pl.ds(pl.multiple_of(j * d_slice, d_slice), d_slice)], land_dn.at[t - 1], at.z_dev(t)))
        landed.append(net.push(ggu.at[j], land_gu.at[t - 1], at.z_dev(t)))
    step = 16
    ins = []
    for t in halves(at):
        for c in loads[t]:
            c.wait()
        arrive(mates[t])

        def add(i, _, t=t):
            rows = pl.ds(pl.multiple_of(i * step, step), step)
            own[t, rows, :] = (own[t, rows, :].astype(f32) + core_in[t, rows, :].astype(f32)).astype(bf16)
            own_x[t, rows, :] = (own_x[t, rows, :].astype(f32) + core_x[t, rows, :].astype(f32)).astype(bf16)
            return 0

        lax.fori_loop(0, 2 * tok // step, add, 0)
        if t:
            ins.append(net.push(own.at[t], chip_in.at[t - 1], at.chip_dev(t)))
            ins.append(net.push(own_x.at[t], chip_x.at[t - 1], at.chip_dev(t)))
    arrive(ins)

    def partner(i, _):
        rows = pl.ds(pl.multiple_of(i * step, step), step)
        src = pl.ds(pl.multiple_of(tok + i * step, step), step)
        total, total_x = own[0, src, :].astype(f32), own_x[0, src, :].astype(f32)
        for t in range(1, at.chips):
            total += chip_in[t - 1, src, :].astype(f32)
            total_x += chip_x[t - 1, src, :].astype(f32)
        half_out[rows, :] = total.astype(bf16)
        half_x[rows, :] = total_x.astype(bf16)
        return 0

    lax.fori_loop(0, tok // step, partner, 0)
    swaps = [net.push(half_out, swap_in, at.z_dev(group)), net.push(half_x, swap_x, at.z_dev(group))]
    arrive(swaps)
    gain_two[...] = jnp.zeros_like(gain_two)

    def owner(i, _):
        rows = pl.ds(pl.multiple_of(i * step, step), step)
        grad = own[0, rows, :].astype(f32) + swap_in[rows, :].astype(f32)
        routed = own_x[0, rows, :].astype(f32) + swap_x[rows, :].astype(f32)
        for t in range(1, at.chips):
            grad += chip_in[t - 1, rows, :].astype(f32)
            routed += chip_x[t - 1, rows, :].astype(f32)
        routed = routed + pltpu.roll(routed, 64, 1)
        weight = rw[rows, :]
        d_logit = weight * (routed - jnp.sum(weight * routed, axis=1, keepdims=True))
        high = d_logit.astype(bf16)
        low = (d_logit - high.astype(f32)).astype(bf16)
        logit[0, rows, :] = high
        logit[1, rows, :] = low
        grad += mm(high, router_t[...]) + mm(low, router_t[...])
        value = x1[rows, :]
        r = inv_rms(value)
        c = grad * gains[1:2, :]
        back = cot[rows, :].astype(f32) + r * c - value * (r * r * r * jnp.mean(c * value, axis=-1, keepdims=True))
        gx1[rows, :] = back
        d_out[rows, :] = back.astype(bf16)
        per = grad * value * r
        gain_two[...] += per[:8] + per[8:]
        return 0

    lax.fori_loop(0, tok // step, owner, 0)
    mine = do_all.at[pl.ds(pl.multiple_of(z * tok, tok), tok)]
    keep = net.copy(d_out, mine)
    copies = [net.push(d_out, mine, at.z_dev(t)) for t in range(1, at.n_shard)]
    g_router[...] = mm_tn(logit[0], b[...]) + mm_tn(logit[1], b[...])
    keep.wait()
    arrive(copies + landed)
    net.sent()


def rope_rows(value, cos, sin):
    return value * cos + pltpu.roll(value, HEAD_DIM // 2, 1) * sin


def rope_rows_back(grad, cos, sin):
    return grad * cos + pltpu.roll(grad * sin, HEAD_DIM // 2, 1)


def eight(per):
    return jnp.sum(per.reshape(per.shape[0] // 8, 8, per.shape[1]), axis=0)


def span(i, size):
    if isinstance(i, int):
        return pl.ds(i * size, size)
    return pl.ds(pl.multiple_of(i * size, size), size)


def soft_block(q_ref, k_ref, seg_row, seg_col, h, i, block, scale):
    rows, keys = pl.ds(i * block, block), pl.ds(0, (i + 1) * block)
    scores = mm_nt(q_ref[rows, span(h, HEAD_DIM)], k_ref[keys, :]) * scale
    width = (i + 1) * block
    at_q = i * block + lax.broadcasted_iota(jnp.int32, (block, width), 0)
    at_k = lax.broadcasted_iota(jnp.int32, (block, width), 1)
    allowed = (at_k <= at_q) & (seg_row[0:1, keys] == seg_col[rows, 0:1])
    scores = jnp.where(allowed, scores, neg_fill)
    raised = jnp.exp(scores - jnp.max(scores, axis=-1, keepdims=True))
    return raised / jnp.sum(raised, axis=-1, keepdims=True)


def front_kernel(
    dims, x, small, seg_own, w_qkv, w_out, w_gu, w_dn, cot, mask, cos_h, sin_h,
    small_out, seg_out, heads_out, a_out, raw_out, q_out, k_out, v_out, o_out, x1_out, b_out,
    gate_up, down, cot_all, mask_all, b_all,
    x_all, small_all, seg_col, heads, a, raw, q, k, v, o, w_o, part, parts_in, cos, sin, gains, seg_row, x1, b_own,
    send, recv, local,
):
    at = Place(*dims)
    net = Net(send, recv, local)
    z, e, group = at.z, at.e, at.group
    tok = x.shape[0]
    length, width = x_all.shape
    mine = z // group
    rows_e, cols = heads.shape[2], heads.shape[3]
    hd = cols - 2 * HEAD_DIM
    n_heads = hd // HEAD_DIM
    q_width = HEADS * HEAD_DIM
    d_slice = w_gu.shape[1]
    scale = HEAD_DIM ** (-0.5)
    block = tok

    def heads_of(dest):
        kv = (dest * n_heads) // (HEADS // KV_HEADS)
        rows = span(e, rows_e)
        return [
            (w_qkv.at[rows, span(dest, hd)], heads.at[z, e, :, pl.ds(0, hd)]),
            (w_qkv.at[rows, span(HEADS + kv, HEAD_DIM)], heads.at[z, e, :, pl.ds(hd, HEAD_DIM)]),
            (w_qkv.at[rows, span(HEADS + KV_HEADS + kv, HEAD_DIM)], heads.at[z, e, :, pl.ds(hd + HEAD_DIM, HEAD_DIM)]),
        ]

    def d_cols(ref, who):
        return ref.at[:, span(who, d_slice)]

    half0, half1 = pl.ds(0, tok), pl.ds(tok, tok)
    first = [
        net.copy(x, x_all.at[span(z, tok)]),
        net.copy(small, small_all.at[z]),
        net.copy(seg_own, seg_col.at[span(z, tok)]),
        net.copy(cos_h, cos),
        net.copy(sin_h, sin),
    ]
    local_heads = [net.copy(s, d) for s, d in heads_of(z)]
    local_cot = [net.copy(cot, cot_all.at[e, half0]), net.copy(mask, mask_all.at[e, half0])]
    load_out = net.copy(w_out, w_o)
    here = [net.copy(w_gu.at[mine], gate_up.at[z]), net.copy(w_dn.at[mine], d_cols(down, z))]
    greet(everyone(at))
    got_heads = [net.push(s, d, at.z_dev(t)) for t in range(1, at.n_shard) for s, d in heads_of(z ^ t)]
    got_x = []
    for t in range(1, at.n_shard):
        got_x.append(net.push(small, small_all.at[z], at.z_dev(t)))
        got_x.append(net.push(seg_own, seg_col.at[span(z, tok)], at.z_dev(t)))
        got_x.append(net.push(x, x_all.at[span(z, tok)], at.z_dev(t)))
    for c in local_heads:
        c.wait()
    arrive(got_heads)
    pieces = [lambda who: heads.at[:, who]]
    heads_state = spread(net, at, pieces)
    for c in first:
        c.wait()
    arrive(got_x)
    other = (z ^ group) // group
    from_partner = [
        (net.push(w_gu.at[other], gate_up.at[z], at.z_dev(group)), gate_up.at[z ^ group]),
        (net.push(w_dn.at[other], d_cols(down, z), at.z_dev(group)), d_cols(down, z ^ group)),
    ]
    got_w = []
    for t in range(1, group):
        got_w.append(net.push(w_gu.at[mine], gate_up.at[z], at.z_dev(t)))
        got_w.append(net.push(w_dn.at[mine], d_cols(down, z), at.z_dev(t)))
    got_cot = [
        net.push(cot, cot_all.at[e, half1], at.z_dev(group)),
        net.push(mask, mask_all.at[e, half1], at.z_dev(group)),
    ]

    qk = []
    for s in range(at.n_shard):
        rows = small_all[s, 0:16, :].astype(f32)
        gains[0:2, span(s, d_slice)] = rows[0:2]
        seg_row[0:1, span(s, tok)] = rows[4:5, :tok]
        qk.append(rows[2:4, :HEAD_DIM])
    qk = sum(qk[1:], qk[0])
    step = 16

    def norm_rows(i, _):
        rows = span(i, step)
        value = x_all[rows, :].astype(f32)
        a[rows, :] = (value * inv_rms(value) * gains[0:1, :]).astype(bf16)
        return 0

    lax.fori_loop(0, length // step, norm_rows, 0)
    last = pass_on(net, at, pieces, heads_state)
    arrive(last)
    keep = [net.copy(heads, heads_out), net.copy(a, a_out), net.copy(small_all, small_out), net.copy(seg_col, seg_out)]

    wide = tiled(cols, 256)

    def project(i, _):
        tile = span(i, wide)
        raw[:, tile] = mm(a[...], heads[:, :, :, tile].reshape(width, wide))
        return 0

    lax.fori_loop(0, cols // wide, project, 0)
    keep.append(net.copy(raw, raw_out))

    def head_rows(i, _):
        rows = span(i, block)
        cos_b, sin_b = cos[rows, :], sin[rows, :]
        for h in range(n_heads + 1):
            value = raw[rows, pl.ds(h * HEAD_DIM, HEAD_DIM)]
            gain = qk[0:1] if h < n_heads else qk[1:2]
            value = rope_rows(value * inv_rms(value) * gain, cos_b, sin_b).astype(bf16)
            if h < n_heads:
                q[rows, pl.ds(h * HEAD_DIM, HEAD_DIM)] = value
            else:
                k[rows, :] = value
        v[rows, :] = raw[rows, pl.ds(hd + HEAD_DIM, HEAD_DIM)].astype(bf16)
        return 0

    lax.fori_loop(0, length // block, head_rows, 0)
    keep += [net.copy(q, q_out), net.copy(k, k_out), net.copy(v, v_out)]
    for c in local_cot:
        c.wait()
    arrive(got_cot)
    cots = [lambda who: cot_all.at[who], lambda who: mask_all.at[who]]
    cot_state = spread(net, at, cots)

    def one_head(h, _):
        for i in range(length // block):
            soft = soft_block(q, k, seg_row, seg_col, h, i, block, scale).astype(bf16)
            mixed = mm(soft, v[pl.ds(0, (i + 1) * block), :])
            o[pl.ds(i * block, block), span(h, HEAD_DIM)] = mixed.astype(bf16)
        return 0

    lax.fori_loop(0, n_heads, one_head, 0)
    keep.append(net.copy(o, o_out))
    load_out.wait()
    wide_o = tiled(width, 256)

    def out_tile(i, _):
        tile = span(i, wide_o)
        part[:, tile] = mm(o[...], w_o[:, tile]).astype(bf16)
        return 0

    lax.fori_loop(0, width // wide_o, out_tile, 0)
    sums = [net.push(part.at[span(z ^ t, tok)], parts_in.at[t - 1], at.z_dev(t)) for t in range(1, at.n_shard)]
    last = pass_on(net, at, cots, cot_state)
    for copy, ref in from_partner:
        copy.wait_recv()
        for t in range(1, group):
            got_w.append(net.push(ref, ref, at.z_dev(t)))
    arrive(sums)

    def middle_rows(i, _):
        rows = span(i, step)
        total = part[pl.ds(pl.multiple_of(z * tok + i * step, step), step), :].astype(f32)
        for t in range(1, at.n_shard):
            total += parts_in[t - 1, rows, :].astype(f32)
        value = x_all[pl.ds(pl.multiple_of(z * tok + i * step, step), step), :].astype(f32) + total
        x1[rows, :] = value
        b_own[rows, :] = (value * inv_rms(value) * gains[1:2, :]).astype(bf16)
        return 0

    lax.fori_loop(0, tok // step, middle_rows, 0)
    local_b = net.copy(b_own, b_all.at[e, half0])
    swap = net.push(b_own, b_all.at[e, half1], at.z_dev(group))
    keep += [net.copy(x1, x1_out), net.copy(b_own, b_out)]
    local_b.wait()
    swap.wait_recv()
    rows_b = [lambda who: b_all.at[who]]
    last += pass_on(net, at, rows_b, spread(net, at, rows_b))
    arrive(last + got_w)
    for c in keep + here:
        c.wait()
    net.sent()


def back_kernel(
    dims, do_h, w_out, o_h, q_h, k_h, v_h, raw_h, cos_h, sin_h, seg_h, small, ggu, gdn, land_gu, land_dn, out_part, x1,
    d_qkv_out, qk_gain, share_out, hidden, two_gu, two_dn, own_gu, own_dn, out_core,
    do_all, w_o, o, q, k, v, raw, cos, sin, seg_col, seg_row, mix, d_qkv, dk, dv,
    sum_gu, add_gu, sum_dn, add_dn, out_own, out_add, out_in, half_out, swap_in, g_out, g_core, g_in,
    send, recv, local,
):
    at = Place(*dims)
    net = Net(send, recv, local)
    z, e, group = at.z, at.e, at.group
    length, width = do_all.shape
    tok = x1.shape[0]
    cols = raw.shape[1]
    hd = cols - 2 * HEAD_DIM
    n_heads = hd // HEAD_DIM
    d_slice = ggu.shape[1]
    scale = HEAD_DIM ** (-0.5)
    block = tok
    step = 16
    far = z ^ group

    def d_cols(ref, who):
        return ref.at[:, span(who, d_slice)]

    load_dn = [net.copy(d_cols(gdn, far), sum_dn)] + [net.copy(land_dn.at[t - 1], add_dn.at[t - 1]) for t in range(1, group)]
    load_gu = [net.copy(ggu.at[far], sum_gu)] + [net.copy(land_gu.at[t - 1], add_gu.at[t - 1]) for t in range(1, group)]
    load_a = [net.copy(do_h, do_all), net.copy(o_h, o)]
    load_own = {t: net.copy(out_part.at[at.slot(t)], out_own.at[t]) for t in halves(at)}
    load_b = [
        net.copy(s, d)
        for s, d in ((w_out, w_o), (q_h, q), (k_h, k), (v_h, v), (raw_h, raw), (cos_h, cos), (sin_h, sin), (seg_h, seg_col))
    ]
    greet(everyone(at))
    mates = {t: net.push(out_part.at[at.slot(t, 1)], out_core.at[t], at.mate()) for t in halves(at)}

    def add_up(total, adds):
        def rows_of(i, _):
            rows = span(i, step)
            value = total[rows, :].astype(f32)
            for t in range(1, group):
                value += adds[t - 1, rows, :].astype(f32)
            total[rows, :] = value.astype(bf16)
            return 0

        lax.fori_loop(0, total.shape[0] // step, rows_of, 0)

    for c in load_gu:
        c.wait()
    add_up(sum_gu, add_gu)
    got = [net.push(sum_gu, two_gu, at.z_dev(group))]
    for c in load_dn:
        c.wait()
    add_up(sum_dn, add_dn)
    got.append(net.push(sum_dn, two_dn, at.z_dev(group)))
    for t in range(1, group):
        got.append(net.push(ggu.at[z ^ t], own_gu.at[t - 1], at.z_dev(t)))
        got.append(net.push(d_cols(gdn, z ^ t), own_dn.at[t - 1], at.z_dev(t)))

    for c in load_a:
        c.wait()
    share = share_out.shape[0]

    wide = tiled(hd, 256)
    each = wide // share

    def out_grad(i, _):
        tile = mm_tn(o[:, span(i, wide)], do_all[...]).astype(bf16)
        for j in range(each):
            g_out[each * i + j] = tile[j * share : (j + 1) * share]
        return 0

    lax.fori_loop(0, hd // wide, out_grad, 0)
    g_mates = {t: net.push(g_out.at[at.slot(t, 1)], g_core.at[t], at.mate()) for t in halves(at)}

    outs = []
    for t in halves(at):
        load_own[t].wait()
        mates[t].wait_recv()
        c = net.copy(out_core.at[t], out_add)
        c.wait()

        def add(i, _, t=t):
            rows = span(i, step)
            out_own[t, rows, :] = (out_own[t, rows, :].astype(f32) + out_add[rows, :].astype(f32)).astype(bf16)
            return 0

        lax.fori_loop(0, 2 * tok // step, add, 0)
        if t:
            outs.append(net.push(out_own.at[t], out_in.at[t - 1], at.chip_dev(t)))
    for c in load_b:
        c.wait()
    qk = []
    for s in range(at.n_shard):
        rows = small[s, 0:16, :].astype(f32)
        seg_row[0:1, span(s, tok)] = rows[4:5, :tok]
        qk.append(rows[2:4, :HEAD_DIM])
    qk = sum(qk[1:], qk[0])

    def mix_tile(i, _):
        tile = span(i, wide)
        mix[:, tile] = mm_nt(do_all[...], w_o[tile, :]).astype(bf16)
        return 0

    lax.fori_loop(0, hd // wide, mix_tile, 0)
    g_outs = []
    for t in halves(at):
        g_mates[t].wait_recv()

        def add(i, _, t=t):
            rows = span(i, step)
            s = at.slot(t)
            g_out[s, rows, :] = (g_out[s, rows, :].astype(f32) + g_core[t, rows, :].astype(f32)).astype(bf16)
            return 0

        lax.fori_loop(0, share // step, add, 0)
        if t:
            g_outs.append(net.push(g_out.at[at.slot(t)], g_in.at[t - 1], at.chip_dev(t)))

    dk[...] = jnp.zeros_like(dk)
    dv[...] = jnp.zeros_like(dv)
    qk_gain[...] = jnp.zeros_like(qk_gain)

    def one_head(h, _):
        lanes = span(h, HEAD_DIM)
        for i in range(length // block):
            rows, keys = pl.ds(i * block, block), pl.ds(0, (i + 1) * block)
            soft = soft_block(q, k, seg_row, seg_col, h, i, block, scale)
            d_mix = mix[rows, lanes]
            d_soft = mm_nt(d_mix, v[keys, :])
            d_scores = (soft * (d_soft - jnp.sum(soft * d_soft, axis=-1, keepdims=True))).astype(bf16)
            dv[keys, :] += mm_tn(soft.astype(bf16), d_mix)
            dk[keys, :] += mm_tn(d_scores, q[rows, lanes]) * scale
            dq = mm(d_scores, k[keys, :]) * scale
            value = raw[rows, lanes]
            back, per = rms_back(value, qk[0:1], rope_rows_back(dq, cos[rows, :], sin[rows, :]))
            d_qkv[rows, lanes] = back.astype(bf16)
            qk_gain[0:8, :] += eight(per)
        return 0

    lax.fori_loop(0, n_heads, one_head, 0)
    for i in range(length // block):
        rows = pl.ds(i * block, block)
        value = raw[rows, pl.ds(hd, HEAD_DIM)]
        back, per = rms_back(value, qk[1:2], rope_rows_back(dk[rows, :], cos[rows, :], sin[rows, :]))
        d_qkv[rows, pl.ds(hd, HEAD_DIM)] = back.astype(bf16)
        d_qkv[rows, pl.ds(hd + HEAD_DIM, HEAD_DIM)] = dv[rows, :].astype(bf16)
        qk_gain[8:16, :] += eight(per)
    keep = net.copy(d_qkv, d_qkv_out)

    arrive(outs)

    def sum_in(rows):
        total = out_own[0, rows, :].astype(f32)
        for t in range(1, at.chips):
            total += out_in[t - 1, rows, :].astype(f32)
        return total

    def partner(i, _):
        half_out[span(i, step), :] = sum_in(pl.ds(pl.multiple_of(tok + i * step, step), step)).astype(bf16)
        return 0

    lax.fori_loop(0, tok // step, partner, 0)
    swap = net.push(half_out, swap_in, at.z_dev(group))
    arrive(g_outs)

    def own_share(i, _):
        rows = span(i, step)
        total = g_out[e, rows, :].astype(f32)
        for t in range(1, at.chips):
            total += g_in[t - 1, rows, :].astype(f32)
        share_out[rows, :] = total.astype(bf16)
        return 0

    lax.fori_loop(0, share // step, own_share, 0)
    swap.wait_recv()

    def hidden_rows(i, _):
        rows = span(i, step)
        hidden[rows, :] = (x1[rows, :] + sum_in(rows) + swap_in[rows, :].astype(f32)).astype(bf16)
        return 0

    lax.fori_loop(0, tok // step, hidden_rows, 0)
    arrive(got)
    keep.wait()
    net.sent()


def tail_kernel(
    dims, d_qkv_h, heads_h, a_h, gx1, x, gains, gain_two, g_router, qk_gain, share_out,
    g_hidden, g_qkv, g_att, small_sum,
    d_qkv, heads, a, part, parts_in, g_heads, core_in, chip_in, mine, turn_in, share, sm, sm_z, sm_core, sm_chip,
    send, recv, local,
):
    at = Place(*dims)
    net = Net(send, recv, local)
    z, e, group = at.z, at.e, at.group
    length, cols = d_qkv.shape
    tok, width = x.shape
    hd = cols - 2 * HEAD_DIM
    n_heads = hd // HEAD_DIM
    rows_e = heads.shape[2]
    d_slice = width // at.n_shard
    step = 16
    load_a = [net.copy(d_qkv_h, d_qkv), net.copy(heads_h, heads)]
    load_b = net.copy(a_h, a)
    own_att = net.copy(share_out, g_att.at[e])
    greet(everyone(at))
    own_att.wait()
    atts = [lambda who: g_att.at[who]]
    att_state = spread(net, at, atts)
    for c in load_a:
        c.wait()

    wide = tiled(d_slice, 256)
    each = wide // rows_e

    def rows_tile(s, _):
        for j in range(d_slice // wide):
            some = heads[s, pl.ds(each * j, each)].reshape(wide, cols)
            here = pl.ds(pl.multiple_of(s * d_slice + j * wide, wide), wide)
            part[:, here] = mm_nt(d_qkv[...], some).astype(bf16)
        return 0

    lax.fori_loop(0, at.n_shard, rows_tile, 0)
    sums = [net.push(part.at[span(z ^ t, tok)], parts_in.at[t - 1], at.z_dev(t)) for t in range(1, at.n_shard)]
    load_b.wait()

    def grad_tile(s, _):
        for j in range(d_slice // wide):
            some = a[:, pl.ds(pl.multiple_of(s * d_slice + j * wide, wide), wide)]
            tile = mm_tn(some, d_qkv[...]).astype(bf16)
            for i in range(each):
                g_heads[each * j + i, s] = tile[i * rows_e : (i + 1) * rows_e]
        return 0

    lax.fori_loop(0, at.n_shard, grad_tile, 0)
    mates = {t: net.push(g_heads.at[at.slot(t, 1)], core_in.at[t], at.mate()) for t in halves(at)}
    chips = []
    for t in halves(at):
        mates[t].wait_recv()
        who = at.slot(t)

        def add(s, _, t=t, who=who):
            g_heads[who, s] = (g_heads[who, s].astype(f32) + core_in[t, s].astype(f32)).astype(bf16)
            return 0

        lax.fori_loop(0, at.n_shard, add, 0)
        if t:
            chips.append(net.push(g_heads.at[who], chip_in.at[t - 1], at.chip_dev(t)))
    atts_last = pass_on(net, at, atts, att_state)
    arrive(sums)
    sm[...] = jnp.zeros_like(sm)
    gain_one = jnp.zeros((8, width), f32)

    def owner(i, gain_one):
        rows = span(i, step)
        here = pl.ds(pl.multiple_of(z * tok + i * step, step), step)
        da = part[here, :].astype(f32)
        for t in range(1, at.n_shard):
            da += parts_in[t - 1, rows, :].astype(f32)
        back, per = rms_back(x[rows, :].astype(f32), gains[0:1, :], da)
        g_hidden[rows, :] = gx1[rows, :] + back
        return gain_one + eight(per)

    gain_one = lax.fori_loop(0, tok // step, owner, gain_one)
    row_one = jnp.sum(gain_one, axis=0, keepdims=True)
    row_two = jnp.sum(gain_two[...], axis=0, keepdims=True)
    row_q = jnp.sum(qk_gain[0:8, :], axis=0, keepdims=True)
    row_k = jnp.sum(qk_gain[8:16, :], axis=0, keepdims=True)
    for s in range(at.n_shard):
        piece = pl.ds(s * d_slice, d_slice)
        lanes = slice(s * d_slice, (s + 1) * d_slice)
        sm[s, 0:1, :] = row_one[:, lanes]
        sm[s, 1:2, :] = row_two[:, lanes]
        sm[s, 2:3, pl.ds(0, HEAD_DIM)] = row_q
        sm[s, 3:4, pl.ds(0, HEAD_DIM)] = row_k
        sm[s, 8:, :] = g_router[0 : sm.shape[1] - 8, piece]
    small_z = [net.push(sm.at[z ^ t], sm_z.at[t - 1], at.z_dev(t)) for t in range(1, at.n_shard)]
    arrive(chips)

    def total(s, _):
        value = g_heads[e, s].astype(f32)
        for t in range(1, at.chips):
            value += chip_in[t - 1, s].astype(f32)
        mine[s] = value.astype(bf16)
        return 0

    lax.fori_loop(0, at.n_shard, total, 0)
    turns = [net.push(mine.at[z ^ t], turn_in.at[z], at.z_dev(t)) for t in range(1, at.n_shard)]
    turn_own = net.copy(mine.at[z], turn_in.at[z])
    arrive(small_z)
    value = sm[z]
    for t in range(1, at.n_shard):
        value += sm_z[t - 1]
    sm[z] = value
    c = net.push(sm.at[z], sm_core, at.mate())
    turn_own.wait()
    arrive(turns)
    for s in range(at.n_shard):
        share[:, pl.ds(s * hd, hd)] = turn_in[s, :, pl.ds(0, hd)]
    for m in range(KV_HEADS):
        some = [s for s in range(at.n_shard) if (s * n_heads) // (HEADS // KV_HEADS) == m]
        for first, to in ((hd, HEADS + m), (hd + HEAD_DIM, HEADS + KV_HEADS + m)):
            value = turn_in[some[0], :, pl.ds(first, HEAD_DIM)].astype(f32)
            for s in some[1:]:
                value += turn_in[s, :, pl.ds(first, HEAD_DIM)].astype(f32)
            share[:, pl.ds(to * HEAD_DIM, HEAD_DIM)] = value.astype(bf16)
    keep = net.copy(share, g_qkv.at[e])
    c.wait_recv()
    sm_core[...] = sm[z] + sm_core[...]
    smalls = [net.push(sm_core, sm_chip.at[t - 1], at.chip_dev(t)) for t in range(1, at.chips)]
    keep.wait()
    qkvs = [lambda who: g_qkv.at[who]]
    last = pass_on(net, at, qkvs, spread(net, at, qkvs))
    arrive(smalls)
    value = sm_core[...]
    for t in range(1, at.chips):
        value += sm_chip[t - 1]
    small_sum[...] = value
    arrive(last + atts_last)
    net.sent()


def shards(
    hidden_in,
    segments,
    routes,
    norm_gains,
    qk_gains,
    w_qkv,
    w_attn_out,
    w_router,
    w_gate_up,
    w_down,
    cotangent,
):
    n_expert = lax.axis_size("expert")
    n_shard = lax.axis_size("shard")
    me_e = lax.axis_index("expert")
    me_z = lax.axis_index("shard")
    tok, width = hidden_in.shape
    exp_dev = w_gate_up.shape[1]
    experts_all = w_router.shape[2]
    d_slice, ff2 = w_gate_up.shape[2:]
    ff = ff2 // 2
    group = n_shard // exp_dev
    mine = me_z // group
    length = n_shard * tok
    h_dev = HEADS // n_shard
    hd = h_dev * HEAD_DIM
    cols = hd + 2 * HEAD_DIM
    qkv_cols = w_qkv.shape[2]
    rows_e = d_slice // n_expert
    share = hd // n_expert
    chips = n_expert // 2
    qk_part = HEAD_DIM // n_shard
    dims = (n_expert, n_shard, group)
    n_small = 16 + experts_all
    sds = jax.ShapeDtypeStruct
    vm = pltpu.VMEM
    any_spec = pl.BlockSpec(memory_space=pl.ANY)
    vmem_spec = pl.BlockSpec(memory_space=pltpu.VMEM)

    small = jnp.zeros((16, d_slice), bf16)
    small = small.at[0:2, :].set(norm_gains[0])
    small = lax.dynamic_update_slice(small, qk_gains[0], (2, me_z * qk_part))
    small = small.at[4, :tok].set(segments.astype(bf16))
    small = jnp.concatenate([small, w_router[0].T], axis=0)
    seg_own = jnp.broadcast_to(segments.astype(f32)[:, None], (tok, 128))
    ids = jnp.arange(128, dtype=jnp.int32)
    mask = jnp.sum((routes[:, :, None] == ids[None, None, :]).astype(f32), axis=1).astype(bf16)
    cos, sin = rotary_tables(length)

    outs = [
        sds((n_shard, n_small, d_slice), bf16),
        sds((length, 128), f32),
        sds((n_shard, n_expert, rows_e, cols), bf16),
        sds((length, width), bf16),
        sds((length, cols), f32),
        sds((length, hd), bf16),
        sds((length, HEAD_DIM), bf16),
        sds((length, HEAD_DIM), bf16),
        sds((length, hd), bf16),
        sds((tok, width), f32),
        sds((tok, width), bf16),
        sds((n_shard, d_slice, ff2), bf16),
        sds((ff, width), bf16),
        sds((n_expert, 2 * tok, width), bf16),
        sds((n_expert, 2 * tok, 128), bf16),
        sds((n_expert, 2 * tok, width), bf16),
    ]
    front = comm_call(
        functools.partial(front_kernel, dims),
        0,
        160,
        40,
        [
            vm((length, width), bf16),
            vm((n_shard, n_small, d_slice), bf16),
            vm((length, 128), f32),
            vm((n_shard, n_expert, rows_e, cols), bf16),
            vm((length, width), bf16),
            vm((length, cols), f32),
            vm((length, hd), bf16),
            vm((length, HEAD_DIM), bf16),
            vm((length, HEAD_DIM), bf16),
            vm((length, hd), bf16),
            vm((hd, width), bf16),
            vm((length, width), bf16),
            vm((n_shard - 1, tok, width), bf16),
            vm((length, HEAD_DIM), f32),
            vm((length, HEAD_DIM), f32),
            vm((8, width), f32),
            vm((8, length), f32),
            vm((tok, width), f32),
            vm((tok, width), bf16),
        ],
        outs,
        56,
    )
    (small_all, seg_col, heads, a, raw, q, k, v, o, x1, b, gate_up, down, cot_all, mask_all, b_all) = front(
        hidden_in, small, seg_own, w_qkv[0], w_attn_out[0], w_gate_up[0], w_down[0], cotangent, mask, cos, sin
    )
    gains = jnp.zeros((8, width), f32)
    gains = gains.at[0:2].set(small_all[:, 0:2].astype(f32).transpose(1, 0, 2).reshape(2, width))
    router_t = small_all[:, 16:].transpose(1, 0, 2).reshape(experts_all, width)

    def route_weights(rows, chosen):
        logits = mm_nt(rows, router_t)
        masked = jnp.where(chosen, logits, neg_fill)
        raised = jnp.where(chosen, jnp.exp(masked - jnp.max(masked, axis=1, keepdims=True)), 0.0)
        return raised / jnp.sum(raised, axis=1, keepdims=True)

    rows_all = n_expert * 2 * tok
    b_rows = b_all.reshape(rows_all, width)
    my_expert = me_e * exp_dev + mine
    rw_all = route_weights(b_rows, mask_all.reshape(rows_all, 128)[:, :experts_all] > 0)
    is_mine = ids[:experts_all] == my_expert
    rw_mine = jnp.sum(jnp.where(is_mine[None, :], rw_all, 0.0), axis=1, keepdims=True)
    rw = route_weights(b, mask[:, :experts_all] > 0)
    rw = jnp.concatenate([rw, jnp.zeros((tok, 128 - experts_all), f32)], axis=1)
    w_gu = gate_up.reshape(width, ff2)
    pre = mm(b_rows, w_gu)
    g, u = pre[:, :ff], pre[:, ff:]
    sig = jax.nn.sigmoid(g)
    act = g * sig
    hidden = (act * u).astype(bf16)
    y_f = mm(hidden, down).astype(bf16).astype(f32)
    cot_f = cot_all.reshape(rows_all, width).astype(f32)
    d_route = jnp.sum(cot_f * y_f, axis=1, keepdims=True)
    out_part = (rw_mine * y_f).astype(bf16)
    d_y = (rw_mine * cot_f).astype(bf16)
    d_hidden = mm_nt(d_y, down)
    d_pre = jnp.concatenate(
        [d_hidden * u * sig * (1.0 + g * (1.0 - sig)), d_hidden * act], axis=1
    ).astype(bf16)
    d_b = mm_nt(d_pre, w_gu).astype(bf16)
    grad_down = mm_tn(hidden, d_y).astype(bf16)
    grad_gate_up = mm_tn(b_rows, d_pre).astype(bf16).reshape(n_shard, d_slice, ff2)
    high = lax.reduce_precision(d_route, 8, 7)
    low = d_route - high
    extra = jnp.where(ids[None] == my_expert, high, jnp.where(ids[None] == my_expert + 64, low, 0.0)).astype(bf16)

    per_e = (n_expert, 2 * tok)
    piece = (chips, 2 * tok)
    router_pad = jnp.concatenate([router_t, jnp.zeros((128 - experts_all, width), bf16)], axis=0)
    gx1, d_o, gain_two, g_router, land_gu, land_dn = comm_call(
        functools.partial(norm_kernel, dims),
        1,
        60,
        40,
        [
            vm(piece + (width,), bf16),
            vm(piece + (128,), bf16),
            vm(piece + (width,), bf16),
            vm(piece + (128,), bf16),
            vm((chips - 1, 2 * tok, width), bf16),
            vm((chips - 1, 2 * tok, 128), bf16),
            vm((tok, width), bf16),
            vm((tok, 128), bf16),
            vm((tok, width), bf16),
            vm((tok, 128), bf16),
            vm((2, tok, 128), bf16),
            vm((tok, width), bf16),
        ],
        [
            sds((tok, width), f32),
            sds((length, width), bf16),
            sds((8, width), f32),
            sds((128, width), f32),
            sds((group - 1, d_slice, ff2), bf16),
            sds((group - 1, ff, d_slice), bf16),
        ],
        56,
        in_specs=[any_spec] * 4 + [vmem_spec] * 6,
        out_specs=[vmem_spec, any_spec, vmem_spec, vmem_spec, any_spec, any_spec],
    )(
        d_b.reshape(per_e + (width,)),
        extra.reshape(per_e + (128,)),
        grad_gate_up,
        grad_down,
        x1,
        b,
        cotangent,
        rw,
        router_pad,
        gains,
    )

    d_qkv, qk_gain, share_out, hidden_out, two_gu, two_dn, own_gu, own_dn, _ = comm_call(
        functools.partial(back_kernel, dims),
        2,
        80,
        60,
        [
            vm((length, width), bf16),
            vm((hd, width), bf16),
            vm((length, hd), bf16),
            vm((length, hd), bf16),
            vm((length, HEAD_DIM), bf16),
            vm((length, HEAD_DIM), bf16),
            vm((length, cols), f32),
            vm((length, HEAD_DIM), f32),
            vm((length, HEAD_DIM), f32),
            vm((length, 128), f32),
            vm((8, length), f32),
            vm((length, hd), bf16),
            vm((length, cols), bf16),
            vm((length, HEAD_DIM), f32),
            vm((length, HEAD_DIM), f32),
            vm((d_slice, ff2), bf16),
            vm((group - 1, d_slice, ff2), bf16),
            vm((ff, d_slice), bf16),
            vm((group - 1, ff, d_slice), bf16),
            vm(piece + (width,), bf16),
            vm((2 * tok, width), bf16),
            vm((chips - 1, 2 * tok, width), bf16),
            vm((tok, width), bf16),
            vm((tok, width), bf16),
            vm((n_expert, share, width), bf16),
            vm((chips, share, width), bf16),
            vm((chips - 1, share, width), bf16),
        ],
        [
            sds((length, cols), bf16),
            sds((16, HEAD_DIM), f32),
            sds((share, width), bf16),
            sds((tok, width), bf16),
            sds((d_slice, ff2), bf16),
            sds((ff, d_slice), bf16),
            sds((group - 1, d_slice, ff2), bf16),
            sds((group - 1, ff, d_slice), bf16),
            sds((chips, 2 * tok, width), bf16),
        ],
        60,
        in_specs=[any_spec] * 10 + [vmem_spec] + [any_spec] * 5 + [vmem_spec],
        out_specs=[any_spec] + [vmem_spec] * 3 + [any_spec] * 5,
    )(
        d_o,
        w_attn_out[0],
        o,
        q,
        k,
        v,
        raw,
        cos,
        sin,
        seg_col,
        small_all,
        grad_gate_up,
        grad_down,
        land_gu,
        land_dn,
        out_part.reshape(per_e + (width,)),
        x1,
    )

    small_rows = (8 + -(-experts_all // 8) * 8, d_slice)
    grad_hidden, grad_qkv, grad_out, sums = comm_call(
        functools.partial(tail_kernel, dims),
        3,
        100,
        16,
        [
            vm((length, cols), bf16),
            vm((n_shard, n_expert, rows_e, cols), bf16),
            vm((length, width), bf16),
            vm((length, width), bf16),
            vm((n_shard - 1, tok, width), bf16),
            vm((n_expert, n_shard, rows_e, cols), bf16),
            vm((chips, n_shard, rows_e, cols), bf16),
            vm((chips - 1, n_shard, rows_e, cols), bf16),
            vm((n_shard, rows_e, cols), bf16),
            vm((n_shard, rows_e, cols), bf16),
            vm((rows_e, qkv_cols), bf16),
            vm((n_shard,) + small_rows, f32),
            vm((n_shard - 1,) + small_rows, f32),
            vm(small_rows, f32),
            vm((chips - 1,) + small_rows, f32),
        ],
        [
            sds((tok, width), f32),
            sds((n_expert, rows_e, qkv_cols), bf16),
            sds((n_expert, share, width), bf16),
            sds(small_rows, f32),
        ],
        56,
        in_specs=[any_spec] * 3 + [vmem_spec] * 6 + [any_spec],
        out_specs=[vmem_spec, any_spec, any_spec, vmem_spec],
    )(d_qkv, heads, a, gx1, hidden_in, gains, gain_two, g_router, qk_gain, share_out)

    def settle(own, others, other):
        total = own.astype(f32) + jnp.sum(others.astype(f32), axis=0)
        other = other.astype(f32)
        return jnp.stack([jnp.where(mine == 0, total, other), jnp.where(mine == 0, other, total)])[None]

    own_gate_up = lax.dynamic_index_in_dim(grad_gate_up, me_z, 0, keepdims=False)
    own_down = lax.dynamic_slice_in_dim(grad_down, me_z * d_slice, d_slice, 1)
    qk_grad = lax.dynamic_slice_in_dim(sums[2:4, :HEAD_DIM], me_z * qk_part, qk_part, 1)
    return (
        hidden_out,
        grad_hidden,
        sums[0:2][None],
        qk_grad[None],
        grad_qkv.reshape(d_slice, qkv_cols).astype(f32)[None],
        grad_out.reshape(hd, width).astype(f32)[None],
        sums[8 : 8 + experts_all].T[None],
        settle(own_gate_up, own_gu, two_gu),
        settle(own_down, own_dn, two_dn),
    )


def solution(mesh):
    in_specs = (
        P(("expert", "shard"), None),
        P(("expert", "shard")),
        P(("expert", "shard"), None),
        P(None, None, "shard"),
        P(None, None, "shard"),
        P(None, "shard", None),
        P(None, "shard", None),
        P(None, "shard", None),
        P(None, "expert", "shard", None),
        P(None, "expert", None, "shard"),
        P(("expert", "shard"), None),
    )
    out_specs = (
        P(("expert", "shard"), None),
        P(("expert", "shard"), None),
        P(None, None, "shard"),
        P(None, None, "shard"),
        P(None, "shard", None),
        P(None, "shard", None),
        P(None, "shard", None),
        P(None, "expert", "shard", None),
        P(None, "expert", None, "shard"),
    )
    return jax.shard_map(shards, mesh=mesh, in_specs=in_specs, out_specs=out_specs, check_vma=False)
```

time: 2470 us -> 916 us (0.37)
  waiting for transfers between devices: 1930 us -> 0 us
  Pallas kernels: 0 us -> 751 us
  blocking collectives: 158 us -> 0 us
  local copies, waits for them, and re-layouts: 95.4 us -> 10.5 us
  matrix products: 163 us -> 107 us
  other arithmetic: 75.8 us -> 37.4 us
    reduce_scatter x6 -> x0, waiting for transfers between devices: 885 us -> none  [the longest x1 350 us: shards(): lax.psum_scatter(grad_qkv.astype(jnp.bfloat16), 'shard', scatter_dimensio...]
    pallas_call x0 -> x4, Pallas kernels: none -> 751 us  [call(): pl.pallas_call(kernel, out_shape=outs, in_specs=in_specs or [any_spec] *...]
    all_gather x4 -> x0, waiting for transfers between devices: 733 us -> none  [the longest x1 301 us: shards(): qkv_weight = lax.all_gather(w_qkv[layer_index], 'shard', axis=0, tiled=True)]
    psum x1 -> x0, waiting for transfers between devices: 137 us -> none  [shards(): lax.psum(qkv_part.astype(jnp.bfloat16), 'expert').astype(jnp.float32)]
    all_gather x6 -> x0, blocking collectives: 134 us -> none  [the longest x1 32.1 us: shards(): lax.all_gather(key_rows.astype(jnp.bfloat16), 'shard', axis=0, tiled=True)]
    all_to_all x4 -> x0, waiting for transfers between devices: 130 us -> none  [the longest x1 53 us: shards(): lax.all_to_all(rows_grad, 'expert', split_axis=0, concat_axis=0, tiled=True)]
    dot_general x21 -> x8, matrix products: 163 us -> 107 us  [dot(): lax.dot_general(left, right, (dims, ((), ())), preferred_element_type=out)]
    unnamed x17 -> x0, waiting for transfers between devices: 45.3 us -> none
  transfers between devices with their start and end apart: 18 -> 0, of which waited for: 15 -> 0; matrix products, arithmetic and copies ran while one was open for 10% -> 0% of each run, Pallas kernels for 0% -> 0%
where the time goes in v1:
time: 916 us; the launch traced here: 907 us
  Pallas kernels  751 us (82%)
  matrix products  107 us (12%)
  other arithmetic  37.4 us (4%)
  local copies, waits for them, and re-layouts  10.5 us (1%)
    pallas_call x4, Pallas kernels, call(): pl.pallas_call(kernel, out_shape=outs, in_specs=in_specs or [any_spec] *...  751 us
    dot_general x8, matrix products, dot(): lax.dot_general(left, right, (dims, ((), ())), preferred_element_type=out)  107 us

profile of v1, /device:TPU:0, one launch (start us, length us, event | category | flops | bytes accessed | tf_op | source)
XLA Modules:
  0.0 906.7 jit_solution(15823855795396968469)
XLA Ops:
  0.6 0.7 scatter.14
  1.3 1.5 dynamic_update_slice.3
  2.8 0.7 fusion.17
  3.5 0.1 scatter.18
  3.6 1.3 pad_maximum_fusion.5.small
  5.0 0.7 broadcast_in_dim.101.seg_own
  5.7 0.8 copy.24
  6.5 0.9 convert_reduce_fusion.mask
  7.3 1.0 fusion.10
  8.3 1.0 pad_maximum_fusion.3
  9.4 338.6 %shard_map.178 = (bf16[4,32,512]{2,1,0:T(8,128)(2,1)}, f32[512,128]{1,0:T(8,128)}, bf16[4,8,64,1280]{3,2,1,0:T(8,128)(2,1)}, bf16[512,2048]{1,0:T(8,128)(2,1)}, ...) custom-call(bf16[128,2048]{1,0:T(8,128)(2,1)} %x.11, ...), custom_call_target="tpu_custom_call" | custom-call | tf_op jit(solution)/shard_map/pallas_call | solution.py:152
  348.0 19.5 %fusion.20 = f32[2048,1536]{0,1:T(8,128)} fusion(bf16[2048,2048]{1,0:T(8,128)(2,1)} %bitcast.83, bf16[2048,1536]{1,0:T(8,128)(2,1)} %bitcast.101), kind=kOutput, calls=%fused_computation.67 | convolution fusion | flops 12884901888 | bytes 27262976 | tf_op jit(solution)/shard_map/dot_general | solution.py:24
  367.6 0.2 copy.29
  367.8 5.7 fusion.18
  373.5 0.1 fusion.11
  373.6 0.1 select_reduce_fusion
  373.7 8.2 fusion.1
  381.9 18.4 %multiply_convert_fusion.2 = (bf16[2048,768]{0,1:T(8,128)(2,1)}, bf16[2048,768]{0,1:T(8,128)(2,1)}, bf16[2048,768]{0,1:T(8,128)(2,1)}) fusion(f32[2048,1536]{0,1:T(8,128)} %fusion.20, bf16[2048,2048]{1,0:T(8,128)(2,1)} %fusion.1, bf16[768,2048]{1,0:T(8,128)(2,1)} %get-tuple-element.83), kind=kOutput, calls=%fused_computation.13 | convolution fusion | flops 6466043904 | bytes 33554432 | tf_op jit(solution)/shard_map/dot_general | solution.py:24
  400.2 19.5 %convolution_convert_fusion.1 = bf16[2048,2048]{1,0:T(8,128)(2,1)} fusion(bf16[2048,1536]{1,0:T(8,128)(2,1)} %bitcast.102, bf16[2048,768]{0,1:T(8,128)(2,1)} %get-tuple-element.114, bf16[2048,768]{0,1:T(8,128)(2,1)} %get-tuple-element.113), kind=kOutput, calls=%fused_computation.7 | convolution fusion | flops 12901679104 | bytes 20971520 | tf_op jit(solution)/shard_map/dot_general | solution.py:24
  419.8 0.0 copy-done.12
  419.8 13.3 %fusion = (bf16[2048,2048]{1,0:T(8,128)(2,1)}, f32[2048]{0:T(1024)S(1)}) fusion(f32[2048]{0:T(1024)S(1)} %select_reduce_fusion, bf16[8,256,2048]{2,1,0:T(8,128)(2,1)} %get-tuple-element.82, bf16[2048,768]{0,1:T(8,128)(2,1)} %get-tuple-element.115, bf16[768,2048]{1,0:T(8,128)(2,1)S(1)} %copy-done.12), kind=kOutput, calls=%fused_computation.3 | convolution fusion | flops 6471809024 | bytes 23085056 | tf_op jit(solution)/shard_map/dot_general | solution.py:24
  433.1 1.4 select_convert_fusion.ex
  434.5 19.5 %convolution_convert_fusion.2 = bf16[2048,1536]{1,0:T(8,128)(2,1)} fusion(bf16[2048,2048]{1,0:T(8,128)(2,1)} %bitcast.85, bf16[2048,768]{0,1:T(8,128)(2,1)} %get-tuple-element.114, bf16[2048,768]{0,1:T(8,128)(2,1)} %get-tuple-element.113), kind=kOutput, calls=%fused_computation.8 | convolution fusion | flops 12900630528 | bytes 20971520 | tf_op jit(solution)/shard_map/dot_general | solution.py:24
  454.0 10.2 %convolution_convert_fusion.3.gdn = bf16[768,2048]{1,0:T(8,128)(2,1)} fusion(bf16[2048,768]{0,1:T(8,128)(2,1)S(1)} %copy-done.13, bf16[2048,2048]{1,0:T(8,128)(2,1)} %fusion.1), kind=kOutput, calls=%fused_computation.20 | convolution fusion | flops 6444023808 | bytes 14680064 | tf_op jit(solution)/shard_map/dot_general | solution.py:24
  464.3 0.4 fusion.19
  464.6 0.2 fusion.13
  464.8 0.1 fusion.12
  465.0 0.6 concatenate.29.rw
  465.6 0.8 concatenate.30.router_t
  466.5 0.7 pad_convert_fusion.gains
  467.1 153.7 %shard_map.179 = (f32[128,2048]{1,0:T(8,128)}, bf16[512,2048]{1,0:T(8,128)(2,1)}, f32[8,2048]{1,0:T(8,128)}, f32[128,2048]{1,0:T(8,128)}, bf16[1,512,1536]{2,1,0:T(8,128)(2,1)}, /*index=5*/bf16[1,768,512]{2,1,0:T(8,128)(2,1)}) custom-call(bf16[8,256,2048]{2,1,0:T(8,128)(2,1)} %bitcast.86, bf16[8,256,128]{2,1,0:T(8,128)(2,1)} %select_convert_fusion.ex, ...), custom_call_target="tpu_custom_call" | custom-call | tf_op jit(solution)/shard_map/pallas_call | solution.py:152
  620.8 136.4 %shard_map.180 = (bf16[512,1280]{1,0:T(8,128)(2,1)}, f32[16,128]{1,0:T(8,128)}, bf16[128,2048]{1,0:T(8,128)(2,1)}, bf16[128,2048]{1,0:T(8,128)(2,1)}, bf16[512,1...) custom-call(bf16[512,2048]{1,0:T(8,128)(2,1)} %get-tuple-element.87., ...), custom_call_target="tpu_custom_call" | custom-call | tf_op jit(solution)/shard_map/pallas_call | solution.py:152
  757.2 122.2 %shard_map.181 = (f32[128,2048]{1,0:T(8,128)}, bf16[8,64,5120]{2,1,0:T(8,128)(2,1)}, bf16[8,128,2048]{2,1,0:T(8,128)(2,1)}, f32[24,512]{1,0:T(8,128)}) custom-call(bf16[512,1280]{1,0:T(8,128)(2,1)} %get-tuple-element.97.d_qkv_h, bf16[4,8,64,1280]{3,2,1,0:T(8,128)(2,1)} %get-tuple-element.98.heads_h, bf16[512,2048]{1,0:T(8,128)(2,1)} %get-tuple-element.99.a_h, ...), custom_call_target="tpu_custom_call" | custom-call | tf_op jit(solution)/shard_map/pallas_call | solution.py:152
  879.4 1.3 slice_bitcast_fusion.2
  880.7 0.7 slice.89
  881.4 0.6 dynamic-slice_bitcast_fusion
  882.0 8.1 bitcast_convert_fusion
  890.1 0.0 copy-done
  890.1 4.4 bitcast_convert_fusion.1
  894.5 0.6 slice_bitcast_fusion.1
  895.2 0.0 copy-done.2
  895.2 2.4 fusion.4
  897.6 3.2 maximum_bitcast_fusion
  900.7 0.0 copy-done.5
  900.7 1.7 fusion.6
  902.5 2.0 maximum_bitcast_fusion.1
  904.5 0.8 copy.35
  905.2 1.0 copy.36
  (33 shorter events, 0.1 us)
Async XLA Ops:
  348.0 19.6 %copy-start.10 = (bf16[4,32,512]{2,1,0:T(8,128)(2,1)S(1)}, bf16[4,32,512]{2,1,0:T(8,128)(2,1)}, u32[]{:S(2)}) copy-start(bf16[4,32,512]{2,1,0:T(8,128)(2,1)} %get-tuple-element.81.small) | copy-start | bytes 393220
  348.0 19.6 %copy-start.8 = (bf16[8,256,128]{2,1,0:T(8,128)(2,1)S(1)}, bf16[8,256,128]{2,1,0:T(8,128)(2,1)}, u32[]{:S(2)}) copy-start(bf16[8,256,128]{2,1,0:T(8,128)(2,1)} %get-tuple-element.79) | copy-start | bytes 1572868
  400.2 19.5 %copy-start.12 = (bf16[768,2048]{1,0:T(8,128)(2,1)S(1)}, bf16[768,2048]{1,0:T(8,128)(2,1)}, u32[]{:S(2)}) copy-start(bf16[768,2048]{1,0:T(8,128)(2,1)} %get-tuple-element.83) | copy-start | bytes 9437188
  434.5 19.5 %copy-start.13 = (bf16[2048,768]{0,1:T(8,128)(2,1)S(1)}, bf16[2048,768]{0,1:T(8,128)(2,1)}, u32[]{:S(2)}) copy-start(bf16[2048,768]{0,1:T(8,128)(2,1)} %get-tuple-element.115) | copy-start | bytes 9437188
  454.0 10.2 %copy-start.6 = (bf16[128,128]{1,0:T(8,128)(2,1)S(1)}, bf16[128,128]{1,0:T(8,128)(2,1)}, u32[]{:S(2)}) copy-start(bf16[128,128]{1,0:T(8,128)(2,1)} %convert_reduce_fusion.mask) | copy-start | bytes 98308
  454.0 10.2 %copy-start.7 = (bf16[128,2048]{1,0:T(8,128)(2,1)S(1)}, bf16[128,2048]{1,0:T(8,128)(2,1)}, u32[]{:S(2)}) copy-start(bf16[128,2048]{1,0:T(8,128)(2,1)} %get-tuple-element.86.b) | copy-start | bytes 1572868
  882.0 8.1 copy-start
  890.1 4.5 copy-start.11
  890.1 5.1 copy-start.1
  890.1 5.1 copy-start.2
  897.5 3.2 copy-start.4
  897.6 3.2 copy-start.5
  900.7 3.7 copy-start.9
  900.7 4.5 copy-start.3

commit v2 on v1

--- a/solution.py
+++ b/solution.py
@@ -101,6 +101,10 @@
         copy = pltpu.make_async_copy(src, dst, self.local.at[i])
         copy.start()
         return copy
+
+    def done(self, copy):
+        copy.wait_send()
+        self.open = [c for c in self.open if c is not copy]
 
     def sent(self):
         for copy in self.open:
@@ -179,102 +183,6 @@
     return list(range(1, at.chips)) + [0]
 
 
-def norm_kernel(
-    dims, db, ex, ggu, gdn, x1, b, cot, rw, router_t, gains,
-    gx1, do_all, gain_two, g_router, land_gu, land_dn,
-    own, own_x, core_in, core_x, chip_in, chip_x, half_out, half_x, swap_in, swap_x, logit, d_out,
-    send, recv, local,
-):
-    at = Place(*dims)
-    net = Net(send, recv, local)
-    z, e, group = at.z, at.e, at.group
-    tok = x1.shape[0]
-    loads = {}
-    for t in halves(at):
-        loads[t] = (net.copy(db.at[at.slot(t)], own.at[t]), net.copy(ex.at[at.slot(t)], own_x.at[t]))
-    greet(everyone(at))
-    mates = {}
-    for t in halves(at):
-        mates[t] = (
-            net.push(db.at[at.slot(t, 1)], core_in.at[t], at.mate()),
-            net.push(ex.at[at.slot(t, 1)], core_x.at[t], at.mate()),
-        )
-    d_slice = ggu.shape[1]
-    landed = []
-    for t in range(1, group):
-        j = z ^ t ^ group
-        landed.append(net.push(gdn.at[:, pl.ds(pl.multiple_of(j * d_slice, d_slice), d_slice)], land_dn.at[t - 1], at.z_dev(t)))
-        landed.append(net.push(ggu.at[j], land_gu.at[t - 1], at.z_dev(t)))
-    step = 16
-    ins = []
-    for t in halves(at):
-        for c in loads[t]:
-            c.wait()
-        arrive(mates[t])
-
-        def add(i, _, t=t):
-            rows = pl.ds(pl.multiple_of(i * step, step), step)
-            own[t, rows, :] = (own[t, rows, :].astype(f32) + core_in[t, rows, :].astype(f32)).astype(bf16)
-            own_x[t, rows, :] = (own_x[t, rows, :].astype(f32) + core_x[t, rows, :].astype(f32)).astype(bf16)
-            return 0
-
-        lax.fori_loop(0, 2 * tok // step, add, 0)
-        if t:
-            ins.append(net.push(own.at[t], chip_in.at[t - 1], at.chip_dev(t)))
-            ins.append(net.push(own_x.at[t], chip_x.at[t - 1], at.chip_dev(t)))
-    arrive(ins)
-
-    def partner(i, _):
-        rows = pl.ds(pl.multiple_of(i * step, step), step)
-        src = pl.ds(pl.multiple_of(tok + i * step, step), step)
-        total, total_x = own[0, src, :].astype(f32), own_x[0, src, :].astype(f32)
-        for t in range(1, at.chips):
-            total += chip_in[t - 1, src, :].astype(f32)
-            total_x += chip_x[t - 1, src, :].astype(f32)
-        half_out[rows, :] = total.astype(bf16)
-        half_x[rows, :] = total_x.astype(bf16)
-        return 0
-
-    lax.fori_loop(0, tok // step, partner, 0)
-    swaps = [net.push(half_out, swap_in, at.z_dev(group)), net.push(half_x, swap_x, at.z_dev(group))]
-    arrive(swaps)
-    gain_two[...] = jnp.zeros_like(gain_two)
-
-    def owner(i, _):
-        rows = pl.ds(pl.multiple_of(i * step, step), step)
-        grad = own[0, rows, :].astype(f32) + swap_in[rows, :].astype(f32)
-        routed = own_x[0, rows, :].astype(f32) + swap_x[rows, :].astype(f32)
-        for t in range(1, at.chips):
-            grad += chip_in[t - 1, rows, :].astype(f32)
-            routed += chip_x[t - 1, rows, :].astype(f32)
-        routed = routed + pltpu.roll(routed, 64, 1)
-        weight = rw[rows, :]
-        d_logit = weight * (routed - jnp.sum(weight * routed, axis=1, keepdims=True))
-        high = d_logit.astype(bf16)
-        low = (d_logit - high.astype(f32)).astype(bf16)
-        logit[0, rows, :] = high
-        logit[1, rows, :] = low
-        grad += mm(high, router_t[...]) + mm(low, router_t[...])
-        value = x1[rows, :]
-        r = inv_rms(value)
-        c = grad * gains[1:2, :]
-        back = cot[rows, :].astype(f32) + r * c - value * (r * r * r * jnp.mean(c * value, axis=-1, keepdims=True))
-        gx1[rows, :] = back
-        d_out[rows, :] = back.astype(bf16)
-        per = grad * value * r
-        gain_two[...] += per[:8] + per[8:]
-        return 0
-
-    lax.fori_loop(0, tok // step, owner, 0)
-    mine = do_all.at[pl.ds(pl.multiple_of(z * tok, tok), tok)]
-    keep = net.copy(d_out, mine)
-    copies = [net.push(d_out, mine, at.z_dev(t)) for t in range(1, at.n_shard)]
-    g_router[...] = mm_tn(logit[0], b[...]) + mm_tn(logit[1], b[...])
-    keep.wait()
-    arrive(copies + landed)
-    net.sent()
-
-
 def rope_rows(value, cos, sin):
     return value * cos + pltpu.roll(value, HEAD_DIM // 2, 1) * sin
 
@@ -308,7 +216,7 @@
 def front_kernel(
     dims, x, small, seg_own, w_qkv, w_out, w_gu, w_dn, cot, mask, cos_h, sin_h,
     small_out, seg_out, heads_out, a_out, raw_out, q_out, k_out, v_out, o_out, x1_out, b_out,
-    gate_up, down, cot_all, mask_all, b_all,
+    gate_up, down, cot_all, mask_all, b_pair,
     x_all, small_all, seg_col, heads, a, raw, q, k, v, o, w_o, part, parts_in, cos, sin, gains, seg_row, x1, b_own,
     send, recv, local,
 ):
@@ -366,10 +274,27 @@
         c.wait()
     arrive(got_x)
     other = (z ^ group) // group
-    from_partner = [
-        (net.push(w_gu.at[other], gate_up.at[z], at.z_dev(group)), gate_up.at[z ^ group]),
-        (net.push(w_dn.at[other], d_cols(down, z), at.z_dev(group)), d_cols(down, z ^ group)),
+    cut = d_slice // 2
+    low, high = pl.ds(0, cut), pl.ds(cut, cut)
+    pieces_w = [
+        (w_gu.at[other, low], gate_up.at[z, low], gate_up.at[z ^ group, low]),
+        (w_gu.at[other, high], gate_up.at[z, high], gate_up.at[z ^ group, high]),
+        (w_dn.at[other], d_cols(down, z), d_cols(down, z ^ group)),
     ]
+    from_partner = {}
+
+    def fetch_piece(i):
+        src, dst, got = pieces_w[i]
+        from_partner[i] = (net.push(src, dst, at.z_dev(group)), got)
+
+    fetch_piece(0)
+
+    def hand_on(i):
+        copy, ref = from_partner[i]
+        copy.wait_recv()
+        for t in range(1, group):
+            got_w.append(net.push(ref, ref, at.z_dev(t)))
+
     got_w = []
     for t in range(1, group):
         got_w.append(net.push(w_gu.at[mine], gate_up.at[z], at.z_dev(t)))
@@ -431,6 +356,8 @@
     cots = [lambda who: cot_all.at[who], lambda who: mask_all.at[who]]
     cot_state = spread(net, at, cots)
 
+    fetch_piece(1)
+
     def one_head(h, _):
         for i in range(length // block):
             soft = soft_block(q, k, seg_row, seg_col, h, i, block, scale).astype(bf16)
@@ -439,6 +366,8 @@
         return 0
 
     lax.fori_loop(0, n_heads, one_head, 0)
+    hand_on(0)
+    fetch_piece(2)
     keep.append(net.copy(o, o_out))
     load_out.wait()
     wide_o = tiled(width, 256)
@@ -451,10 +380,7 @@
     lax.fori_loop(0, width // wide_o, out_tile, 0)
     sums = [net.push(part.at[span(z ^ t, tok)], parts_in.at[t - 1], at.z_dev(t)) for t in range(1, at.n_shard)]
     last = pass_on(net, at, cots, cot_state)
-    for copy, ref in from_partner:
-        copy.wait_recv()
-        for t in range(1, group):
-            got_w.append(net.push(ref, ref, at.z_dev(t)))
+    hand_on(1)
     arrive(sums)
 
     def middle_rows(i, _):
@@ -468,24 +394,361 @@
         return 0
 
     lax.fori_loop(0, tok // step, middle_rows, 0)
-    local_b = net.copy(b_own, b_all.at[e, half0])
-    swap = net.push(b_own, b_all.at[e, half1], at.z_dev(group))
-    keep += [net.copy(x1, x1_out), net.copy(b_own, b_out)]
-    local_b.wait()
+    swap = net.push(b_own, b_pair.at[half1], at.z_dev(group))
+    keep += [net.copy(b_own, b_pair.at[half0]), net.copy(x1, x1_out), net.copy(b_own, b_out)]
+    hand_on(2)
     swap.wait_recv()
-    rows_b = [lambda who: b_all.at[who]]
-    last += pass_on(net, at, rows_b, spread(net, at, rows_b))
     arrive(last + got_w)
     for c in keep + here:
         c.wait()
     net.sent()
 
 
+def expert_kernel(
+    dims, b_pair, cot_all, mask_all, gate_up, down, router_t,
+    out_part, ggu, gdn, db_in, ex_in, land_gu, land_dn, core_in, core_x,
+    w_gu, w_dn, rows, cot_t, mask_t, gu, hid, d_pre, d_y, stage, stage_x, own, own_x, add, add_x, w_r, d_r, g_tile, d_tile,
+    tile_sem, send, recv, local,
+):
+    at = Place(*dims)
+    net = Net(send, recv, local)
+    z, e, group = at.z, at.e, at.group
+    n_slices, d_slice, ff2 = gate_up.shape
+    ff, width = w_dn.shape
+    two = b_pair.shape[0]
+    four = 2 * two
+    expert = e * (at.n_shard // group) + z // group
+    step = 16
+    fine = tiled(ff, 256)
+    wide = tiled(width, 512)
+
+    pair = net.copy(b_pair, rows.at[0, 1])
+    loads = [net.copy(gate_up.at[s], w_gu.at[pl.ds(s * d_slice, d_slice)]) for s in range(n_slices)]
+    loads.append(net.copy(down, w_dn))
+
+    def fetch(t):
+        return [
+            net.copy(cot_all.at[at.slot(t, 1)], cot_t.at[0]),
+            net.copy(cot_all.at[at.slot(t)], cot_t.at[1]),
+            net.copy(mask_all.at[at.slot(t, 1)], mask_t.at[0]),
+            net.copy(mask_all.at[at.slot(t)], mask_t.at[1]),
+        ]
+
+    fetched = fetch(0)
+    greet([at.chip_dev(t) for t in range(1, at.chips)] + [at.mate()] + [at.z_dev(t) for t in range(1, group)])
+    from_mate = {0: net.push(b_pair, rows.at[0, 0], at.mate())}
+    near = [t for t in (1, 2) if t < at.chips]
+    far = [t for t in range(1, at.chips) if t not in near]
+    from_chip = {t: net.push(b_pair, rows.at[t, 1], at.chip_dev(t)) for t in near}
+
+    def pass_rows(t):
+        from_chip[t].wait_recv()
+        from_mate[t] = net.push(rows.at[t, 1], rows.at[t, 0], at.mate())
+
+    mates, outs = {}, []
+
+    def finish(t):
+        arrive(mates[t])
+        c, cx = net.copy(core_in.at[t], add), net.copy(core_x.at[t], add_x)
+        c.wait()
+        cx.wait()
+
+        def add_rows(i, _):
+            r = span(i, step)
+            own[t, r, :] = (own[t, r, :].astype(f32) + add[r, :].astype(f32)).astype(bf16)
+            own_x[t, r, :] = (own_x[t, r, :].astype(f32) + add_x[r, :].astype(f32)).astype(bf16)
+            return 0
+
+        lax.fori_loop(0, two // step, add_rows, 0)
+        if t:
+            outs.append(net.push(own.at[t], db_in.at[t], at.chip_dev(t)))
+            outs.append(net.push(own_x.at[t], ex_in.at[t], at.chip_dev(t)))
+
+    lanes = lax.broadcasted_iota(jnp.int32, (four, 128), 1)
+    used = {}
+
+    def work(t, fetched, before, after):
+        logits = mm_nt(rows[t].reshape(four, width), router_t[...])
+        chosen = mask_t[...].reshape(four, 128).astype(f32) > 0
+        masked = jnp.where(chosen, logits, neg_fill)
+        raised = jnp.where(chosen, jnp.exp(masked - jnp.max(masked, axis=1, keepdims=True)), 0.0)
+        weight = raised / jnp.sum(raised, axis=1, keepdims=True)
+        weight = jnp.sum(jnp.where(lanes == expert, weight, 0.0), axis=1, keepdims=True)
+        w_r[...] = jnp.broadcast_to(weight, (four, 128))
+        d_r[...] = jnp.zeros_like(d_r)
+
+        def up(j, _):
+            tile, tile_u = span(j, fine), pl.ds(pl.multiple_of(ff + j * fine, fine), fine)
+            x = rows[t].reshape(four, width)
+            g = mm(x, w_gu[:, tile])
+            u = mm(x, w_gu[:, tile_u])
+            gu[:, tile] = g
+            gu[:, tile_u] = u
+            hid[t, :, tile] = (g * jax.nn.sigmoid(g) * u).astype(bf16)
+            return 0
+
+        lax.fori_loop(0, ff // fine, up, 0)
+        before()
+        for c in fetched:
+            c.wait()
+
+        def back_y(n, _):
+            tile = span(n, wide)
+            y = mm(hid[t], w_dn[:, tile]).astype(bf16).astype(f32)
+            c = cot_t[:, :, tile].reshape(four, wide).astype(f32)
+            w = w_r[:, 0:1]
+            d_r[...] += jnp.broadcast_to(jnp.sum(c * y, axis=1, keepdims=True), (four, 128))
+            d_y[t, :, tile] = (w * c).astype(bf16)
+            cot_t[:, :, tile] = (w * y).astype(bf16).reshape(2, two, wide)
+            return 0
+
+        lax.fori_loop(0, width // wide, back_y, 0)
+        kept = [
+            net.copy(cot_t.at[0], out_part.at[at.slot(t, 1)]),
+            net.copy(cot_t.at[1], out_part.at[at.slot(t)]),
+        ]
+
+        def back_h(j, _):
+            tile, tile_u = span(j, fine), pl.ds(pl.multiple_of(ff + j * fine, fine), fine)
+            d_h = mm_nt(d_y[t], w_dn[tile, :])
+            g, u = gu[:, tile], gu[:, tile_u]
+            sig = jax.nn.sigmoid(g)
+            d_pre[t, :, tile] = (d_h * u * sig * (1.0 + g * (1.0 - sig))).astype(bf16)
+            d_pre[t, :, tile_u] = (d_h * g * sig).astype(bf16)
+            return 0
+
+        lax.fori_loop(0, ff // fine, back_h, 0)
+        for c in kept:
+            c.wait()
+        after()
+        p = t % 2
+        for c in used.pop(p, []):
+            net.done(c)
+
+        def back_b(n, _):
+            tile = span(n, wide)
+            value = mm_nt(d_pre[t], w_gu[tile, :]).astype(bf16)
+            stage[p, :, tile] = value[:two]
+            own[t, :, tile] = value[two:]
+            return 0
+
+        lax.fori_loop(0, width // wide, back_b, 0)
+        routed = d_r[...]
+        high = routed.astype(bf16)
+        low = (routed - high.astype(f32)).astype(bf16)
+        none = jnp.zeros_like(high)
+        extra = jnp.where(lanes == expert, high, jnp.where(lanes == expert + 64, low, none))
+        stage_x[p] = extra[:two]
+        own_x[t] = extra[two:]
+        mates[t] = [
+            net.push(stage.at[p], core_in.at[t], at.mate()),
+            net.push(stage_x.at[p], core_x.at[t], at.mate()),
+        ]
+        used[p] = mates[t]
+
+    pair.wait()
+    from_mate[0].wait_recv()
+    for c in loads:
+        c.wait()
+    for c in fetched[2:]:
+        c.wait()
+    order = list(range(at.chips))
+    state = {"next": fetched[:2]}
+    for t in order:
+        if t == 1:
+            for i in near:
+                pass_rows(i)
+            for i in far:
+                from_chip[i] = net.push(b_pair, rows.at[i, 1], at.chip_dev(i))
+        if t:
+            if t in far:
+                pass_rows(t)
+            from_mate[t].wait_recv()
+
+        def before(t=t):
+            if t:
+                finish(t - 1)
+
+        def after(t=t):
+            if t + 1 < at.chips:
+                more = fetch(t + 1)
+                state["next"] = more[:2]
+                state["mask"] = more[2:]
+
+        work(t, state["next"], before, after)
+        for c in state.pop("mask", []):
+            c.wait()
+    finish(at.chips - 1)
+    keep = [net.copy(own.at[0], db_in.at[0]), net.copy(own_x.at[0], ex_in.at[0])]
+
+    part = tiled(width, 256)
+    per = d_slice // part
+
+    def out_copy(slot, i):
+        who = z ^ (n_slices - 1 - i // per)
+        return pltpu.make_async_copy(g_tile.at[slot], ggu.at[who, span(i % per, part)], tile_sem.at[slot])
+
+    def grad_up(i, _):
+        slot = i % 2
+
+        @pl.when(i >= 2)
+        def _():
+            out_copy(slot, i - 2).wait()
+
+        who = z ^ (n_slices - 1 - i // per)
+        x = rows[:, :, :, span(who * per + i % per, part)].reshape(at.chips * four, part)
+        g_tile[slot] = mm_tn(x, d_pre[...].reshape(at.chips * four, ff2)).astype(bf16)
+        out_copy(slot, i).start()
+        return 0
+
+    def down_copy(slot, i):
+        return pltpu.make_async_copy(d_tile.at[slot], gdn.at[span(i, fine)], tile_sem.at[slot])
+
+    def grad_down(i, _):
+        slot = i % 2
+
+        @pl.when(i >= 2)
+        def _():
+            down_copy(slot, i - 2).wait()
+
+        h = hid[:, :, span(i, fine)].reshape(at.chips * four, fine)
+        d_tile[slot] = mm_tn(h, d_y[...].reshape(at.chips * four, width)).astype(bf16)
+        down_copy(slot, i).start()
+        return 0
+
+    n_down = ff // fine
+    lax.fori_loop(0, n_down, grad_down, 0)
+    for i in range(max(0, n_down - 2), n_down):
+        down_copy(i % 2, i).wait()
+    for t in range(1, group):
+        outs.append(net.push(gdn.at[:, span(z ^ t ^ group, d_slice)], land_dn.at[t - 1], at.z_dev(t)))
+    n_up, n_early = width // part, (group - 1) * per
+    lax.fori_loop(0, n_early, grad_up, 0)
+    for i in range(n_early - 2, n_early):
+        out_copy(i % 2, i).wait()
+    half = pl.ds(0, d_slice // 2)
+    for t in range(1, group):
+        outs.append(net.push(ggu.at[z ^ t ^ group, half], land_gu.at[t - 1], at.z_dev(t)))
+
+    def grad_rest(i, _):
+        slot = i % 2
+
+        @pl.when(i >= n_early + 2)
+        def _():
+            out_copy(slot, i - 2).wait()
+
+        who = z ^ (n_slices - 1 - i // per)
+        x = rows[:, :, :, span(who * per + i % per, part)].reshape(at.chips * four, part)
+        g_tile[slot] = mm_tn(x, d_pre[...].reshape(at.chips * four, ff2)).astype(bf16)
+        out_copy(slot, i).start()
+        return 0
+
+    lax.fori_loop(n_early, n_up, grad_rest, 0)
+    for i in range(n_up - 2, n_up):
+        out_copy(i % 2, i).wait()
+    for c in keep:
+        c.wait()
+    arrive(outs)
+    net.sent()
+
+
+def norm_kernel(
+    dims, early, db, ex, ggu, gdn, out_part, x1, b, cot, rw, router_t, gains,
+    gx1, do_all, gain_two, g_router, land_gu, late_gu, land_dn, out_in,
+    own, own_x, half_out, half_x, swap_in, swap_x, logit, d_out, out_own, out_core,
+    send, recv, local,
+):
+    at = Place(*dims)
+    net = Net(send, recv, local)
+    z, e, group = at.z, at.e, at.group
+    tok = x1.shape[0]
+    n_parts = db.shape[0]
+    loads = [net.copy(db, own), net.copy(ex, own_x)]
+    load_own = {t: net.copy(out_part.at[at.slot(t)], out_own.at[t]) for t in halves(at)}
+    greet(everyone(at))
+    step = 16
+    for c in loads:
+        c.wait()
+
+    def sums(src):
+        total, total_x = own[0, src, :].astype(f32), own_x[0, src, :].astype(f32)
+        for t in range(1, n_parts):
+            total += own[t, src, :].astype(f32)
+            total_x += own_x[t, src, :].astype(f32)
+        return total, total_x
+
+    def partner(i, _):
+        total, total_x = sums(pl.ds(pl.multiple_of(tok + i * step, step), step))
+        half_out[span(i, step), :] = total.astype(bf16)
+        half_x[span(i, step), :] = total_x.astype(bf16)
+        return 0
+
+    lax.fori_loop(0, tok // step, partner, 0)
+    swaps = [net.push(half_out, swap_in, at.z_dev(group)), net.push(half_x, swap_x, at.z_dev(group))]
+    d_slice = ggu.shape[1]
+    landed = []
+    for t in range(1, group):
+        j = z ^ t ^ group
+        if not early:
+            landed.append(net.push(ggu.at[j, pl.ds(0, d_slice // 2)], land_gu.at[t - 1], at.z_dev(t)))
+            landed.append(net.push(gdn.at[:, span(j, d_slice)], land_dn.at[t - 1], at.z_dev(t)))
+        landed.append(net.push(ggu.at[j, pl.ds(d_slice // 2, d_slice // 2)], late_gu.at[t - 1], at.z_dev(t)))
+    mates = {t: net.push(out_part.at[at.slot(t, 1)], out_core.at[t], at.mate()) for t in halves(at)}
+    outs = []
+    for t in halves(at):
+        load_own[t].wait()
+        mates[t].wait_recv()
+
+        def add(i, _, t=t):
+            rows = span(i, step)
+            out_own[t, rows, :] = (out_own[t, rows, :].astype(f32) + out_core[t, rows, :].astype(f32)).astype(bf16)
+            return 0
+
+        lax.fori_loop(0, 2 * tok // step, add, 0)
+        if t:
+            outs.append(net.push(out_own.at[t], out_in.at[t], at.chip_dev(t)))
+    keep_own = net.copy(out_own.at[0], out_in.at[0])
+    arrive(swaps)
+    gain_two[...] = jnp.zeros_like(gain_two)
+
+    def owner(i, _):
+        rows = span(i, step)
+        grad, routed = sums(rows)
+        grad += swap_in[rows, :].astype(f32)
+        routed += swap_x[rows, :].astype(f32)
+        routed = routed + pltpu.roll(routed, 64, 1)
+        weight = rw[rows, :]
+        d_logit = weight * (routed - jnp.sum(weight * routed, axis=1, keepdims=True))
+        high = d_logit.astype(bf16)
+        low = (d_logit - high.astype(f32)).astype(bf16)
+        logit[0, rows, :] = high
+        logit[1, rows, :] = low
+        grad += mm(high, router_t[...]) + mm(low, router_t[...])
+        value = x1[rows, :]
+        r = inv_rms(value)
+        c = grad * gains[1:2, :]
+        back = cot[rows, :].astype(f32) + r * c - value * (r * r * r * jnp.mean(c * value, axis=-1, keepdims=True))
+        gx1[rows, :] = back
+        d_out[rows, :] = back.astype(bf16)
+        gain_two[...] += eight(grad * value * r)
+        return 0
+
+    lax.fori_loop(0, tok // step, owner, 0)
+    mine = do_all.at[span(z, tok)]
+    keep = net.copy(d_out, mine)
+    copies = [net.push(d_out, mine, at.z_dev(t)) for t in range(1, at.n_shard)]
+    g_router[...] = mm_tn(logit[0], b[...]) + mm_tn(logit[1], b[...])
+    keep.wait()
+    keep_own.wait()
+    arrive(copies + landed + outs)
+    net.sent()
+
+
 def back_kernel(
-    dims, do_h, w_out, o_h, q_h, k_h, v_h, raw_h, cos_h, sin_h, seg_h, small, ggu, gdn, land_gu, land_dn, out_part, x1,
-    d_qkv_out, qk_gain, share_out, hidden, two_gu, two_dn, own_gu, own_dn, out_core,
+    dims, do_h, w_out, o_h, q_h, k_h, v_h, raw_h, cos_h, sin_h, seg_h, small, ggu, gdn, land_gu, late_gu, land_dn, out_parts, x1,
+    d_qkv_out, qk_gain, g_att, hidden, two_gu, own_gu, far_dn,
     do_all, w_o, o, q, k, v, raw, cos, sin, seg_col, seg_row, mix, d_qkv, dk, dv,
-    sum_gu, add_gu, sum_dn, add_dn, out_own, out_add, out_in, half_out, swap_in, g_out, g_core, g_in,
+    sum_gu, add_gu, sum_dn, add_dn, out_in, half_out, swap_in, g_out, g_core, g_in, share_own,
     send, recv, local,
 ):
     at = Place(*dims)
@@ -506,15 +769,29 @@
         return ref.at[:, span(who, d_slice)]
 
     load_dn = [net.copy(d_cols(gdn, far), sum_dn)] + [net.copy(land_dn.at[t - 1], add_dn.at[t - 1]) for t in range(1, group)]
-    load_gu = [net.copy(ggu.at[far], sum_gu)] + [net.copy(land_gu.at[t - 1], add_gu.at[t - 1]) for t in range(1, group)]
+    cut = d_slice // 2
+    halves_gu = [pl.ds(0, cut), pl.ds(cut, cut)]
+    load_gu = [
+        [net.copy(ggu.at[far, r], sum_gu.at[i])] + [net.copy(land.at[t - 1], add_gu.at[i, t - 1]) for t in range(1, group)]
+        for i, (r, land) in enumerate(zip(halves_gu, (land_gu, late_gu)))
+    ]
     load_a = [net.copy(do_h, do_all), net.copy(o_h, o)]
-    load_own = {t: net.copy(out_part.at[at.slot(t)], out_own.at[t]) for t in halves(at)}
+    load_out = net.copy(out_parts, out_in)
     load_b = [
         net.copy(s, d)
         for s, d in ((w_out, w_o), (q_h, q), (k_h, k), (v_h, v), (raw_h, raw), (cos_h, cos), (sin_h, sin), (seg_h, seg_col))
     ]
     greet(everyone(at))
-    mates = {t: net.push(out_part.at[at.slot(t, 1)], out_core.at[t], at.mate()) for t in halves(at)}
+
+    def sum_in(rows):
+        total = out_in[0, rows, :].astype(f32)
+        for t in range(1, at.chips):
+            total += out_in[t, rows, :].astype(f32)
+        return total
+
+    def partner(i, _):
+        half_out[span(i, step), :] = sum_in(pl.ds(pl.multiple_of(tok + i * step, step), step)).astype(bf16)
+        return 0
 
     def add_up(total, adds):
         def rows_of(i, _):
@@ -527,21 +804,25 @@
 
         lax.fori_loop(0, total.shape[0] // step, rows_of, 0)
 
-    for c in load_gu:
-        c.wait()
-    add_up(sum_gu, add_gu)
-    got = [net.push(sum_gu, two_gu, at.z_dev(group))]
+    load_out.wait()
+    lax.fori_loop(0, tok // step, partner, 0)
+    swap = net.push(half_out, swap_in, at.z_dev(group))
+    got = []
+    for i in range(2):
+        for c in load_gu[i]:
+            c.wait()
+        add_up(sum_gu.at[i], add_gu.at[i])
+        got.append(net.push(sum_gu.at[i], two_gu.at[halves_gu[i]], at.z_dev(group)))
+    for t in range(1, group):
+        got.append(net.push(ggu.at[z ^ t], own_gu.at[t - 1], at.z_dev(t)))
     for c in load_dn:
         c.wait()
     add_up(sum_dn, add_dn)
-    got.append(net.push(sum_dn, two_dn, at.z_dev(group)))
-    for t in range(1, group):
-        got.append(net.push(ggu.at[z ^ t], own_gu.at[t - 1], at.z_dev(t)))
-        got.append(net.push(d_cols(gdn, z ^ t), own_dn.at[t - 1], at.z_dev(t)))
+    keep_dn = net.copy(sum_dn, far_dn)
 
     for c in load_a:
         c.wait()
-    share = share_out.shape[0]
+    share = share_own.shape[0]
 
     wide = tiled(hd, 256)
     each = wide // share
@@ -555,21 +836,6 @@
     lax.fori_loop(0, hd // wide, out_grad, 0)
     g_mates = {t: net.push(g_out.at[at.slot(t, 1)], g_core.at[t], at.mate()) for t in halves(at)}
 
-    outs = []
-    for t in halves(at):
-        load_own[t].wait()
-        mates[t].wait_recv()
-        c = net.copy(out_core.at[t], out_add)
-        c.wait()
-
-        def add(i, _, t=t):
-            rows = span(i, step)
-            out_own[t, rows, :] = (out_own[t, rows, :].astype(f32) + out_add[rows, :].astype(f32)).astype(bf16)
-            return 0
-
-        lax.fori_loop(0, 2 * tok // step, add, 0)
-        if t:
-            outs.append(net.push(out_own.at[t], out_in.at[t - 1], at.chip_dev(t)))
     for c in load_b:
         c.wait()
     qk = []
@@ -630,20 +896,6 @@
         qk_gain[8:16, :] += eight(per)
     keep = net.copy(d_qkv, d_qkv_out)
 
-    arrive(outs)
-
-    def sum_in(rows):
-        total = out_own[0, rows, :].astype(f32)
-        for t in range(1, at.chips):
-            total += out_in[t - 1, rows, :].astype(f32)
-        return total
-
-    def partner(i, _):
-        half_out[span(i, step), :] = sum_in(pl.ds(pl.multiple_of(tok + i * step, step), step)).astype(bf16)
-        return 0
-
-    lax.fori_loop(0, tok // step, partner, 0)
-    swap = net.push(half_out, swap_in, at.z_dev(group))
     arrive(g_outs)
 
     def own_share(i, _):
@@ -651,10 +903,14 @@
         total = g_out[e, rows, :].astype(f32)
         for t in range(1, at.chips):
             total += g_in[t - 1, rows, :].astype(f32)
-        share_out[rows, :] = total.astype(bf16)
+        share_own[rows, :] = total.astype(bf16)
         return 0
 
     lax.fori_loop(0, share // step, own_share, 0)
+    keep_att = net.copy(share_own, g_att.at[e])
+    keep_att.wait()
+    atts = [lambda who: g_att.at[who]]
+    att_state = spread(net, at, atts)
     swap.wait_recv()
 
     def hidden_rows(i, _):
@@ -663,14 +919,15 @@
         return 0
 
     lax.fori_loop(0, tok // step, hidden_rows, 0)
-    arrive(got)
+    arrive(pass_on(net, at, atts, att_state) + got)
     keep.wait()
+    keep_dn.wait()
     net.sent()
 
 
 def tail_kernel(
-    dims, d_qkv_h, heads_h, a_h, gx1, x, gains, gain_two, g_router, qk_gain, share_out,
-    g_hidden, g_qkv, g_att, small_sum,
+    dims, d_qkv_h, heads_h, a_h, gdn, far_dn, gx1, x, gains, gain_two, g_router, qk_gain,
+    g_hidden, g_qkv, small_sum, two_dn, own_dn,
     d_qkv, heads, a, part, parts_in, g_heads, core_in, chip_in, mine, turn_in, share, sm, sm_z, sm_core, sm_chip,
     send, recv, local,
 ):
@@ -686,26 +943,13 @@
     step = 16
     load_a = [net.copy(d_qkv_h, d_qkv), net.copy(heads_h, heads)]
     load_b = net.copy(a_h, a)
-    own_att = net.copy(share_out, g_att.at[e])
     greet(everyone(at))
-    own_att.wait()
-    atts = [lambda who: g_att.at[who]]
-    att_state = spread(net, at, atts)
     for c in load_a:
         c.wait()
 
     wide = tiled(d_slice, 256)
     each = wide // rows_e
 
-    def rows_tile(s, _):
-        for j in range(d_slice // wide):
-            some = heads[s, pl.ds(each * j, each)].reshape(wide, cols)
-            here = pl.ds(pl.multiple_of(s * d_slice + j * wide, wide), wide)
-            part[:, here] = mm_nt(d_qkv[...], some).astype(bf16)
-        return 0
-
-    lax.fori_loop(0, at.n_shard, rows_tile, 0)
-    sums = [net.push(part.at[span(z ^ t, tok)], parts_in.at[t - 1], at.z_dev(t)) for t in range(1, at.n_shard)]
     load_b.wait()
 
     def grad_tile(s, _):
@@ -718,6 +962,16 @@
 
     lax.fori_loop(0, at.n_shard, grad_tile, 0)
     mates = {t: net.push(g_heads.at[at.slot(t, 1)], core_in.at[t], at.mate()) for t in halves(at)}
+
+    def rows_tile(s, _):
+        for j in range(d_slice // wide):
+            some = heads[s, pl.ds(each * j, each)].reshape(wide, cols)
+            here = pl.ds(pl.multiple_of(s * d_slice + j * wide, wide), wide)
+            part[:, here] = mm_nt(d_qkv[...], some).astype(bf16)
+        return 0
+
+    lax.fori_loop(0, at.n_shard, rows_tile, 0)
+    sums = [net.push(part.at[span(z ^ t, tok)], parts_in.at[t - 1], at.z_dev(t)) for t in range(1, at.n_shard)]
     chips = []
     for t in halves(at):
         mates[t].wait_recv()
@@ -730,7 +984,21 @@
         lax.fori_loop(0, at.n_shard, add, 0)
         if t:
             chips.append(net.push(g_heads.at[who], chip_in.at[t - 1], at.chip_dev(t)))
-    atts_last = pass_on(net, at, atts, att_state)
+    arrive(chips)
+
+    def total(s, _):
+        value = g_heads[e, s].astype(f32)
+        for t in range(1, at.chips):
+            value += chip_in[t - 1, s].astype(f32)
+        mine[s] = value.astype(bf16)
+        return 0
+
+    lax.fori_loop(0, at.n_shard, total, 0)
+    turns = [net.push(mine.at[z ^ t], turn_in.at[z], at.z_dev(t)) for t in range(1, at.n_shard)]
+    turn_own = net.copy(mine.at[z], turn_in.at[z])
+    got = [net.push(far_dn, two_dn, at.z_dev(group))]
+    for t in range(1, group):
+        got.append(net.push(gdn.at[:, span(z ^ t, d_slice)], own_dn.at[t - 1], at.z_dev(t)))
     arrive(sums)
     sm[...] = jnp.zeros_like(sm)
     gain_one = jnp.zeros((8, width), f32)
@@ -759,24 +1027,6 @@
         sm[s, 3:4, pl.ds(0, HEAD_DIM)] = row_k
         sm[s, 8:, :] = g_router[0 : sm.shape[1] - 8, piece]
     small_z = [net.push(sm.at[z ^ t], sm_z.at[t - 1], at.z_dev(t)) for t in range(1, at.n_shard)]
-    arrive(chips)
-
-    def total(s, _):
-        value = g_heads[e, s].astype(f32)
-        for t in range(1, at.chips):
-            value += chip_in[t - 1, s].astype(f32)
-        mine[s] = value.astype(bf16)
-        return 0
-
-    lax.fori_loop(0, at.n_shard, total, 0)
-    turns = [net.push(mine.at[z ^ t], turn_in.at[z], at.z_dev(t)) for t in range(1, at.n_shard)]
-    turn_own = net.copy(mine.at[z], turn_in.at[z])
-    arrive(small_z)
-    value = sm[z]
-    for t in range(1, at.n_shard):
-        value += sm_z[t - 1]
-    sm[z] = value
-    c = net.push(sm.at[z], sm_core, at.mate())
     turn_own.wait()
     arrive(turns)
     for s in range(at.n_shard):
@@ -789,18 +1039,25 @@
                 value += turn_in[s, :, pl.ds(first, HEAD_DIM)].astype(f32)
             share[:, pl.ds(to * HEAD_DIM, HEAD_DIM)] = value.astype(bf16)
     keep = net.copy(share, g_qkv.at[e])
+    keep.wait()
+    qkvs = [lambda who: g_qkv.at[who]]
+    state = spread(net, at, qkvs)
+    arrive(small_z)
+    value = sm[z]
+    for t in range(1, at.n_shard):
+        value += sm_z[t - 1]
+    sm[z] = value
+    c = net.push(sm.at[z], sm_core, at.mate())
     c.wait_recv()
     sm_core[...] = sm[z] + sm_core[...]
     smalls = [net.push(sm_core, sm_chip.at[t - 1], at.chip_dev(t)) for t in range(1, at.chips)]
-    keep.wait()
-    qkvs = [lambda who: g_qkv.at[who]]
-    last = pass_on(net, at, qkvs, spread(net, at, qkvs))
+    last = pass_on(net, at, qkvs, state)
     arrive(smalls)
     value = sm_core[...]
     for t in range(1, at.chips):
         value += sm_chip[t - 1]
     small_sum[...] = value
-    arrive(last + atts_last)
+    arrive(last + got)
     net.sent()
 
 
@@ -870,7 +1127,7 @@
         sds((ff, width), bf16),
         sds((n_expert, 2 * tok, width), bf16),
         sds((n_expert, 2 * tok, 128), bf16),
-        sds((n_expert, 2 * tok, width), bf16),
+        sds((2 * tok, width), bf16),
     ]
     front = comm_call(
         functools.partial(front_kernel, dims),
@@ -901,7 +1158,7 @@
         outs,
         56,
     )
-    (small_all, seg_col, heads, a, raw, q, k, v, o, x1, b, gate_up, down, cot_all, mask_all, b_all) = front(
+    (small_all, seg_col, heads, a, raw, q, k, v, o, x1, b, gate_up, down, cot_all, mask_all, b_pair) = front(
         hidden_in, small, seg_own, w_qkv[0], w_attn_out[0], w_gate_up[0], w_down[0], cotangent, mask, cos, sin
     )
     gains = jnp.zeros((8, width), f32)
@@ -914,83 +1171,125 @@
         raised = jnp.where(chosen, jnp.exp(masked - jnp.max(masked, axis=1, keepdims=True)), 0.0)
         return raised / jnp.sum(raised, axis=1, keepdims=True)
 
-    rows_all = n_expert * 2 * tok
-    b_rows = b_all.reshape(rows_all, width)
-    my_expert = me_e * exp_dev + mine
-    rw_all = route_weights(b_rows, mask_all.reshape(rows_all, 128)[:, :experts_all] > 0)
-    is_mine = ids[:experts_all] == my_expert
-    rw_mine = jnp.sum(jnp.where(is_mine[None, :], rw_all, 0.0), axis=1, keepdims=True)
     rw = route_weights(b, mask[:, :experts_all] > 0)
     rw = jnp.concatenate([rw, jnp.zeros((tok, 128 - experts_all), f32)], axis=1)
-    w_gu = gate_up.reshape(width, ff2)
-    pre = mm(b_rows, w_gu)
-    g, u = pre[:, :ff], pre[:, ff:]
-    sig = jax.nn.sigmoid(g)
-    act = g * sig
-    hidden = (act * u).astype(bf16)
-    y_f = mm(hidden, down).astype(bf16).astype(f32)
-    cot_f = cot_all.reshape(rows_all, width).astype(f32)
-    d_route = jnp.sum(cot_f * y_f, axis=1, keepdims=True)
-    out_part = (rw_mine * y_f).astype(bf16)
-    d_y = (rw_mine * cot_f).astype(bf16)
-    d_hidden = mm_nt(d_y, down)
-    d_pre = jnp.concatenate(
-        [d_hidden * u * sig * (1.0 + g * (1.0 - sig)), d_hidden * act], axis=1
-    ).astype(bf16)
-    d_b = mm_nt(d_pre, w_gu).astype(bf16)
-    grad_down = mm_tn(hidden, d_y).astype(bf16)
-    grad_gate_up = mm_tn(b_rows, d_pre).astype(bf16).reshape(n_shard, d_slice, ff2)
-    high = lax.reduce_precision(d_route, 8, 7)
-    low = d_route - high
-    extra = jnp.where(ids[None] == my_expert, high, jnp.where(ids[None] == my_expert + 64, low, 0.0)).astype(bf16)
-
+    router_pad = jnp.concatenate([router_t, jnp.zeros((128 - experts_all, width), bf16)], axis=0)
     per_e = (n_expert, 2 * tok)
     piece = (chips, 2 * tok)
-    router_pad = jnp.concatenate([router_t, jnp.zeros((128 - experts_all, width), bf16)], axis=0)
-    gx1, d_o, gain_two, g_router, land_gu, land_dn = comm_call(
-        functools.partial(norm_kernel, dims),
+    four = 4 * tok
+    if chips <= 4:
+        out_part, grad_gate_up, grad_down, db_in, ex_in, land_gu, land_dn, _, _ = comm_call(
+            functools.partial(expert_kernel, dims),
+            4,
+            60,
+            60,
+            [
+                vm((width, ff2), bf16),
+                vm((ff, width), bf16),
+                vm((chips, 2, 2 * tok, width), bf16),
+                vm((2, 2 * tok, width), bf16),
+                vm((2, 2 * tok, 128), bf16),
+                vm((four, ff2), f32),
+                vm((chips, four, ff), bf16),
+                vm((chips, four, ff2), bf16),
+                vm((chips, four, width), bf16),
+                vm((2, 2 * tok, width), bf16),
+                vm((2, 2 * tok, 128), bf16),
+                vm(piece + (width,), bf16),
+                vm(piece + (128,), bf16),
+                vm((2 * tok, width), bf16),
+                vm((2 * tok, 128), bf16),
+                vm((four, 128), f32),
+                vm((four, 128), f32),
+                vm((2, tiled(width, 256), ff2), bf16),
+                vm((2, tiled(ff, 256), width), bf16),
+                pltpu.SemaphoreType.DMA((2,)),
+            ],
+            [
+                sds(per_e + (width,), bf16),
+                sds((n_shard, d_slice, ff2), bf16),
+                sds((ff, width), bf16),
+                sds(piece + (width,), bf16),
+                sds(piece + (128,), bf16),
+                sds((group - 1, d_slice // 2, ff2), bf16),
+                sds((group - 1, ff, d_slice), bf16),
+                sds(piece + (width,), bf16),
+                sds(piece + (128,), bf16),
+            ],
+            60,
+            in_specs=[any_spec] * 5 + [vmem_spec],
+        )(b_pair, cot_all, mask_all, gate_up, down, router_pad)
+    else:
+        rows_all = n_expert * 2 * tok
+        b_rows = lax.all_gather(b_pair, "expert", axis=0, tiled=True)
+        my_expert = me_e * exp_dev + mine
+        rw_all = route_weights(b_rows, mask_all.reshape(rows_all, 128)[:, :experts_all] > 0)
+        is_mine = ids[:experts_all] == my_expert
+        rw_mine = jnp.sum(jnp.where(is_mine[None, :], rw_all, 0.0), axis=1, keepdims=True)
+        w_gu = gate_up.reshape(width, ff2)
+        pre = mm(b_rows, w_gu)
+        g, u = pre[:, :ff], pre[:, ff:]
+        sig = jax.nn.sigmoid(g)
+        act = g * sig
+        hidden = (act * u).astype(bf16)
+        y_f = mm(hidden, down).astype(bf16).astype(f32)
+        cot_f = cot_all.reshape(rows_all, width).astype(f32)
+        d_route = jnp.sum(cot_f * y_f, axis=1, keepdims=True)
+        out_part = (rw_mine * y_f).astype(bf16)
+        d_y = (rw_mine * cot_f).astype(bf16)
+        d_hidden = mm_nt(d_y, down)
+        d_pre = jnp.concatenate(
+            [d_hidden * u * sig * (1.0 + g * (1.0 - sig)), d_hidden * act], axis=1
+        ).astype(bf16)
+        d_b = mm_nt(d_pre, w_gu).astype(bf16)
+        grad_down = mm_tn(hidden, d_y).astype(bf16)
+        grad_gate_up = mm_tn(b_rows, d_pre).astype(bf16).reshape(n_shard, d_slice, ff2)
+        high = lax.reduce_precision(d_route, 8, 7)
+        low = d_route - high
+        extra = jnp.where(ids[None] == my_expert, high, jnp.where(ids[None] == my_expert + 64, low, 0.0)).astype(bf16)
+
+        def home(value):
+            return lax.psum_scatter(value, "expert", scatter_dimension=0, tiled=True)[None]
+
+        db_in, ex_in = home(d_b), home(extra)
+
+    n_parts = db_in.shape[0]
+    early = chips <= 4
+    gx1, d_o, gain_two, g_router, norm_gu, late_gu, norm_dn, out_in = comm_call(
+        functools.partial(norm_kernel, dims, early),
         1,
         60,
-        40,
+        24,
         [
-            vm(piece + (width,), bf16),
-            vm(piece + (128,), bf16),
-            vm(piece + (width,), bf16),
-            vm(piece + (128,), bf16),
-            vm((chips - 1, 2 * tok, width), bf16),
-            vm((chips - 1, 2 * tok, 128), bf16),
+            vm((n_parts, 2 * tok, width), bf16),
+            vm((n_parts, 2 * tok, 128), bf16),
             vm((tok, width), bf16),
             vm((tok, 128), bf16),
             vm((tok, width), bf16),
             vm((tok, 128), bf16),
             vm((2, tok, 128), bf16),
             vm((tok, width), bf16),
+            vm(piece + (width,), bf16),
+            vm(piece + (width,), bf16),
         ],
         [
             sds((tok, width), f32),
             sds((length, width), bf16),
             sds((8, width), f32),
             sds((128, width), f32),
-            sds((group - 1, d_slice, ff2), bf16),
-            sds((group - 1, ff, d_slice), bf16),
+            sds((group - 1, d_slice // 2, ff2), bf16) if not early else sds((16, 128), bf16),
+            sds((group - 1, d_slice // 2, ff2), bf16),
+            sds((group - 1, ff, d_slice), bf16) if not early else sds((16, 128), bf16),
+            sds(piece + (width,), bf16),
         ],
-        56,
-        in_specs=[any_spec] * 4 + [vmem_spec] * 6,
-        out_specs=[vmem_spec, any_spec, vmem_spec, vmem_spec, any_spec, any_spec],
-    )(
-        d_b.reshape(per_e + (width,)),
-        extra.reshape(per_e + (128,)),
-        grad_gate_up,
-        grad_down,
-        x1,
-        b,
-        cotangent,
-        rw,
-        router_pad,
-        gains,
-    )
-
-    d_qkv, qk_gain, share_out, hidden_out, two_gu, two_dn, own_gu, own_dn, _ = comm_call(
+        60,
+        in_specs=[any_spec] * 5 + [vmem_spec] * 6,
+        out_specs=[vmem_spec, any_spec, vmem_spec, vmem_spec] + [any_spec] * 4,
+    )(db_in, ex_in, grad_gate_up, grad_down, out_part.reshape(per_e + (width,)), x1, b, cotangent, rw, router_pad, gains)
+    if not early:
+        land_gu, land_dn = norm_gu, norm_dn
+
+    d_qkv, qk_gain, grad_out, hidden_out, two_gu, own_gu, far_dn = comm_call(
         functools.partial(back_kernel, dims),
         2,
         80,
@@ -1011,33 +1310,30 @@
             vm((length, cols), bf16),
             vm((length, HEAD_DIM), f32),
             vm((length, HEAD_DIM), f32),
-            vm((d_slice, ff2), bf16),
-            vm((group - 1, d_slice, ff2), bf16),
+            vm((2, d_slice // 2, ff2), bf16),
+            vm((2, group - 1, d_slice // 2, ff2), bf16),
             vm((ff, d_slice), bf16),
             vm((group - 1, ff, d_slice), bf16),
             vm(piece + (width,), bf16),
-            vm((2 * tok, width), bf16),
-            vm((chips - 1, 2 * tok, width), bf16),
             vm((tok, width), bf16),
             vm((tok, width), bf16),
             vm((n_expert, share, width), bf16),
             vm((chips, share, width), bf16),
             vm((chips - 1, share, width), bf16),
+            vm((share, width), bf16),
         ],
         [
             sds((length, cols), bf16),
             sds((16, HEAD_DIM), f32),
-            sds((share, width), bf16),
+            sds((n_expert, share, width), bf16),
             sds((tok, width), bf16),
             sds((d_slice, ff2), bf16),
+            sds((group - 1, d_slice, ff2), bf16),
             sds((ff, d_slice), bf16),
-            sds((group - 1, d_slice, ff2), bf16),
-            sds((group - 1, ff, d_slice), bf16),
-            sds((chips, 2 * tok, width), bf16),
         ],
         60,
-        in_specs=[any_spec] * 10 + [vmem_spec] + [any_spec] * 5 + [vmem_spec],
-        out_specs=[any_spec] + [vmem_spec] * 3 + [any_spec] * 5,
+        in_specs=[any_spec] * 10 + [vmem_spec] + [any_spec] * 6 + [vmem_spec],
+        out_specs=[any_spec, vmem_spec, any_spec, vmem_spec] + [any_spec] * 3,
     )(
         d_o,
         w_attn_out[0],
@@ -1053,13 +1349,14 @@
         grad_gate_up,
         grad_down,
         land_gu,
+        late_gu,
         land_dn,
-        out_part.reshape(per_e + (width,)),
+        out_in,
         x1,
     )
 
     small_rows = (8 + -(-experts_all // 8) * 8, d_slice)
-    grad_hidden, grad_qkv, grad_out, sums = comm_call(
+    grad_hidden, grad_qkv, sums, two_dn, own_dn = comm_call(
         functools.partial(tail_kernel, dims),
         3,
         100,
@@ -1084,13 +1381,14 @@
         [
             sds((tok, width), f32),
             sds((n_expert, rows_e, qkv_cols), bf16),
-            sds((n_expert, share, width), bf16),
             sds(small_rows, f32),
+            sds((ff, d_slice), bf16),
+            sds((group - 1, ff, d_slice), bf16),
         ],
         56,
-        in_specs=[any_spec] * 3 + [vmem_spec] * 6 + [any_spec],
-        out_specs=[vmem_spec, any_spec, any_spec, vmem_spec],
-    )(d_qkv, heads, a, gx1, hidden_in, gains, gain_two, g_router, qk_gain, share_out)
+        in_specs=[any_spec] * 5 + [vmem_spec] * 6,
+        out_specs=[vmem_spec, any_spec, vmem_spec, any_spec, any_spec],
+    )(d_qkv, heads, a, grad_down, far_dn, gx1, hidden_in, gains, gain_two, g_router, qk_gain)
 
     def settle(own, others, other):
         total = own.astype(f32) + jnp.sum(others.astype(f32), axis=0)

time: 916 us -> 788 us (0.86)
  matrix products: 107 us -> 1.4 us
  Pallas kernels: 751 us -> 734 us
  other arithmetic: 37.4 us -> 28.1 us
    dot_general x8 -> x1, matrix products: 107 us -> 1.4 us  [dot(): lax.dot_general(left, right, (dims, ((), ())), preferred_element_type=out)]
    pallas_call x4 -> x5, Pallas kernels: 751 us -> 734 us  [call(): pl.pallas_call(kernel, out_shape=outs, in_specs=in_specs or [any_spec] *...]
    convert_element_type x2 -> x0, other arithmetic: 9.6 us -> none  [the longest x1 8.2 us: shards(): d_y = (rw_mine * cot_f).astype(bf16)]
where the time goes in v2:
time: 788 us; the launch traced here: 777 us
  Pallas kernels  734 us (93%)
  other arithmetic  28.1 us (4%)
  local copies, waits for them, and re-layouts  12.6 us (2%)
    pallas_call x5, Pallas kernels, call(): pl.pallas_call(kernel, out_shape=outs, in_specs=in_specs or [any_spec] *...  734 us

profile of v2, /device:TPU:0, one launch (start us, length us, event | category | flops | bytes accessed | tf_op | source)
XLA Modules:
  0.0 777.2 jit_solution(793515506716296527)
XLA Ops:
  0.6 0.7 scatter.14
  1.3 1.5 dynamic_update_slice.3
  2.8 0.7 fusion.9
  3.5 0.1 scatter.18
  3.6 1.3 pad_maximum_fusion.2.small
  5.0 1.0 fusion.6
  6.0 1.0 pad_maximum_fusion
  7.0 0.8 copy.23
  7.8 0.9 convert_reduce_fusion.mask
  8.6 0.7 broadcast_in_dim.19.seg_own
  9.3 0.0 copy-start.3
  9.3 304.4 %shard_map.178 = (bf16[4,32,512]{2,1,0:T(8,128)(2,1)}, f32[512,128]{1,0:T(8,128)}, bf16[4,8,64,1280]{3,2,1,0:T(8,128)(2,1)}, bf16[512,2048]{1,0:T(8,128)(2,1)}, ...) custom-call(bf16[128,2048]{1,0:T(8,128)(2,1)} %x.11, ...), custom_call_target="tpu_custom_call" | custom-call | tf_op jit(solution)/shard_map/pallas_call | solution.py:156
  313.7 0.8 slice_bitcast_fusion
  314.6 0.0 copy-done.3
  314.6 1.4 fusion.10
  316.0 0.2 fusion.8
  316.2 0.1 fusion.7
  316.3 0.6 concatenate.25.rw
  316.9 0.8 concatenate.24.router_t
  317.8 128.0 %shard_map.179 = (bf16[8,256,2048]{2,1,0:T(8,128)(2,1)}, bf16[4,512,1536]{2,1,0:T(8,128)(2,1)}, bf16[768,2048]{1,0:T(8,128)(2,1)}, bf16[4,256,2048]{2,1,0:T(8,12...) custom-call(bf16[256,2048]{1,0:T(8,128)(2,1)} %get-tuple-element.86., ...), custom_call_target="tpu_custom_call" | custom-call | tf_op jit(solution)/shard_map/pallas_call | solution.py:156
  445.7 0.8 slice.71
  446.5 0.6 pad_convert_fusion.gains
  447.2 75.9 %shard_map.180 = (f32[128,2048]{1,0:T(8,128)}, bf16[512,2048]{1,0:T(8,128)(2,1)}, f32[8,2048]{1,0:T(8,128)}, f32[128,2048]{1,0:T(8,128)}, bf16[16,128]{1,0:T(8,1...) custom-call(bf16[4,256,2048]{2,1,0:T(8,128)(2,1)} %get-tuple-element.92.db, ...), custom_call_target="tpu_custom_call" | custom-call | tf_op jit(solution)/shard_map/pallas_call | solution.py:156
  523.1 103.0 %shard_map.181 = (bf16[512,1280]{1,0:T(8,128)(2,1)}, f32[16,128]{1,0:T(8,128)}, bf16[8,128,2048]{2,1,0:T(8,128)(2,1)}, bf16[128,2048]{1,0:T(8,128)(2,1)}, bf16[5...) custom-call(bf16[512,2048]{1,0:T(8,128)(2,1)} %get-tuple-element.99.do_h, ...), custom_call_target="tpu_custom_call" | custom-call | tf_op jit(solution)/shard_map/pallas_call | solution.py:156
  626.1 122.5 %shard_map.182 = (f32[128,2048]{1,0:T(8,128)}, bf16[8,64,5120]{2,1,0:T(8,128)(2,1)}, f32[24,512]{1,0:T(8,128)}, bf16[768,512]{1,0:T(8,128)(2,1)}, bf16[1,768,512]{2,1,0:T(8,128)(2,1)}) custom-call(bf16[512,1280]{1,0:T(8,128)(2,1)} %get-tuple-element.111.d_qkv_h, bf16[4,8,64,1280]{3,2,1,0:T(8,128)(2,1)} %get-tuple-element.112.heads_h, ...), custom_call_target="tpu_custom_call" | custom-call | tf_op jit(solution)/shard_map/pallas_call | solution.py:156
  748.7 2.1 fusion.2
  750.7 0.0 copy-start
  750.7 0.0 copy-start.1
  750.7 2.0 maximum_bitcast_fusion.1
  752.7 0.0 copy-done
  752.7 1.0 copy-done.1
  753.7 2.4 fusion
  756.1 0.0 slice-start
  756.1 0.0 slice-start.1
  756.1 3.6 maximum_bitcast_fusion
  759.8 0.5 slice-done
  760.3 0.6 slice-done.1
  760.9 0.0 copy-start.5
  760.9 5.4 bitcast_convert_fusion
  766.3 0.0 copy-done.5
  766.3 0.6 slice_bitcast_fusion.1
  767.0 0.6 dynamic-slice_bitcast_fusion
  767.6 0.6 slice_bitcast_fusion.2
  768.2 6.8 bitcast_convert_fusion.1
  775.0 0.0 copy-done.4
  775.0 0.8 copy.32
  775.8 0.0 copy-done.2
  775.8 1.0 copy.33
  (6 shorter events, 0.0 us)
Async XLA Ops:
  9.3 305.2 %copy-start.3 = (bf16[128,128]{1,0:T(8,128)(2,1)S(1)}, bf16[128,128]{1,0:T(8,128)(2,1)}, u32[]{:S(2)}) copy-start(bf16[128,128]{1,0:T(8,128)(2,1)} %convert_reduce_fusion.mask) | copy-start | bytes 98308
  750.7 2.0 copy-start
  750.7 3.0 copy-start.1
  756.1 4.1 slice-start
  756.1 4.7 slice-start.1
  760.9 5.4 copy-start.5
  768.2 6.8 copy-start.4
  768.2 7.6 copy-start.2

commit v3 on v2

--- a/solution.py
+++ b/solution.py
@@ -214,9 +214,9 @@
 
 
 def front_kernel(
-    dims, x, small, seg_own, w_qkv, w_out, w_gu, w_dn, cot, mask, cos_h, sin_h,
+    dims, x, small, seg_own, w_qkv, w_out, w_gu, cot, mask, cos_h, sin_h,
     small_out, seg_out, heads_out, a_out, raw_out, q_out, k_out, v_out, o_out, x1_out, b_out,
-    gate_up, down, cot_all, mask_all, b_pair,
+    gate_up, cot_all, mask_all, b_pair,
     x_all, small_all, seg_col, heads, a, raw, q, k, v, o, w_o, part, parts_in, cos, sin, gains, seg_row, x1, b_own,
     send, recv, local,
 ):
@@ -243,9 +243,6 @@
             (w_qkv.at[rows, span(HEADS + KV_HEADS + kv, HEAD_DIM)], heads.at[z, e, :, pl.ds(hd + HEAD_DIM, HEAD_DIM)]),
         ]
 
-    def d_cols(ref, who):
-        return ref.at[:, span(who, d_slice)]
-
     half0, half1 = pl.ds(0, tok), pl.ds(tok, tok)
     first = [
         net.copy(x, x_all.at[span(z, tok)]),
@@ -257,7 +254,6 @@
     local_heads = [net.copy(s, d) for s, d in heads_of(z)]
     local_cot = [net.copy(cot, cot_all.at[e, half0]), net.copy(mask, mask_all.at[e, half0])]
     load_out = net.copy(w_out, w_o)
-    here = [net.copy(w_gu.at[mine], gate_up.at[z]), net.copy(w_dn.at[mine], d_cols(down, z))]
     greet(everyone(at))
     got_heads = [net.push(s, d, at.z_dev(t)) for t in range(1, at.n_shard) for s, d in heads_of(z ^ t)]
     got_x = []
@@ -279,7 +275,6 @@
     pieces_w = [
         (w_gu.at[other, low], gate_up.at[z, low], gate_up.at[z ^ group, low]),
         (w_gu.at[other, high], gate_up.at[z, high], gate_up.at[z ^ group, high]),
-        (w_dn.at[other], d_cols(down, z), d_cols(down, z ^ group)),
     ]
     from_partner = {}
 
@@ -298,7 +293,6 @@
     got_w = []
     for t in range(1, group):
         got_w.append(net.push(w_gu.at[mine], gate_up.at[z], at.z_dev(t)))
-        got_w.append(net.push(w_dn.at[mine], d_cols(down, z), at.z_dev(t)))
     got_cot = [
         net.push(cot, cot_all.at[e, half1], at.z_dev(group)),
         net.push(mask, mask_all.at[e, half1], at.z_dev(group)),
@@ -367,7 +361,6 @@
 
     lax.fori_loop(0, n_heads, one_head, 0)
     hand_on(0)
-    fetch_piece(2)
     keep.append(net.copy(o, o_out))
     load_out.wait()
     wide_o = tiled(width, 256)
@@ -380,7 +373,6 @@
     lax.fori_loop(0, width // wide_o, out_tile, 0)
     sums = [net.push(part.at[span(z ^ t, tok)], parts_in.at[t - 1], at.z_dev(t)) for t in range(1, at.n_shard)]
     last = pass_on(net, at, cots, cot_state)
-    hand_on(1)
     arrive(sums)
 
     def middle_rows(i, _):
@@ -396,18 +388,18 @@
     lax.fori_loop(0, tok // step, middle_rows, 0)
     swap = net.push(b_own, b_pair.at[half1], at.z_dev(group))
     keep += [net.copy(b_own, b_pair.at[half0]), net.copy(x1, x1_out), net.copy(b_own, b_out)]
-    hand_on(2)
+    hand_on(1)
     swap.wait_recv()
     arrive(last + got_w)
-    for c in keep + here:
+    for c in keep:
         c.wait()
     net.sent()
 
 
 def expert_kernel(
-    dims, b_pair, cot_all, mask_all, gate_up, down, router_t,
-    out_part, ggu, gdn, db_in, ex_in, land_gu, land_dn, core_in, core_x,
-    w_gu, w_dn, rows, cot_t, mask_t, gu, hid, d_pre, d_y, stage, stage_x, own, own_x, add, add_x, w_r, d_r, g_tile, d_tile,
+    dims, b_pair, cot_all, mask_all, gate_up, w_gu_in, w_dn_in, router_t,
+    out_part, ggu, gdn, db_in, ex_in, land_gu, land_dn,
+    w_gu, w_dn, rows, cot_t, mask_t, hid, d_pre, d_y, stage, stage_x, own, own_x, core_in, core_x, w_r, d_r, g_tile, d_tile,
     tile_sem, send, recv, local,
 ):
     at = Place(*dims)
@@ -417,86 +409,128 @@
     ff, width = w_dn.shape
     two = b_pair.shape[0]
     four = 2 * two
-    expert = e * (at.n_shard // group) + z // group
+    mine, other = z // group, (z ^ group) // group
+    expert = e * (at.n_shard // group) + mine
     step = 16
     fine = tiled(ff, 256)
-    wide = tiled(width, 512)
+    wide = tiled(width, 1024)
+    far = z ^ group
+
+    def d_cols(who):
+        return w_dn.at[:, span(who, d_slice)]
 
     pair = net.copy(b_pair, rows.at[0, 1])
-    loads = [net.copy(gate_up.at[s], w_gu.at[pl.ds(s * d_slice, d_slice)]) for s in range(n_slices)]
-    loads.append(net.copy(down, w_dn))
+    masks = []
+    for t in range(at.chips):
+        masks.append(net.copy(mask_all.at[at.slot(t, 1)], mask_t.at[t, 0]))
+        masks.append(net.copy(mask_all.at[at.slot(t)], mask_t.at[t, 1]))
+    loads = [net.copy(w_gu_in.at[mine], w_gu.at[span(z, d_slice)])]
+    for k in range(1, n_slices):
+        loads.append(net.copy(gate_up.at[z ^ k], w_gu.at[span(z ^ k, d_slice)]))
+    load_dn = net.copy(w_dn_in.at[mine], d_cols(z))
 
     def fetch(t):
         return [
             net.copy(cot_all.at[at.slot(t, 1)], cot_t.at[0]),
             net.copy(cot_all.at[at.slot(t)], cot_t.at[1]),
-            net.copy(mask_all.at[at.slot(t, 1)], mask_t.at[0]),
-            net.copy(mask_all.at[at.slot(t)], mask_t.at[1]),
         ]
 
-    fetched = fetch(0)
-    greet([at.chip_dev(t) for t in range(1, at.chips)] + [at.mate()] + [at.z_dev(t) for t in range(1, group)])
+    order = list(range(1, at.chips)) + [0]
+    fetched = {order[0]: fetch(order[0])}
+    greet(
+        [at.chip_dev(t) for t in range(1, at.chips)] + [at.mate()] + [at.z_dev(t) for t in range(1, group + 1)]
+    )
     from_mate = {0: net.push(b_pair, rows.at[0, 0], at.mate())}
     near = [t for t in (1, 2) if t < at.chips]
-    far = [t for t in range(1, at.chips) if t not in near]
+    beyond = [t for t in range(1, at.chips) if t not in near]
     from_chip = {t: net.push(b_pair, rows.at[t, 1], at.chip_dev(t)) for t in near}
+    from_partner = net.push(w_dn_in.at[other], d_cols(z), at.z_dev(group))
+    got_dn = [net.push(w_dn_in.at[mine], d_cols(z), at.z_dev(t)) for t in range(1, group)]
+
+    relayed = []
 
     def pass_rows(t):
-        from_chip[t].wait_recv()
+        if t in from_chip:
+            from_chip[t].wait_recv()
+        else:
+            arrive(relayed)
         from_mate[t] = net.push(rows.at[t, 1], rows.at[t, 0], at.mate())
 
-    mates, outs = {}, []
-
-    def finish(t):
-        arrive(mates[t])
-        c, cx = net.copy(core_in.at[t], add), net.copy(core_x.at[t], add_x)
-        c.wait()
-        cx.wait()
-
-        def add_rows(i, _):
-            r = span(i, step)
-            own[t, r, :] = (own[t, r, :].astype(f32) + add[r, :].astype(f32)).astype(bf16)
-            own_x[t, r, :] = (own_x[t, r, :].astype(f32) + add_x[r, :].astype(f32)).astype(bf16)
-            return 0
-
-        lax.fori_loop(0, two // step, add_rows, 0)
-        if t:
-            outs.append(net.push(own.at[t], db_in.at[t], at.chip_dev(t)))
-            outs.append(net.push(own_x.at[t], ex_in.at[t], at.chip_dev(t)))
-
     lanes = lax.broadcasted_iota(jnp.int32, (four, 128), 1)
-    used = {}
-
-    def work(t, fetched, before, after):
+
+    def up_rows(t):
         logits = mm_nt(rows[t].reshape(four, width), router_t[...])
-        chosen = mask_t[...].reshape(four, 128).astype(f32) > 0
+        chosen = mask_t[t].reshape(four, 128).astype(f32) > 0
         masked = jnp.where(chosen, logits, neg_fill)
         raised = jnp.where(chosen, jnp.exp(masked - jnp.max(masked, axis=1, keepdims=True)), 0.0)
         weight = raised / jnp.sum(raised, axis=1, keepdims=True)
         weight = jnp.sum(jnp.where(lanes == expert, weight, 0.0), axis=1, keepdims=True)
-        w_r[...] = jnp.broadcast_to(weight, (four, 128))
-        d_r[...] = jnp.zeros_like(d_r)
+        w_r[t] = jnp.broadcast_to(weight, (four, 128))
 
         def up(j, _):
             tile, tile_u = span(j, fine), pl.ds(pl.multiple_of(ff + j * fine, fine), fine)
             x = rows[t].reshape(four, width)
             g = mm(x, w_gu[:, tile])
             u = mm(x, w_gu[:, tile_u])
-            gu[:, tile] = g
-            gu[:, tile_u] = u
+            d_pre[t, :, tile] = g.astype(bf16)
+            d_pre[t, :, tile_u] = u.astype(bf16)
             hid[t, :, tile] = (g * jax.nn.sigmoid(g) * u).astype(bf16)
             return 0
 
         lax.fori_loop(0, ff // fine, up, 0)
-        before()
-        for c in fetched:
+
+    for c in masks:
+        c.wait()
+    pair.wait()
+    from_mate[0].wait_recv()
+    for c in loads:
+        c.wait()
+    up_rows(0)
+    for i in near:
+        pass_rows(i)
+        if beyond:
+            part = pl.ds((2 - i) * (two // 2), two // 2)
+            relayed.append(net.push(rows.at[i, 1, part], rows.at[3, 1, part], at.chip_dev(3 - i)))
+    from_partner.wait_recv()
+    for t in range(1, group):
+        got_dn.append(net.push(d_cols(far), d_cols(far), at.z_dev(t)))
+    for t in near:
+        from_mate[t].wait_recv()
+        up_rows(t)
+    for t in beyond:
+        pass_rows(t)
+        from_mate[t].wait_recv()
+        up_rows(t)
+    load_dn.wait()
+    arrive(got_dn)
+
+    mates, outs = {}, []
+
+    def finish(t):
+        arrive(mates[t])
+
+        def add_rows(i, _):
+            r = span(i, step)
+            own[t, r, :] = (own[t, r, :].astype(f32) + core_in[t, r, :].astype(f32)).astype(bf16)
+            own_x[t, r, :] = (own_x[t, r, :].astype(f32) + core_x[t, r, :].astype(f32)).astype(bf16)
+            return 0
+
+        lax.fori_loop(0, two // step, add_rows, 0)
+        if t:
+            outs.append(net.push(own.at[t], db_in.at[t], at.chip_dev(t)))
+            outs.append(net.push(own_x.at[t], ex_in.at[t], at.chip_dev(t)))
+
+    used = {}
+    for i, t in enumerate(order):
+        d_r[...] = jnp.zeros_like(d_r)
+        for c in fetched[t]:
             c.wait()
 
-        def back_y(n, _):
+        def back_y(n, _, t=t):
             tile = span(n, wide)
             y = mm(hid[t], w_dn[:, tile]).astype(bf16).astype(f32)
             c = cot_t[:, :, tile].reshape(four, wide).astype(f32)
-            w = w_r[:, 0:1]
+            w = w_r[t, :, 0:1]
             d_r[...] += jnp.broadcast_to(jnp.sum(c * y, axis=1, keepdims=True), (four, 128))
             d_y[t, :, tile] = (w * c).astype(bf16)
             cot_t[:, :, tile] = (w * y).astype(bf16).reshape(2, two, wide)
@@ -507,11 +541,13 @@
             net.copy(cot_t.at[0], out_part.at[at.slot(t, 1)]),
             net.copy(cot_t.at[1], out_part.at[at.slot(t)]),
         ]
-
-        def back_h(j, _):
+        if i:
+            finish(order[i - 1])
+
+        def back_h(j, _, t=t):
             tile, tile_u = span(j, fine), pl.ds(pl.multiple_of(ff + j * fine, fine), fine)
             d_h = mm_nt(d_y[t], w_dn[tile, :])
-            g, u = gu[:, tile], gu[:, tile_u]
+            g, u = d_pre[t, :, tile].astype(f32), d_pre[t, :, tile_u].astype(f32)
             sig = jax.nn.sigmoid(g)
             d_pre[t, :, tile] = (d_h * u * sig * (1.0 + g * (1.0 - sig))).astype(bf16)
             d_pre[t, :, tile_u] = (d_h * g * sig).astype(bf16)
@@ -520,12 +556,13 @@
         lax.fori_loop(0, ff // fine, back_h, 0)
         for c in kept:
             c.wait()
-        after()
-        p = t % 2
+        if i + 1 < at.chips:
+            fetched[order[i + 1]] = fetch(order[i + 1])
+        p = i % 2
         for c in used.pop(p, []):
             net.done(c)
 
-        def back_b(n, _):
+        def back_b(n, _, t=t, p=p):
             tile = span(n, wide)
             value = mm_nt(d_pre[t], w_gu[tile, :]).astype(bf16)
             stage[p, :, tile] = value[:two]
@@ -545,40 +582,7 @@
             net.push(stage_x.at[p], core_x.at[t], at.mate()),
         ]
         used[p] = mates[t]
-
-    pair.wait()
-    from_mate[0].wait_recv()
-    for c in loads:
-        c.wait()
-    for c in fetched[2:]:
-        c.wait()
-    order = list(range(at.chips))
-    state = {"next": fetched[:2]}
-    for t in order:
-        if t == 1:
-            for i in near:
-                pass_rows(i)
-            for i in far:
-                from_chip[i] = net.push(b_pair, rows.at[i, 1], at.chip_dev(i))
-        if t:
-            if t in far:
-                pass_rows(t)
-            from_mate[t].wait_recv()
-
-        def before(t=t):
-            if t:
-                finish(t - 1)
-
-        def after(t=t):
-            if t + 1 < at.chips:
-                more = fetch(t + 1)
-                state["next"] = more[:2]
-                state["mask"] = more[2:]
-
-        work(t, state["next"], before, after)
-        for c in state.pop("mask", []):
-            c.wait()
-    finish(at.chips - 1)
+    finish(order[-1])
     keep = [net.copy(own.at[0], db_in.at[0]), net.copy(own_x.at[0], ex_in.at[0])]
 
     part = tiled(width, 256)
@@ -654,8 +658,8 @@
 
 def norm_kernel(
     dims, early, db, ex, ggu, gdn, out_part, x1, b, cot, rw, router_t, gains,
-    gx1, do_all, gain_two, g_router, land_gu, late_gu, land_dn, out_in,
-    own, own_x, half_out, half_x, swap_in, swap_x, logit, d_out, out_own, out_core,
+    gx1, do_all, gain_two, g_router, land_gu, late_gu, land_dn, out_sum,
+    own, own_x, half_out, half_x, swap_in, swap_x, logit, d_out, out_own, out_core, out_in,
     send, recv, local,
 ):
     at = Place(*dims)
@@ -706,8 +710,7 @@
 
         lax.fori_loop(0, 2 * tok // step, add, 0)
         if t:
-            outs.append(net.push(out_own.at[t], out_in.at[t], at.chip_dev(t)))
-    keep_own = net.copy(out_own.at[0], out_in.at[0])
+            outs.append(net.push(out_own.at[t], out_in.at[t - 1], at.chip_dev(t)))
     arrive(swaps)
     gain_two[...] = jnp.zeros_like(gain_two)
 
@@ -738,17 +741,29 @@
     keep = net.copy(d_out, mine)
     copies = [net.push(d_out, mine, at.z_dev(t)) for t in range(1, at.n_shard)]
     g_router[...] = mm_tn(logit[0], b[...]) + mm_tn(logit[1], b[...])
+    arrive(outs)
+
+    def out_rows(i, _):
+        rows = span(i, step)
+        total = out_own[0, rows, :].astype(f32)
+        for t in range(1, at.chips):
+            total += out_in[t - 1, rows, :].astype(f32)
+        out_sum[rows, :] = total.astype(bf16)
+        return 0
+
+    lax.fori_loop(0, 2 * tok // step, out_rows, 0)
     keep.wait()
-    keep_own.wait()
-    arrive(copies + landed + outs)
+    arrive(copies + landed)
     net.sent()
 
 
 def back_kernel(
-    dims, do_h, w_out, o_h, q_h, k_h, v_h, raw_h, cos_h, sin_h, seg_h, small, ggu, gdn, land_gu, late_gu, land_dn, out_parts, x1,
-    d_qkv_out, qk_gain, g_att, hidden, two_gu, own_gu, far_dn,
-    do_all, w_o, o, q, k, v, raw, cos, sin, seg_col, seg_row, mix, d_qkv, dk, dv,
-    sum_gu, add_gu, sum_dn, add_dn, out_in, half_out, swap_in, g_out, g_core, g_in, share_own,
+    dims, do_h, w_out, o_h, q_h, k_h, v_h, raw_h, cos_h, sin_h, seg_h, a_h, heads_h, ggu, gdn, land_gu, late_gu, land_dn, out_sum,
+    out_sum_own, small, x1, gx1, x, gains, gain_two, g_router,
+    hidden, g_hidden, small_sum, g_att, g_qkv, two_gu, own_gu, two_dn, own_dn,
+    do_all, w_o, o, q, k, v, raw, cos, sin, seg_col, seg_row, mix, d_qkv, dk, dv, qk_gain, a, heads,
+    sum_gu, add_gu, sum_dn, add_dn, swap_in, g_out, g_core, g_in, share_own,
+    parts_in, g_heads, core_in, chip_in, mine, turn_in, share_qkv, sm, sm_z, sm_core, sm_chip,
     send, recv, local,
 ):
     at = Place(*dims)
@@ -759,6 +774,7 @@
     cols = raw.shape[1]
     hd = cols - 2 * HEAD_DIM
     n_heads = hd // HEAD_DIM
+    rows_e = heads.shape[2]
     d_slice = ggu.shape[1]
     scale = HEAD_DIM ** (-0.5)
     block = tok
@@ -768,7 +784,6 @@
     def d_cols(ref, who):
         return ref.at[:, span(who, d_slice)]
 
-    load_dn = [net.copy(d_cols(gdn, far), sum_dn)] + [net.copy(land_dn.at[t - 1], add_dn.at[t - 1]) for t in range(1, group)]
     cut = d_slice // 2
     halves_gu = [pl.ds(0, cut), pl.ds(cut, cut)]
     load_gu = [
@@ -776,22 +791,14 @@
         for i, (r, land) in enumerate(zip(halves_gu, (land_gu, late_gu)))
     ]
     load_a = [net.copy(do_h, do_all), net.copy(o_h, o)]
-    load_out = net.copy(out_parts, out_in)
     load_b = [
         net.copy(s, d)
         for s, d in ((w_out, w_o), (q_h, q), (k_h, k), (v_h, v), (raw_h, raw), (cos_h, cos), (sin_h, sin), (seg_h, seg_col))
     ]
+    load_c = [net.copy(a_h, a), net.copy(heads_h, heads)]
+    load_dn = [net.copy(d_cols(gdn, far), sum_dn)] + [net.copy(land_dn.at[t - 1], add_dn.at[t - 1]) for t in range(1, group)]
     greet(everyone(at))
-
-    def sum_in(rows):
-        total = out_in[0, rows, :].astype(f32)
-        for t in range(1, at.chips):
-            total += out_in[t, rows, :].astype(f32)
-        return total
-
-    def partner(i, _):
-        half_out[span(i, step), :] = sum_in(pl.ds(pl.multiple_of(tok + i * step, step), step)).astype(bf16)
-        return 0
+    swap = net.push(out_sum.at[pl.ds(tok, tok)], swap_in, at.z_dev(group))
 
     def add_up(total, adds):
         def rows_of(i, _):
@@ -804,26 +811,21 @@
 
         lax.fori_loop(0, total.shape[0] // step, rows_of, 0)
 
-    load_out.wait()
-    lax.fori_loop(0, tok // step, partner, 0)
-    swap = net.push(half_out, swap_in, at.z_dev(group))
     got = []
-    for i in range(2):
+
+    def send_half(i):
         for c in load_gu[i]:
             c.wait()
         add_up(sum_gu.at[i], add_gu.at[i])
         got.append(net.push(sum_gu.at[i], two_gu.at[halves_gu[i]], at.z_dev(group)))
+
+    send_half(0)
     for t in range(1, group):
         got.append(net.push(ggu.at[z ^ t], own_gu.at[t - 1], at.z_dev(t)))
-    for c in load_dn:
-        c.wait()
-    add_up(sum_dn, add_dn)
-    keep_dn = net.copy(sum_dn, far_dn)
 
     for c in load_a:
         c.wait()
     share = share_own.shape[0]
-
     wide = tiled(hd, 256)
     each = wide // share
 
@@ -835,7 +837,6 @@
 
     lax.fori_loop(0, hd // wide, out_grad, 0)
     g_mates = {t: net.push(g_out.at[at.slot(t, 1)], g_core.at[t], at.mate()) for t in halves(at)}
-
     for c in load_b:
         c.wait()
     qk = []
@@ -864,6 +865,7 @@
         lax.fori_loop(0, share // step, add, 0)
         if t:
             g_outs.append(net.push(g_out.at[at.slot(t)], g_in.at[t - 1], at.chip_dev(t)))
+    send_half(1)
 
     dk[...] = jnp.zeros_like(dk)
     dv[...] = jnp.zeros_like(dv)
@@ -894,8 +896,45 @@
         d_qkv[rows, pl.ds(hd, HEAD_DIM)] = back.astype(bf16)
         d_qkv[rows, pl.ds(hd + HEAD_DIM, HEAD_DIM)] = dv[rows, :].astype(bf16)
         qk_gain[8:16, :] += eight(per)
-    keep = net.copy(d_qkv, d_qkv_out)
-
+
+    for c in load_c:
+        c.wait()
+    wide_d = tiled(d_slice, 256)
+    each_d = wide_d // rows_e
+
+    def grad_tile(s, _):
+        for j in range(d_slice // wide_d):
+            some = a[:, pl.ds(pl.multiple_of(s * d_slice + j * wide_d, wide_d), wide_d)]
+            tile = mm_tn(some, d_qkv[...]).astype(bf16)
+            for i in range(each_d):
+                g_heads[each_d * j + i, s] = tile[i * rows_e : (i + 1) * rows_e]
+        return 0
+
+    lax.fori_loop(0, at.n_shard, grad_tile, 0)
+    mates = {t: net.push(g_heads.at[at.slot(t, 1)], core_in.at[t], at.mate()) for t in halves(at)}
+    part = do_all
+
+    def rows_tile(s, _):
+        for j in range(d_slice // wide_d):
+            some = heads[s, pl.ds(each_d * j, each_d)].reshape(wide_d, cols)
+            here = pl.ds(pl.multiple_of(s * d_slice + j * wide_d, wide_d), wide_d)
+            part[:, here] = mm_nt(d_qkv[...], some).astype(bf16)
+        return 0
+
+    lax.fori_loop(0, at.n_shard, rows_tile, 0)
+    sums = [net.push(part.at[span(z ^ t, tok)], parts_in.at[t - 1], at.z_dev(t)) for t in range(1, at.n_shard)]
+    chips = []
+    for t in halves(at):
+        mates[t].wait_recv()
+        who = at.slot(t)
+
+        def add(s, _, t=t, who=who):
+            g_heads[who, s] = (g_heads[who, s].astype(f32) + core_in[t, s].astype(f32)).astype(bf16)
+            return 0
+
+        lax.fori_loop(0, at.n_shard, add, 0)
+        if t:
+            chips.append(net.push(g_heads.at[who], chip_in.at[t - 1], at.chip_dev(t)))
     arrive(g_outs)
 
     def own_share(i, _):
@@ -908,82 +947,17 @@
 
     lax.fori_loop(0, share // step, own_share, 0)
     keep_att = net.copy(share_own, g_att.at[e])
-    keep_att.wait()
-    atts = [lambda who: g_att.at[who]]
-    att_state = spread(net, at, atts)
+    for c in load_dn:
+        c.wait()
+    add_up(sum_dn, add_dn)
     swap.wait_recv()
 
     def hidden_rows(i, _):
         rows = span(i, step)
-        hidden[rows, :] = (x1[rows, :] + sum_in(rows) + swap_in[rows, :].astype(f32)).astype(bf16)
+        hidden[rows, :] = (x1[rows, :] + out_sum_own[rows, :].astype(f32) + swap_in[rows, :].astype(f32)).astype(bf16)
         return 0
 
     lax.fori_loop(0, tok // step, hidden_rows, 0)
-    arrive(pass_on(net, at, atts, att_state) + got)
-    keep.wait()
-    keep_dn.wait()
-    net.sent()
-
-
-def tail_kernel(
-    dims, d_qkv_h, heads_h, a_h, gdn, far_dn, gx1, x, gains, gain_two, g_router, qk_gain,
-    g_hidden, g_qkv, small_sum, two_dn, own_dn,
-    d_qkv, heads, a, part, parts_in, g_heads, core_in, chip_in, mine, turn_in, share, sm, sm_z, sm_core, sm_chip,
-    send, recv, local,
-):
-    at = Place(*dims)
-    net = Net(send, recv, local)
-    z, e, group = at.z, at.e, at.group
-    length, cols = d_qkv.shape
-    tok, width = x.shape
-    hd = cols - 2 * HEAD_DIM
-    n_heads = hd // HEAD_DIM
-    rows_e = heads.shape[2]
-    d_slice = width // at.n_shard
-    step = 16
-    load_a = [net.copy(d_qkv_h, d_qkv), net.copy(heads_h, heads)]
-    load_b = net.copy(a_h, a)
-    greet(everyone(at))
-    for c in load_a:
-        c.wait()
-
-    wide = tiled(d_slice, 256)
-    each = wide // rows_e
-
-    load_b.wait()
-
-    def grad_tile(s, _):
-        for j in range(d_slice // wide):
-            some = a[:, pl.ds(pl.multiple_of(s * d_slice + j * wide, wide), wide)]
-            tile = mm_tn(some, d_qkv[...]).astype(bf16)
-            for i in range(each):
-                g_heads[each * j + i, s] = tile[i * rows_e : (i + 1) * rows_e]
-        return 0
-
-    lax.fori_loop(0, at.n_shard, grad_tile, 0)
-    mates = {t: net.push(g_heads.at[at.slot(t, 1)], core_in.at[t], at.mate()) for t in halves(at)}
-
-    def rows_tile(s, _):
-        for j in range(d_slice // wide):
-            some = heads[s, pl.ds(each * j, each)].reshape(wide, cols)
-            here = pl.ds(pl.multiple_of(s * d_slice + j * wide, wide), wide)
-            part[:, here] = mm_nt(d_qkv[...], some).astype(bf16)
-        return 0
-
-    lax.fori_loop(0, at.n_shard, rows_tile, 0)
-    sums = [net.push(part.at[span(z ^ t, tok)], parts_in.at[t - 1], at.z_dev(t)) for t in range(1, at.n_shard)]
-    chips = []
-    for t in halves(at):
-        mates[t].wait_recv()
-        who = at.slot(t)
-
-        def add(s, _, t=t, who=who):
-            g_heads[who, s] = (g_heads[who, s].astype(f32) + core_in[t, s].astype(f32)).astype(bf16)
-            return 0
-
-        lax.fori_loop(0, at.n_shard, add, 0)
-        if t:
-            chips.append(net.push(g_heads.at[who], chip_in.at[t - 1], at.chip_dev(t)))
     arrive(chips)
 
     def total(s, _):
@@ -996,9 +970,12 @@
     lax.fori_loop(0, at.n_shard, total, 0)
     turns = [net.push(mine.at[z ^ t], turn_in.at[z], at.z_dev(t)) for t in range(1, at.n_shard)]
     turn_own = net.copy(mine.at[z], turn_in.at[z])
-    got = [net.push(far_dn, two_dn, at.z_dev(group))]
+    keep_att.wait()
+    atts = [lambda who: g_att.at[who]]
+    att_state = spread(net, at, atts)
+    got.append(net.push(sum_dn, two_dn, at.z_dev(group)))
     for t in range(1, group):
-        got.append(net.push(gdn.at[:, span(z ^ t, d_slice)], own_dn.at[t - 1], at.z_dev(t)))
+        got.append(net.push(d_cols(gdn, z ^ t), own_dn.at[t - 1], at.z_dev(t)))
     arrive(sums)
     sm[...] = jnp.zeros_like(sm)
     gain_one = jnp.zeros((8, width), f32)
@@ -1030,18 +1007,19 @@
     turn_own.wait()
     arrive(turns)
     for s in range(at.n_shard):
-        share[:, pl.ds(s * hd, hd)] = turn_in[s, :, pl.ds(0, hd)]
+        share_qkv[:, pl.ds(s * hd, hd)] = turn_in[s, :, pl.ds(0, hd)]
     for m in range(KV_HEADS):
         some = [s for s in range(at.n_shard) if (s * n_heads) // (HEADS // KV_HEADS) == m]
         for first, to in ((hd, HEADS + m), (hd + HEAD_DIM, HEADS + KV_HEADS + m)):
             value = turn_in[some[0], :, pl.ds(first, HEAD_DIM)].astype(f32)
             for s in some[1:]:
                 value += turn_in[s, :, pl.ds(first, HEAD_DIM)].astype(f32)
-            share[:, pl.ds(to * HEAD_DIM, HEAD_DIM)] = value.astype(bf16)
-    keep = net.copy(share, g_qkv.at[e])
+            share_qkv[:, pl.ds(to * HEAD_DIM, HEAD_DIM)] = value.astype(bf16)
+    keep = net.copy(share_qkv, g_qkv.at[e])
     keep.wait()
     qkvs = [lambda who: g_qkv.at[who]]
     state = spread(net, at, qkvs)
+    last = pass_on(net, at, atts, att_state)
     arrive(small_z)
     value = sm[z]
     for t in range(1, at.n_shard):
@@ -1051,7 +1029,7 @@
     c.wait_recv()
     sm_core[...] = sm[z] + sm_core[...]
     smalls = [net.push(sm_core, sm_chip.at[t - 1], at.chip_dev(t)) for t in range(1, at.chips)]
-    last = pass_on(net, at, qkvs, state)
+    last += pass_on(net, at, qkvs, state)
     arrive(smalls)
     value = sm_core[...]
     for t in range(1, at.chips):
@@ -1124,7 +1102,6 @@
         sds((tok, width), f32),
         sds((tok, width), bf16),
         sds((n_shard, d_slice, ff2), bf16),
-        sds((ff, width), bf16),
         sds((n_expert, 2 * tok, width), bf16),
         sds((n_expert, 2 * tok, 128), bf16),
         sds((2 * tok, width), bf16),
@@ -1158,8 +1135,8 @@
         outs,
         56,
     )
-    (small_all, seg_col, heads, a, raw, q, k, v, o, x1, b, gate_up, down, cot_all, mask_all, b_pair) = front(
-        hidden_in, small, seg_own, w_qkv[0], w_attn_out[0], w_gate_up[0], w_down[0], cotangent, mask, cos, sin
+    (small_all, seg_col, heads, a, raw, q, k, v, o, x1, b, gate_up, cot_all, mask_all, b_pair) = front(
+        hidden_in, small, seg_own, w_qkv[0], w_attn_out[0], w_gate_up[0], cotangent, mask, cos, sin
     )
     gains = jnp.zeros((8, width), f32)
     gains = gains.at[0:2].set(small_all[:, 0:2].astype(f32).transpose(1, 0, 2).reshape(2, width))
@@ -1178,7 +1155,7 @@
     piece = (chips, 2 * tok)
     four = 4 * tok
     if chips <= 4:
-        out_part, grad_gate_up, grad_down, db_in, ex_in, land_gu, land_dn, _, _ = comm_call(
+        out_part, grad_gate_up, grad_down, db_in, ex_in, land_gu, land_dn = comm_call(
             functools.partial(expert_kernel, dims),
             4,
             60,
@@ -1188,8 +1165,7 @@
                 vm((ff, width), bf16),
                 vm((chips, 2, 2 * tok, width), bf16),
                 vm((2, 2 * tok, width), bf16),
-                vm((2, 2 * tok, 128), bf16),
-                vm((four, ff2), f32),
+                vm((chips, 2, 2 * tok, 128), bf16),
                 vm((chips, four, ff), bf16),
                 vm((chips, four, ff2), bf16),
                 vm((chips, four, width), bf16),
@@ -1197,9 +1173,9 @@
                 vm((2, 2 * tok, 128), bf16),
                 vm(piece + (width,), bf16),
                 vm(piece + (128,), bf16),
-                vm((2 * tok, width), bf16),
-                vm((2 * tok, 128), bf16),
-                vm((four, 128), f32),
+                vm(piece + (width,), bf16),
+                vm(piece + (128,), bf16),
+                vm((chips, four, 128), f32),
                 vm((four, 128), f32),
                 vm((2, tiled(width, 256), ff2), bf16),
                 vm((2, tiled(ff, 256), width), bf16),
@@ -1213,14 +1189,16 @@
                 sds(piece + (128,), bf16),
                 sds((group - 1, d_slice // 2, ff2), bf16),
                 sds((group - 1, ff, d_slice), bf16),
-                sds(piece + (width,), bf16),
-                sds(piece + (128,), bf16),
             ],
             60,
-            in_specs=[any_spec] * 5 + [vmem_spec],
-        )(b_pair, cot_all, mask_all, gate_up, down, router_pad)
+            in_specs=[any_spec] * 6 + [vmem_spec],
+        )(b_pair, cot_all, mask_all, gate_up, w_gate_up[0], w_down[0], router_pad)
     else:
         rows_all = n_expert * 2 * tok
+        w_mine = lax.dynamic_index_in_dim(w_gate_up[0], mine, 0, keepdims=False)
+        gate_up = lax.dynamic_update_index_in_dim(gate_up, w_mine, me_z, 0)
+        down = lax.all_gather(w_down[0], "shard", axis=2, tiled=True)
+        down = lax.dynamic_index_in_dim(down, mine, 0, keepdims=False)
         b_rows = lax.all_gather(b_pair, "expert", axis=0, tiled=True)
         my_expert = me_e * exp_dev + mine
         rw_all = route_weights(b_rows, mask_all.reshape(rows_all, 128)[:, :experts_all] > 0)
@@ -1255,7 +1233,7 @@
 
     n_parts = db_in.shape[0]
     early = chips <= 4
-    gx1, d_o, gain_two, g_router, norm_gu, late_gu, norm_dn, out_in = comm_call(
+    gx1, d_o, gain_two, g_router, norm_gu, late_gu, norm_dn, out_sum = comm_call(
         functools.partial(norm_kernel, dims, early),
         1,
         60,
@@ -1271,6 +1249,7 @@
             vm((tok, width), bf16),
             vm(piece + (width,), bf16),
             vm(piece + (width,), bf16),
+            vm((chips - 1, 2 * tok, width), bf16),
         ],
         [
             sds((tok, width), f32),
@@ -1280,19 +1259,20 @@
             sds((group - 1, d_slice // 2, ff2), bf16) if not early else sds((16, 128), bf16),
             sds((group - 1, d_slice // 2, ff2), bf16),
             sds((group - 1, ff, d_slice), bf16) if not early else sds((16, 128), bf16),
-            sds(piece + (width,), bf16),
+            sds((2 * tok, width), bf16),
         ],
         60,
         in_specs=[any_spec] * 5 + [vmem_spec] * 6,
-        out_specs=[vmem_spec, any_spec, vmem_spec, vmem_spec] + [any_spec] * 4,
+        out_specs=[vmem_spec, any_spec, vmem_spec, vmem_spec] + [any_spec] * 3 + [vmem_spec],
     )(db_in, ex_in, grad_gate_up, grad_down, out_part.reshape(per_e + (width,)), x1, b, cotangent, rw, router_pad, gains)
     if not early:
         land_gu, land_dn = norm_gu, norm_dn
 
-    d_qkv, qk_gain, grad_out, hidden_out, two_gu, own_gu, far_dn = comm_call(
+    small_rows = (8 + -(-experts_all // 8) * 8, d_slice)
+    hidden_out, grad_hidden, sums, grad_out, grad_qkv, two_gu, own_gu, two_dn, own_dn = comm_call(
         functools.partial(back_kernel, dims),
         2,
-        80,
+        140,
         60,
         [
             vm((length, width), bf16),
@@ -1310,62 +1290,18 @@
             vm((length, cols), bf16),
             vm((length, HEAD_DIM), f32),
             vm((length, HEAD_DIM), f32),
+            vm((16, HEAD_DIM), f32),
+            vm((length, width), bf16),
+            vm((n_shard, n_expert, rows_e, cols), bf16),
             vm((2, d_slice // 2, ff2), bf16),
             vm((2, group - 1, d_slice // 2, ff2), bf16),
             vm((ff, d_slice), bf16),
             vm((group - 1, ff, d_slice), bf16),
-            vm(piece + (width,), bf16),
-            vm((tok, width), bf16),
             vm((tok, width), bf16),
             vm((n_expert, share, width), bf16),
             vm((chips, share, width), bf16),
             vm((chips - 1, share, width), bf16),
             vm((share, width), bf16),
-        ],
-        [
-            sds((length, cols), bf16),
-            sds((16, HEAD_DIM), f32),
-            sds((n_expert, share, width), bf16),
-            sds((tok, width), bf16),
-            sds((d_slice, ff2), bf16),
-            sds((group - 1, d_slice, ff2), bf16),
-            sds((ff, d_slice), bf16),
-        ],
-        60,
-        in_specs=[any_spec] * 10 + [vmem_spec] + [any_spec] * 6 + [vmem_spec],
-        out_specs=[any_spec, vmem_spec, any_spec, vmem_spec] + [any_spec] * 3,
-    )(
-        d_o,
-        w_attn_out[0],
-        o,
-        q,
-        k,
-        v,
-        raw,
-        cos,
-        sin,
-        seg_col,
-        small_all,
-        grad_gate_up,
-        grad_down,
-        land_gu,
-        late_gu,
-        land_dn,
-        out_in,
-        x1,
-    )
-
-    small_rows = (8 + -(-experts_all // 8) * 8, d_slice)
-    grad_hidden, grad_qkv, sums, two_dn, own_dn = comm_call(
-        functools.partial(tail_kernel, dims),
-        3,
-        100,
-        16,
-        [
-            vm((length, cols), bf16),
-            vm((n_shard, n_expert, rows_e, cols), bf16),
-            vm((length, width), bf16),
-            vm((length, width), bf16),
             vm((n_shard - 1, tok, width), bf16),
             vm((n_expert, n_shard, rows_e, cols), bf16),
             vm((chips, n_shard, rows_e, cols), bf16),
@@ -1379,16 +1315,47 @@
             vm((chips - 1,) + small_rows, f32),
         ],
         [
+            sds((tok, width), bf16),
             sds((tok, width), f32),
+            sds(small_rows, f32),
+            sds((n_expert, share, width), bf16),
             sds((n_expert, rows_e, qkv_cols), bf16),
-            sds(small_rows, f32),
+            sds((d_slice, ff2), bf16),
+            sds((group - 1, d_slice, ff2), bf16),
             sds((ff, d_slice), bf16),
             sds((group - 1, ff, d_slice), bf16),
         ],
-        56,
-        in_specs=[any_spec] * 5 + [vmem_spec] * 6,
-        out_specs=[vmem_spec, any_spec, vmem_spec, any_spec, any_spec],
-    )(d_qkv, heads, a, grad_down, far_dn, gx1, hidden_in, gains, gain_two, g_router, qk_gain)
+        60,
+        in_specs=[any_spec] * 18 + [vmem_spec] * 8,
+        out_specs=[vmem_spec] * 3 + [any_spec] * 6,
+    )(
+        d_o,
+        w_attn_out[0],
+        o,
+        q,
+        k,
+        v,
+        raw,
+        cos,
+        sin,
+        seg_col,
+        a,
+        heads,
+        grad_gate_up,
+        grad_down,
+        land_gu,
+        late_gu,
+        land_dn,
+        out_sum,
+        out_sum[:tok],
+        small_all,
+        x1,
+        gx1,
+        hidden_in,
+        gains,
+        gain_two,
+        g_router,
+    )
 
     def settle(own, others, other):
         total = own.astype(f32) + jnp.sum(others.astype(f32), axis=0)

time: 788 us -> 749 us (0.951)
  Pallas kernels: 734 us -> 695 us
    pallas_call x5 -> x4, Pallas kernels: 734 us -> 695 us  [call(): pl.pallas_call(kernel, out_shape=outs, in_specs=in_specs or [any_spec] *...]
where the time goes in v3:
time: 749 us; the launch traced here: 738 us
  Pallas kernels  695 us (93%)
  other arithmetic  25.8 us (3%)
  local copies, waits for them, and re-layouts  14.5 us (2%)
    pallas_call x4, Pallas kernels, call(): pl.pallas_call(kernel, out_shape=outs, in_specs=in_specs or [any_spec] *...  695 us

profile of v3, /device:TPU:0, one launch (start us, length us, event | category | flops | bytes accessed | tf_op | source)
XLA Modules:
  0.0 737.8 jit_solution(8823818605448465274)
XLA Ops:
  0.6 0.7 scatter.14
  1.3 1.5 dynamic_update_slice.3
  2.8 0.7 fusion.9
  3.5 0.1 scatter.18
  3.6 1.3 pad_maximum_fusion.2.small
  5.0 1.0 fusion.6
  6.0 1.0 pad_maximum_fusion
  7.0 0.8 copy.23
  7.8 0.9 convert_reduce_fusion.mask
  8.6 0.7 broadcast_in_dim.19.seg_own
  9.3 0.0 copy-start.4
  9.3 266.5 %shard_map.178 = (bf16[4,32,512]{2,1,0:T(8,128)(2,1)}, f32[512,128]{1,0:T(8,128)}, bf16[4,8,64,1280]{3,2,1,0:T(8,128)(2,1)}, bf16[512,2048]{1,0:T(8,128)(2,1)}, ...) custom-call(bf16[128,2048]{1,0:T(8,128)(2,1)} %x.11, ...), custom_call_target="tpu_custom_call" | custom-call | tf_op jit(solution)/shard_map/pallas_call | solution.py:156
  275.9 0.8 slice_bitcast_fusion
  276.7 0.0 copy-done.4
  276.7 1.4 fusion.10
  278.1 0.2 fusion.8
  278.3 0.1 fusion.7
  278.4 0.6 concatenate.25.rw
  279.1 0.8 concatenate.24.router_t
  279.9 143.7 %shard_map.179 = (bf16[8,256,2048]{2,1,0:T(8,128)(2,1)}, bf16[4,512,1536]{2,1,0:T(8,128)(2,1)}, bf16[768,2048]{1,0:T(8,128)(2,1)}, bf16[4,256,2048]{2,1,0:T(8,12...) custom-call(bf16[256,2048]{1,0:T(8,128)(2,1)} %get-tuple-element.82.b_pair, ...), custom_call_target="tpu_custom_call" | custom-call | tf_op jit(solution)/shard_map/pallas_call | solution.py:156
  423.6 0.8 slice.74
  424.4 0.6 pad_convert_fusion.gains
  425.1 72.0 %shard_map.180 = (f32[128,2048]{1,0:T(8,128)}, bf16[512,2048]{1,0:T(8,128)(2,1)}, f32[8,2048]{1,0:T(8,128)}, f32[128,2048]{1,0:T(8,128)}, bf16[16,128]{1,0:T(8,1...) custom-call(bf16[4,256,2048]{2,1,0:T(8,128)(2,1)} %get-tuple-element.87.db, ...), custom_call_target="tpu_custom_call" | custom-call | tf_op jit(solution)/shard_map/pallas_call | solution.py:156
  497.1 1.9 slice.75.out_sum_own
  499.0 212.7 %shard_map.181 = (bf16[128,2048]{1,0:T(8,128)(2,1)}, f32[128,2048]{1,0:T(8,128)}, f32[24,512]{1,0:T(8,128)}, bf16[8,128,2048]{2,1,0:T(8,128)(2,1)}, bf16[8,64,51...) custom-call(bf16[512,2048]{1,0:T(8,128)(2,1)} %get-tuple-element.94., ...), custom_call_target="tpu_custom_call" | custom-call | tf_op jit(solution)/shard_map/pallas_call | solution.py:156
  711.6 2.1 fusion.2
  713.7 0.0 copy-start.1
  713.7 0.0 copy-start.2
  713.7 2.0 maximum_bitcast_fusion.1
  715.7 0.0 copy-done.1
  715.7 1.0 copy-done.2
  716.7 2.4 fusion
  719.1 0.0 slice-start
  719.1 0.0 slice-start.1
  719.1 3.6 maximum_bitcast_fusion
  722.8 0.5 slice-done
  723.2 0.6 slice-done.1
  723.9 5.4 bitcast_convert_fusion
  729.3 0.0 copy-done
  729.3 4.4 bitcast_convert_fusion.1
  733.8 0.0 copy-done.6
  733.8 0.6 slice_bitcast_fusion.1
  734.4 0.6 dynamic-slice_bitcast_fusion
  735.0 0.6 slice_bitcast_fusion.2
  735.6 0.0 copy-done.5
  735.6 0.8 copy.32
  736.4 0.0 copy-done.3
  736.4 1.0 copy.33
  (8 shorter events, 0.0 us)
Async XLA Ops:
  9.3 267.4 %copy-start.4 = (bf16[128,128]{1,0:T(8,128)(2,1)S(1)}, bf16[128,128]{1,0:T(8,128)(2,1)}, u32[]{:S(2)}) copy-start(bf16[128,128]{1,0:T(8,128)(2,1)} %convert_reduce_fusion.mask) | copy-start | bytes 98308
  713.7 2.0 copy-start.1
  713.7 3.0 copy-start.2
  719.1 4.1 slice-start
  719.1 4.7 slice-start.1
  723.9 5.4 copy-start
  729.3 4.5 copy-start.6
  729.3 6.3 copy-start.5
  729.3 7.1 copy-start.3

commit v4 on v3

--- a/solution.py
+++ b/solution.py
@@ -147,6 +147,101 @@
             got = p(at.slot(t))
             mate.append(net.push(got, got, at.mate()))
     return mate
+
+
+def low_bit(k):
+    return k & -k
+
+
+class Gather:
+    def __init__(self, net, at, own, ref, rows):
+        self.net, self.at, self.ref, self.rows = net, at, ref, rows
+        bits = [b for b in (1 << i for i in range(10)) if b < at.n_shard]
+        self.bits = bits[::-1]
+        here = self.place(0)
+        self.copies = {b: net.push(own, here, at.z_dev(b)) for b in self.bits}
+
+    def place(self, k):
+        return self.ref.at[span(self.at.z ^ k, self.rows)]
+
+    def finish(self, then=None):
+        waiting = list(self.bits)
+        while waiting:
+            k = waiting.pop(0)
+            self.copies[k].wait_recv()
+            for b in self.bits:
+                if b < low_bit(k):
+                    got = self.place(k)
+                    self.copies[k | b] = self.net.push(got, got, self.at.z_dev(b))
+                    waiting.append(k | b)
+            if then:
+                then()
+                then = None
+
+
+class Scatter:
+    def __init__(self, net, at, part, landing, rows, step):
+        self.net, self.at, self.part, self.landing, self.rows, self.step = net, at, part, landing, rows, step
+        self.slot, self.bit, self.last = 0, 1, []
+        self.start()
+
+    def block(self, k):
+        return self.part.at[span(self.at.z ^ k, self.rows)]
+
+    def start(self):
+        bit, self.copies = self.bit, []
+        for k in [k for k in range(self.at.n_shard - 1, 0, -1) if k % (2 * bit) == bit]:
+            copy = self.net.push(self.block(k), self.landing.at[self.slot], self.at.z_dev(bit))
+            self.copies.append((k ^ bit, self.slot, copy))
+            self.slot += 1
+
+    def advance(self):
+        self.bit *= 2
+        for to, i, copy in self.copies:
+            copy.wait_recv()
+            if not to:
+                self.last.append(i)
+                continue
+
+            def add(j, _, to=to, i=i):
+                r = span(j, self.step)
+                here = pl.ds(pl.multiple_of((self.at.z ^ to) * self.rows + j * self.step, self.step), self.step)
+                value = self.part[here, :].astype(f32) + self.landing[i, r, :].astype(f32)
+                self.part[here, :] = value.astype(bf16)
+                return 0
+
+            lax.fori_loop(0, self.rows // self.step, add, 0)
+        if self.bit < self.at.n_shard:
+            self.start()
+            return True
+        return False
+
+    def finish(self):
+        while self.advance():
+            pass
+        return self.last
+
+
+def spread_near(net, at, ref):
+    own = ref.at[at.e]
+    mate = [net.push(own, own, at.mate())]
+    out = {t: net.push(own, own, at.chip_dev(t)) for t in (1, 2)}
+    half = ref.shape[1] // 2
+
+    def go_on():
+        relayed = []
+        for t in (1, 2):
+            out[t].wait_recv()
+            got = ref.at[at.slot(t)]
+            mate.append(net.push(got, got, at.mate()))
+            part = ref.at[at.slot(t), pl.ds((2 - t) * half, half)]
+            relayed.append(net.push(part, part, at.chip_dev(3 - t)))
+        arrive(relayed)
+        got = ref.at[at.slot(3)]
+        mate.append(net.push(got, got, at.mate()))
+        return mate
+
+    return go_on
 
 
 def comm_call(kernel, cid, n_remote, n_local, scratch, outs, vmem_mb, in_specs=None, out_specs=None, cost=None):
@@ -260,15 +355,12 @@
     for t in range(1, at.n_shard):
         got_x.append(net.push(small, small_all.at[z], at.z_dev(t)))
         got_x.append(net.push(seg_own, seg_col.at[span(z, tok)], at.z_dev(t)))
-        got_x.append(net.push(x, x_all.at[span(z, tok)], at.z_dev(t)))
+    gather_x = Gather(net, at, x, x_all, tok)
     for c in local_heads:
         c.wait()
     arrive(got_heads)
     pieces = [lambda who: heads.at[:, who]]
     heads_state = spread(net, at, pieces)
-    for c in first:
-        c.wait()
-    arrive(got_x)
     other = (z ^ group) // group
     cut = d_slice // 2
     low, high = pl.ds(0, cut), pl.ds(cut, cut)
@@ -282,7 +374,10 @@
         src, dst, got = pieces_w[i]
         from_partner[i] = (net.push(src, dst, at.z_dev(group)), got)
 
-    fetch_piece(0)
+    for c in first:
+        c.wait()
+    gather_x.finish(lambda: fetch_piece(0))
+    arrive(got_x)
 
     def hand_on(i):
         copy, ref = from_partner[i]
@@ -314,6 +409,7 @@
         return 0
 
     lax.fori_loop(0, length // step, norm_rows, 0)
+    fetch_piece(1)
     last = pass_on(net, at, pieces, heads_state)
     arrive(last)
     keep = [net.copy(heads, heads_out), net.copy(a, a_out), net.copy(small_all, small_out), net.copy(seg_col, seg_out)]
@@ -350,7 +446,6 @@
     cots = [lambda who: cot_all.at[who], lambda who: mask_all.at[who]]
     cot_state = spread(net, at, cots)
 
-    fetch_piece(1)
 
     def one_head(h, _):
         for i in range(length // block):
@@ -371,15 +466,16 @@
         return 0
 
     lax.fori_loop(0, width // wide_o, out_tile, 0)
-    sums = [net.push(part.at[span(z ^ t, tok)], parts_in.at[t - 1], at.z_dev(t)) for t in range(1, at.n_shard)]
-    last = pass_on(net, at, cots, cot_state)
-    arrive(sums)
+    summing = Scatter(net, at, part, parts_in, tok, step)
+    more = summing.advance()
+    hand_on(1)
+    slots = summing.finish() if more else summing.last
 
     def middle_rows(i, _):
         rows = span(i, step)
         total = part[pl.ds(pl.multiple_of(z * tok + i * step, step), step), :].astype(f32)
-        for t in range(1, at.n_shard):
-            total += parts_in[t - 1, rows, :].astype(f32)
+        for t in slots:
+            total += parts_in[t, rows, :].astype(f32)
         value = x_all[pl.ds(pl.multiple_of(z * tok + i * step, step), step), :].astype(f32) + total
         x1[rows, :] = value
         b_own[rows, :] = (value * inv_rms(value) * gains[1:2, :]).astype(bf16)
@@ -388,7 +484,7 @@
     lax.fori_loop(0, tok // step, middle_rows, 0)
     swap = net.push(b_own, b_pair.at[half1], at.z_dev(group))
     keep += [net.copy(b_own, b_pair.at[half0]), net.copy(x1, x1_out), net.copy(b_own, b_out)]
-    hand_on(1)
+    last = pass_on(net, at, cots, cot_state)
     swap.wait_recv()
     arrive(last + got_w)
     for c in keep:
@@ -897,6 +993,21 @@
         d_qkv[rows, pl.ds(hd + HEAD_DIM, HEAD_DIM)] = dv[rows, :].astype(bf16)
         qk_gain[8:16, :] += eight(per)
 
+    arrive(g_outs)
+
+    def own_share(i, _):
+        rows = span(i, step)
+        total = g_out[e, rows, :].astype(f32)
+        for t in range(1, at.chips):
+            total += g_in[t - 1, rows, :].astype(f32)
+        share_own[rows, :] = total.astype(bf16)
+        return 0
+
+    lax.fori_loop(0, share // step, own_share, 0)
+    keep_att = net.copy(share_own, g_att.at[e])
+    keep_att.wait()
+    atts = [lambda who: g_att.at[who]]
+    att_state = spread(net, at, atts)
     for c in load_c:
         c.wait()
     wide_d = tiled(d_slice, 256)
@@ -922,7 +1033,7 @@
         return 0
 
     lax.fori_loop(0, at.n_shard, rows_tile, 0)
-    sums = [net.push(part.at[span(z ^ t, tok)], parts_in.at[t - 1], at.z_dev(t)) for t in range(1, at.n_shard)]
+    sums = Scatter(net, at, part, parts_in, tok, step)
     chips = []
     for t in halves(at):
         mates[t].wait_recv()
@@ -935,18 +1046,7 @@
         lax.fori_loop(0, at.n_shard, add, 0)
         if t:
             chips.append(net.push(g_heads.at[who], chip_in.at[t - 1], at.chip_dev(t)))
-    arrive(g_outs)
-
-    def own_share(i, _):
-        rows = span(i, step)
-        total = g_out[e, rows, :].astype(f32)
-        for t in range(1, at.chips):
-            total += g_in[t - 1, rows, :].astype(f32)
-        share_own[rows, :] = total.astype(bf16)
-        return 0
-
-    lax.fori_loop(0, share // step, own_share, 0)
-    keep_att = net.copy(share_own, g_att.at[e])
+    more = sums.advance()
     for c in load_dn:
         c.wait()
     add_up(sum_dn, add_dn)
@@ -970,13 +1070,10 @@
     lax.fori_loop(0, at.n_shard, total, 0)
     turns = [net.push(mine.at[z ^ t], turn_in.at[z], at.z_dev(t)) for t in range(1, at.n_shard)]
     turn_own = net.copy(mine.at[z], turn_in.at[z])
-    keep_att.wait()
-    atts = [lambda who: g_att.at[who]]
-    att_state = spread(net, at, atts)
     got.append(net.push(sum_dn, two_dn, at.z_dev(group)))
     for t in range(1, group):
         got.append(net.push(d_cols(gdn, z ^ t), own_dn.at[t - 1], at.z_dev(t)))
-    arrive(sums)
+    slots = sums.finish() if more else sums.last
     sm[...] = jnp.zeros_like(sm)
     gain_one = jnp.zeros((8, width), f32)
 
@@ -984,8 +1081,8 @@
         rows = span(i, step)
         here = pl.ds(pl.multiple_of(z * tok + i * step, step), step)
         da = part[here, :].astype(f32)
-        for t in range(1, at.n_shard):
-            da += parts_in[t - 1, rows, :].astype(f32)
+        for t in slots:
+            da += parts_in[t, rows, :].astype(f32)
         back, per = rms_back(x[rows, :].astype(f32), gains[0:1, :], da)
         g_hidden[rows, :] = gx1[rows, :] + back
         return gain_one + eight(per)
@@ -1017,8 +1114,12 @@
             share_qkv[:, pl.ds(to * HEAD_DIM, HEAD_DIM)] = value.astype(bf16)
     keep = net.copy(share_qkv, g_qkv.at[e])
     keep.wait()
-    qkvs = [lambda who: g_qkv.at[who]]
-    state = spread(net, at, qkvs)
+    if at.chips == 4:
+        go_on = spread_near(net, at, g_qkv)
+    else:
+        qkvs = [lambda who: g_qkv.at[who]]
+        state = spread(net, at, qkvs)
+        go_on = functools.partial(pass_on, net, at, qkvs, state)
     last = pass_on(net, at, atts, att_state)
     arrive(small_z)
     value = sm[z]
@@ -1029,7 +1130,7 @@
     c.wait_recv()
     sm_core[...] = sm[z] + sm_core[...]
     smalls = [net.push(sm_core, sm_chip.at[t - 1], at.chip_dev(t)) for t in range(1, at.chips)]
-    last += pass_on(net, at, qkvs, state)
+    last += go_on()
     arrive(smalls)
     value = sm_core[...]
     for t in range(1, at.chips):

time: 749 us -> 697 us (0.931)
  Pallas kernels: 695 us -> 645 us
    pallas_call x4, Pallas kernels: 695 us -> 645 us  [call(): pl.pallas_call(kernel, out_shape=outs, in_specs=in_specs or [any_spec] *...]
where the time goes in v4:
time: 697 us; the launch traced here: 688 us
  Pallas kernels  645 us (93%)
  other arithmetic  25.8 us (4%)
  local copies, waits for them, and re-layouts  14.5 us (2%)
    pallas_call x4, Pallas kernels, call(): pl.pallas_call(kernel, out_shape=outs, in_specs=in_specs or [any_spec] *...  645 us

profile of v4, /device:TPU:0, one launch (start us, length us, event | category | flops | bytes accessed | tf_op | source)
XLA Modules:
  0.0 687.5 jit_solution(13230188483201629078)
XLA Ops:
  0.6 0.7 scatter.14
  1.3 1.5 dynamic_update_slice.3
  2.8 0.7 fusion.9
  3.5 0.1 scatter.18
  3.6 1.3 pad_maximum_fusion.2.small
  5.0 1.0 fusion.6
  6.0 1.0 pad_maximum_fusion
  7.0 0.8 copy.23
  7.8 0.9 convert_reduce_fusion.mask
  8.6 0.7 broadcast_in_dim.19.seg_own
  9.3 0.0 copy-start.4
  9.3 229.8 %shard_map.178 = (bf16[4,32,512]{2,1,0:T(8,128)(2,1)}, f32[512,128]{1,0:T(8,128)}, bf16[4,8,64,1280]{3,2,1,0:T(8,128)(2,1)}, bf16[512,2048]{1,0:T(8,128)(2,1)}, ...) custom-call(bf16[128,2048]{1,0:T(8,128)(2,1)} %x.11, ...), custom_call_target="tpu_custom_call" | custom-call | tf_op jit(solution)/shard_map/pallas_call | solution.py:251
  239.1 0.8 slice_bitcast_fusion
  240.0 0.0 copy-done.4
  240.0 1.4 fusion.10
  241.4 0.2 fusion.8
  241.6 0.1 fusion.7
  241.7 0.6 concatenate.25.rw
  242.4 0.8 concatenate.24.router_t
  243.2 139.3 %shard_map.179 = (bf16[8,256,2048]{2,1,0:T(8,128)(2,1)}, bf16[4,512,1536]{2,1,0:T(8,128)(2,1)}, bf16[768,2048]{1,0:T(8,128)(2,1)}, bf16[4,256,2048]{2,1,0:T(8,12...) custom-call(bf16[256,2048]{1,0:T(8,128)(2,1)} %get-tuple-element.82.b_pair, ...), custom_call_target="tpu_custom_call" | custom-call | tf_op jit(solution)/shard_map/pallas_call | solution.py:251
  382.5 0.8 slice.74
  383.3 0.6 pad_convert_fusion.gains
  383.9 73.2 %shard_map.180 = (f32[128,2048]{1,0:T(8,128)}, bf16[512,2048]{1,0:T(8,128)(2,1)}, f32[8,2048]{1,0:T(8,128)}, f32[128,2048]{1,0:T(8,128)}, bf16[16,128]{1,0:T(8,1...) custom-call(bf16[4,256,2048]{2,1,0:T(8,128)(2,1)} %get-tuple-element.87.db, ...), custom_call_target="tpu_custom_call" | custom-call | tf_op jit(solution)/shard_map/pallas_call | solution.py:251
  457.1 1.9 slice.75.out_sum_own
  459.0 202.3 %shard_map.181 = (bf16[128,2048]{1,0:T(8,128)(2,1)}, f32[128,2048]{1,0:T(8,128)}, f32[24,512]{1,0:T(8,128)}, bf16[8,128,2048]{2,1,0:T(8,128)(2,1)}, bf16[8,64,51...) custom-call(bf16[512,2048]{1,0:T(8,128)(2,1)} %get-tuple-element.94., ...), custom_call_target="tpu_custom_call" | custom-call | tf_op jit(solution)/shard_map/pallas_call | solution.py:251
  661.3 2.1 fusion.2
  663.4 0.0 copy-start.1
  663.4 0.0 copy-start.2
  663.4 2.0 maximum_bitcast_fusion.1
  665.4 0.0 copy-done.1
  665.4 1.0 copy-done.2
  666.4 2.4 fusion
  668.8 0.0 slice-start
  668.8 0.0 slice-start.1
  668.8 3.6 maximum_bitcast_fusion
  672.5 0.5 slice-done
  672.9 0.6 slice-done.1
  673.6 5.4 bitcast_convert_fusion
  679.0 0.0 copy-done
  679.0 4.4 bitcast_convert_fusion.1
  683.5 0.0 copy-done.6
  683.5 0.6 slice_bitcast_fusion.1
  684.1 0.6 dynamic-slice_bitcast_fusion
  684.7 0.6 slice_bitcast_fusion.2
  685.3 0.0 copy-done.5
  685.3 0.8 copy.32
  686.1 0.0 copy-done.3
  686.1 1.0 copy.33
  (8 shorter events, 0.0 us)
Async XLA Ops:
  9.3 230.6 %copy-start.4 = (bf16[128,128]{1,0:T(8,128)(2,1)S(1)}, bf16[128,128]{1,0:T(8,128)(2,1)}, u32[]{:S(2)}) copy-start(bf16[128,128]{1,0:T(8,128)(2,1)} %convert_reduce_fusion.mask) | copy-start | bytes 98308
  663.4 2.0 copy-start.1
  663.4 3.0 copy-start.2
  668.8 4.1 slice-start
  668.8 4.7 slice-start.1
  673.6 5.4 copy-start
  679.0 4.5 copy-start.6
  679.0 6.3 copy-start.5
  679.0 7.1 %copy-start.3 = (f32[128,2048]{1,0:T(8,128)S(1)}, f32[128,2048]{1,0:T(8,128)}, u32[]{:S(2)}) copy-start(f32[128,2048]{1,0:T(8,128)} %get-tuple-element.142) | copy-start | bytes 3145732

commit v5 on v4

--- a/solution.py
+++ b/solution.py
@@ -2,6 +2,7 @@
 
 import jax
 import jax.numpy as jnp
+import numpy as np
 from jax import lax
 from jax.experimental import pallas as pl
 from jax.experimental.pallas import tpu as pltpu
@@ -49,10 +50,10 @@
 
 def rotary_tables(length):
     half = HEAD_DIM // 2
-    frequency = rope_base ** (-(jnp.arange(half, dtype=f32) * 2.0) / HEAD_DIM)
-    angles = jnp.arange(length, dtype=f32)[:, None] * frequency[None, :]
-    cos, sin = jnp.cos(angles), jnp.sin(angles)
-    return jnp.concatenate([cos, cos], axis=1), jnp.concatenate([-sin, sin], axis=1)
+    frequency = np.float32(rope_base) ** (-(np.arange(half, dtype=np.float32) * np.float32(2.0)) / np.float32(HEAD_DIM))
+    angles = np.arange(length, dtype=np.float32)[:, None] * frequency[None, :].astype(np.float32)
+    cos, sin = np.cos(angles), np.sin(angles)
+    return jnp.asarray(np.concatenate([cos, cos], axis=1)), jnp.asarray(np.concatenate([-sin, sin], axis=1))
 
 
 MESH = pl.DeviceIdType.MESH
@@ -311,8 +312,8 @@
 def front_kernel(
     dims, x, small, seg_own, w_qkv, w_out, w_gu, cot, mask, cos_h, sin_h,
     small_out, seg_out, heads_out, a_out, raw_out, q_out, k_out, v_out, o_out, x1_out, b_out,
-    gate_up, cot_all, mask_all, b_pair,
-    x_all, small_all, seg_col, heads, a, raw, q, k, v, o, w_o, part, parts_in, cos, sin, gains, seg_row, x1, b_own,
+    gate_up, cot_all, mask_all, b_pair, gains, router_pad,
+    x_all, small_all, seg_col, heads, a, raw, q, k, v, o, w_o, part, parts_in, cos, sin, seg_row, x1, b_own,
     send, recv, local,
 ):
     at = Place(*dims)
@@ -393,10 +394,13 @@
         net.push(mask, mask_all.at[e, half1], at.z_dev(group)),
     ]
 
+    gains[...] = jnp.zeros_like(gains)
+    router_pad[...] = jnp.zeros_like(router_pad)
     qk = []
     for s in range(at.n_shard):
         rows = small_all[s, 0:16, :].astype(f32)
         gains[0:2, span(s, d_slice)] = rows[0:2]
+        router_pad[0 : small.shape[0] - 16, span(s, d_slice)] = small_all[s, 16:, :]
         seg_row[0:1, span(s, tok)] = rows[4:5, :tok]
         qk.append(rows[2:4, :HEAD_DIM])
     qk = sum(qk[1:], qk[0])
@@ -494,7 +498,7 @@
 
 def expert_kernel(
     dims, b_pair, cot_all, mask_all, gate_up, w_gu_in, w_dn_in, router_t,
-    out_part, ggu, gdn, db_in, ex_in, land_gu, land_dn,
+    out_part, ggu, gdn, db_in, ex_in, land_dn,
     w_gu, w_dn, rows, cot_t, mask_t, hid, d_pre, d_y, stage, stage_x, own, own_x, core_in, core_x, w_r, d_r, g_tile, d_tile,
     tile_sem, send, recv, local,
 ):
@@ -540,7 +544,21 @@
     near = [t for t in (1, 2) if t < at.chips]
     beyond = [t for t in range(1, at.chips) if t not in near]
     from_chip = {t: net.push(b_pair, rows.at[t, 1], at.chip_dev(t)) for t in near}
-    from_partner = net.push(w_dn_in.at[other], d_cols(z), at.z_dev(group))
+    half_ff = [pl.ds(0, ff // 2), pl.ds(ff // 2, ff // 2)]
+
+    def dn_part(who, i):
+        return w_dn.at[half_ff[i], span(who, d_slice)]
+
+    def fetch_dn(i):
+        return net.push(w_dn_in.at[other, half_ff[i]], dn_part(z, i), at.z_dev(group))
+
+    from_partner = [fetch_dn(0)]
+
+    def hand_on(i):
+        from_partner[i].wait_recv()
+        for t in range(1, group):
+            got_dn.append(net.push(dn_part(far, i), dn_part(far, i), at.z_dev(t)))
+
     got_dn = [net.push(w_dn_in.at[mine], d_cols(z), at.z_dev(t)) for t in range(1, group)]
 
     relayed = []
@@ -582,17 +600,17 @@
     for c in loads:
         c.wait()
     up_rows(0)
+    from_partner.append(fetch_dn(1))
     for i in near:
         pass_rows(i)
         if beyond:
             part = pl.ds((2 - i) * (two // 2), two // 2)
             relayed.append(net.push(rows.at[i, 1, part], rows.at[3, 1, part], at.chip_dev(3 - i)))
-    from_partner.wait_recv()
-    for t in range(1, group):
-        got_dn.append(net.push(d_cols(far), d_cols(far), at.z_dev(t)))
+    hand_on(0)
     for t in near:
         from_mate[t].wait_recv()
         up_rows(t)
+    hand_on(1)
     for t in beyond:
         pass_rows(t)
         from_mate[t].wait_recv()
@@ -726,9 +744,6 @@
     lax.fori_loop(0, n_early, grad_up, 0)
     for i in range(n_early - 2, n_early):
         out_copy(i % 2, i).wait()
-    half = pl.ds(0, d_slice // 2)
-    for t in range(1, group):
-        outs.append(net.push(ggu.at[z ^ t ^ group, half], land_gu.at[t - 1], at.z_dev(t)))
 
     def grad_rest(i, _):
         slot = i % 2
@@ -753,9 +768,9 @@
 
 
 def norm_kernel(
-    dims, early, db, ex, ggu, gdn, out_part, x1, b, cot, rw, router_t, gains,
-    gx1, do_all, gain_two, g_router, land_gu, late_gu, land_dn, out_sum,
-    own, own_x, half_out, half_x, swap_in, swap_x, logit, d_out, out_own, out_core, out_in,
+    dims, early, db, ex, ggu, gdn, out_part, x1, b, cot, mask, router_t, gains,
+    gx1, do_all, gain_two, g_router, land_gu, late_gu, land_dn, out_own_sum, out_sum,
+    own, own_x, half_out, half_x, swap_in, swap_x, logit, d_out, out_own, out_core, out_in, rw,
     send, recv, local,
 ):
     at = Place(*dims)
@@ -789,11 +804,16 @@
     landed = []
     for t in range(1, group):
         j = z ^ t ^ group
+        landed.append(net.push(ggu.at[j, pl.ds(0, d_slice // 2)], land_gu.at[t - 1], at.z_dev(t)))
         if not early:
-            landed.append(net.push(ggu.at[j, pl.ds(0, d_slice // 2)], land_gu.at[t - 1], at.z_dev(t)))
             landed.append(net.push(gdn.at[:, span(j, d_slice)], land_dn.at[t - 1], at.z_dev(t)))
         landed.append(net.push(ggu.at[j, pl.ds(d_slice // 2, d_slice // 2)], late_gu.at[t - 1], at.z_dev(t)))
     mates = {t: net.push(out_part.at[at.slot(t, 1)], out_core.at[t], at.mate()) for t in halves(at)}
+    logits = mm_nt(b[...], router_t[...])
+    chosen = mask[...].astype(f32) > 0
+    masked = jnp.where(chosen, logits, neg_fill)
+    raised = jnp.where(chosen, jnp.exp(masked - jnp.max(masked, axis=1, keepdims=True)), 0.0)
+    rw[...] = raised / jnp.sum(raised, axis=1, keepdims=True)
     outs = []
     for t in halves(at):
         load_own[t].wait()
@@ -839,15 +859,23 @@
     g_router[...] = mm_tn(logit[0], b[...]) + mm_tn(logit[1], b[...])
     arrive(outs)
 
-    def out_rows(i, _):
+    def out_rows(i):
         rows = span(i, step)
         total = out_own[0, rows, :].astype(f32)
         for t in range(1, at.chips):
             total += out_in[t - 1, rows, :].astype(f32)
-        out_sum[rows, :] = total.astype(bf16)
-        return 0
-
-    lax.fori_loop(0, 2 * tok // step, out_rows, 0)
+        return total.astype(bf16)
+
+    def own_rows(i, _):
+        out_own_sum[span(i, step), :] = out_rows(i)
+        return 0
+
+    def partner_rows(i, _):
+        out_sum[span(i, step), :] = out_rows(tok // step + i)
+        return 0
+
+    lax.fori_loop(0, tok // step, own_rows, 0)
+    lax.fori_loop(0, tok // step, partner_rows, 0)
     keep.wait()
     arrive(copies + landed)
     net.sent()
@@ -894,7 +922,7 @@
     load_c = [net.copy(a_h, a), net.copy(heads_h, heads)]
     load_dn = [net.copy(d_cols(gdn, far), sum_dn)] + [net.copy(land_dn.at[t - 1], add_dn.at[t - 1]) for t in range(1, group)]
     greet(everyone(at))
-    swap = net.push(out_sum.at[pl.ds(tok, tok)], swap_in, at.z_dev(group))
+    swap = net.push(out_sum, swap_in, at.z_dev(group))
 
     def add_up(total, adds):
         def rows_of(i, _):
@@ -1180,11 +1208,17 @@
     any_spec = pl.BlockSpec(memory_space=pl.ANY)
     vmem_spec = pl.BlockSpec(memory_space=pltpu.VMEM)
 
-    small = jnp.zeros((16, d_slice), bf16)
-    small = small.at[0:2, :].set(norm_gains[0])
-    small = lax.dynamic_update_slice(small, qk_gains[0], (2, me_z * qk_part))
-    small = small.at[4, :tok].set(segments.astype(bf16))
-    small = jnp.concatenate([small, w_router[0].T], axis=0)
+    lane = jnp.arange(HEAD_DIM, dtype=jnp.int32)
+    qk_placed = jnp.where((lane // qk_part == me_z)[None], jnp.tile(qk_gains[0], (1, n_shard)), jnp.zeros((), bf16))
+    small = jnp.concatenate(
+        [
+            norm_gains[0],
+            jnp.pad(qk_placed, ((0, 0), (0, d_slice - HEAD_DIM))),
+            jnp.pad(segments.astype(bf16)[None], ((0, 11), (0, d_slice - tok))),
+            w_router[0].T,
+        ],
+        axis=0,
+    )
     seg_own = jnp.broadcast_to(segments.astype(f32)[:, None], (tok, 128))
     ids = jnp.arange(128, dtype=jnp.int32)
     mask = jnp.sum((routes[:, :, None] == ids[None, None, :]).astype(f32), axis=1).astype(bf16)
@@ -1206,6 +1240,8 @@
         sds((n_expert, 2 * tok, width), bf16),
         sds((n_expert, 2 * tok, 128), bf16),
         sds((2 * tok, width), bf16),
+        sds((8, width), f32),
+        sds((128, width), bf16),
     ]
     front = comm_call(
         functools.partial(front_kernel, dims),
@@ -1228,20 +1264,18 @@
             vm((n_shard - 1, tok, width), bf16),
             vm((length, HEAD_DIM), f32),
             vm((length, HEAD_DIM), f32),
-            vm((8, width), f32),
             vm((8, length), f32),
             vm((tok, width), f32),
             vm((tok, width), bf16),
         ],
         outs,
         56,
+        out_specs=[any_spec] * (len(outs) - 2) + [vmem_spec] * 2,
     )
-    (small_all, seg_col, heads, a, raw, q, k, v, o, x1, b, gate_up, cot_all, mask_all, b_pair) = front(
+    (small_all, seg_col, heads, a, raw, q, k, v, o, x1, b, gate_up, cot_all, mask_all, b_pair, gains, router_pad) = front(
         hidden_in, small, seg_own, w_qkv[0], w_attn_out[0], w_gate_up[0], cotangent, mask, cos, sin
     )
-    gains = jnp.zeros((8, width), f32)
-    gains = gains.at[0:2].set(small_all[:, 0:2].astype(f32).transpose(1, 0, 2).reshape(2, width))
-    router_t = small_all[:, 16:].transpose(1, 0, 2).reshape(experts_all, width)
+    router_t = router_pad[:experts_all]
 
     def route_weights(rows, chosen):
         logits = mm_nt(rows, router_t)
@@ -1249,14 +1283,11 @@
         raised = jnp.where(chosen, jnp.exp(masked - jnp.max(masked, axis=1, keepdims=True)), 0.0)
         return raised / jnp.sum(raised, axis=1, keepdims=True)
 
-    rw = route_weights(b, mask[:, :experts_all] > 0)
-    rw = jnp.concatenate([rw, jnp.zeros((tok, 128 - experts_all), f32)], axis=1)
-    router_pad = jnp.concatenate([router_t, jnp.zeros((128 - experts_all, width), bf16)], axis=0)
     per_e = (n_expert, 2 * tok)
     piece = (chips, 2 * tok)
     four = 4 * tok
     if chips <= 4:
-        out_part, grad_gate_up, grad_down, db_in, ex_in, land_gu, land_dn = comm_call(
+        out_part, grad_gate_up, grad_down, db_in, ex_in, land_dn = comm_call(
             functools.partial(expert_kernel, dims),
             4,
             60,
@@ -1288,7 +1319,6 @@
                 sds((ff, width), bf16),
                 sds(piece + (width,), bf16),
                 sds(piece + (128,), bf16),
-                sds((group - 1, d_slice // 2, ff2), bf16),
                 sds((group - 1, ff, d_slice), bf16),
             ],
             60,
@@ -1334,7 +1364,7 @@
 
     n_parts = db_in.shape[0]
     early = chips <= 4
-    gx1, d_o, gain_two, g_router, norm_gu, late_gu, norm_dn, out_sum = comm_call(
+    gx1, d_o, gain_two, g_router, land_gu, late_gu, norm_dn, out_own_sum, out_sum = comm_call(
         functools.partial(norm_kernel, dims, early),
         1,
         60,
@@ -1351,23 +1381,25 @@
             vm(piece + (width,), bf16),
             vm(piece + (width,), bf16),
             vm((chips - 1, 2 * tok, width), bf16),
+            vm((tok, 128), f32),
         ],
         [
             sds((tok, width), f32),
             sds((length, width), bf16),
             sds((8, width), f32),
             sds((128, width), f32),
-            sds((group - 1, d_slice // 2, ff2), bf16) if not early else sds((16, 128), bf16),
+            sds((group - 1, d_slice // 2, ff2), bf16),
             sds((group - 1, d_slice // 2, ff2), bf16),
             sds((group - 1, ff, d_slice), bf16) if not early else sds((16, 128), bf16),
-            sds((2 * tok, width), bf16),
+            sds((tok, width), bf16),
+            sds((tok, width), bf16),
         ],
         60,
         in_specs=[any_spec] * 5 + [vmem_spec] * 6,
-        out_specs=[vmem_spec, any_spec, vmem_spec, vmem_spec] + [any_spec] * 3 + [vmem_spec],
-    )(db_in, ex_in, grad_gate_up, grad_down, out_part.reshape(per_e + (width,)), x1, b, cotangent, rw, router_pad, gains)
+        out_specs=[vmem_spec, any_spec, vmem_spec, vmem_spec] + [any_spec] * 3 + [vmem_spec] * 2,
+    )(db_in, ex_in, grad_gate_up, grad_down, out_part.reshape(per_e + (width,)), x1, b, cotangent, mask, router_pad, gains)
     if not early:
-        land_gu, land_dn = norm_gu, norm_dn
+        land_dn = norm_dn
 
     small_rows = (8 + -(-experts_all // 8) * 8, d_slice)
     hidden_out, grad_hidden, sums, grad_out, grad_qkv, two_gu, own_gu, two_dn, own_dn = comm_call(
@@ -1448,7 +1480,7 @@
         late_gu,
         land_dn,
         out_sum,
-        out_sum[:tok],
+        out_own_sum,
         small_all,
         x1,
         gx1,

time: 697 us -> 686 us (0.984)
  no operation moved by 1% of the time
where the time goes in v5:
time: 686 us; the launch traced here: 677 us
  Pallas kernels  645 us (94%)
  other arithmetic  22.9 us (3%)
  local copies, waits for them, and re-layouts  8 us (1%)
    pallas_call x4, Pallas kernels, call(): pl.pallas_call(kernel, out_shape=outs, in_specs=in_specs or [any_spec] *...  645 us

profile of v5, /device:TPU:0, one launch (start us, length us, event | category | flops | bytes accessed | tf_op | source)
XLA Modules:
  0.0 676.9 jit_solution(11765117539995854451)
XLA Ops:
  0.7 0.7 tile.11
  1.3 0.1 tile.12
  1.4 0.7 fusion.12
  2.2 1.3 fusion.9.small
  3.5 0.8 copy.23
  4.3 0.9 convert_reduce_fusion.mask
  5.1 0.7 broadcast_in_dim.44.seg_own
  5.9 230.5 %shard_map.196 = (bf16[4,32,512]{2,1,0:T(8,128)(2,1)}, f32[512,128]{1,0:T(8,128)}, bf16[4,8,64,1280]{3,2,1,0:T(8,128)(2,1)}, bf16[512,2048]{1,0:T(8,128)(2,1)}, ...) custom-call(bf16[128,2048]{1,0:T(8,128)(2,1)} %x.7, ...), custom_call_target="tpu_custom_call" | custom-call | tf_op jit(solution)/shard_map/pallas_call | solution.py:252
  236.4 125.3 %shard_map.197 = (bf16[8,256,2048]{2,1,0:T(8,128)(2,1)}, bf16[4,512,1536]{2,1,0:T(8,128)(2,1)}, bf16[768,2048]{1,0:T(8,128)(2,1)}, bf16[4,256,2048]{2,1,0:T(8,12...) custom-call(bf16[256,2048]{1,0:T(8,128)(2,1)} %get-tuple-element.49.b_pair, ...), custom_call_target="tpu_custom_call" | custom-call | tf_op jit(solution)/shard_map/pallas_call | solution.py:252
  361.7 90.5 %shard_map.198 = (f32[128,2048]{1,0:T(8,128)}, bf16[512,2048]{1,0:T(8,128)(2,1)}, f32[8,2048]{1,0:T(8,128)}, f32[128,2048]{1,0:T(8,128)}, bf16[1,256,1536]{2,1,0...) custom-call(bf16[4,256,2048]{2,1,0:T(8,128)(2,1)} %get-tuple-element, ...), custom_call_target="tpu_custom_call" | custom-call | tf_op jit(solution)/shard_map/pallas_call | solution.py:252
  452.2 198.5 %shard_map.199 = (bf16[128,2048]{1,0:T(8,128)(2,1)}, f32[128,2048]{1,0:T(8,128)}, f32[24,512]{1,0:T(8,128)}, bf16[8,128,2048]{2,1,0:T(8,128)(2,1)}, bf16[8,64,51...) custom-call(bf16[512,2048]{1,0:T(8,128)(2,1)} %get-tuple-element.62., ...), custom_call_target="tpu_custom_call" | custom-call | tf_op jit(solution)/shard_map/pallas_call | solution.py:252
  650.7 2.1 fusion.2
  652.7 0.0 copy-start.1
  652.7 0.0 copy-start.2
  652.7 2.0 maximum_bitcast_fusion.1
  654.7 0.0 copy-done.1
  654.7 1.0 copy-done.2
  655.7 2.4 fusion
  658.1 0.0 slice-start
  658.1 0.0 slice-start.1
  658.1 3.6 maximum_bitcast_fusion
  661.8 0.5 slice-done
  662.3 0.6 slice-done.1
  662.9 0.0 copy-start
  662.9 5.4 bitcast_convert_fusion
  668.3 0.0 copy-done
  668.3 0.0 copy-start.5
  668.3 0.0 copy-start.4
  668.3 0.0 copy-start.3
  668.3 4.4 bitcast_convert_fusion.1
  672.8 0.0 copy-done.5
  672.8 0.6 slice_bitcast_fusion
  673.4 0.6 dynamic-slice_bitcast_fusion
  674.0 0.6 slice_bitcast_fusion.1
  674.6 0.0 copy-done.4
  674.6 0.8 copy.26
  675.4 0.0 copy-done.3
  675.4 1.0 copy.27
  (4 shorter events, 0.0 us)
Async XLA Ops:
  652.7 2.0 copy-start.1
  652.7 3.0 copy-start.2
  658.1 4.1 slice-start
  658.1 4.7 slice-start.1
  662.9 5.4 copy-start
  668.3 4.5 copy-start.5
  668.3 6.3 copy-start.4
  668.3 7.1 %copy-start.3 = (f32[128,2048]{1,0:T(8,128)S(1)}, f32[128,2048]{1,0:T(8,128)}, u32[]{:S(2)}) copy-start(f32[128,2048]{1,0:T(8,128)} %get-tuple-element.105) | copy-start | bytes 3145732

commit v6 on v5

--- a/solution.py
+++ b/solution.py
@@ -1493,7 +1493,8 @@
     def settle(own, others, other):
         total = own.astype(f32) + jnp.sum(others.astype(f32), axis=0)
         other = other.astype(f32)
-        return jnp.stack([jnp.where(mine == 0, total, other), jnp.where(mine == 0, other, total)])[None]
+        is_own = jnp.arange(exp_dev, dtype=jnp.int32)[:, None, None] == mine
+        return jnp.where(is_own, total[None], other[None])[None]
 
     own_gate_up = lax.dynamic_index_in_dim(grad_gate_up, me_z, 0, keepdims=False)
     own_down = lax.dynamic_slice_in_dim(grad_down, me_z * d_slice, d_slice, 1)

time: 686 us -> 685 us (level)
  no operation moved by 1% of the time
where the time goes in v6:
time: 685 us; the launch traced here: 675 us
  Pallas kernels  645 us (94%)
  other arithmetic  23.5 us (3%)
    pallas_call x4, Pallas kernels, call(): pl.pallas_call(kernel, out_shape=outs, in_specs=in_specs or [any_spec] *...  645 us

profile of v6, /device:TPU:0, one launch (start us, length us, event | category | flops | bytes accessed | tf_op | source)
XLA Modules:
  0.0 675.4 jit_solution(9683196118629209822)
XLA Ops:
  0.7 0.7 tile.11
  1.3 0.1 tile.12
  1.4 0.7 fusion.8
  2.2 1.3 fusion.5.small
  3.5 0.8 copy.23
  4.3 0.9 convert_reduce_fusion.mask
  5.1 0.7 broadcast_in_dim.96.seg_own
  5.9 230.5 %shard_map.196 = (bf16[4,32,512]{2,1,0:T(8,128)(2,1)}, f32[512,128]{1,0:T(8,128)}, bf16[4,8,64,1280]{3,2,1,0:T(8,128)(2,1)}, bf16[512,2048]{1,0:T(8,128)(2,1)}, ...) custom-call(bf16[128,2048]{1,0:T(8,128)(2,1)} %x.7, ...), custom_call_target="tpu_custom_call" | custom-call | tf_op jit(solution)/shard_map/pallas_call | solution.py:252
  236.4 125.3 %shard_map.197 = (bf16[8,256,2048]{2,1,0:T(8,128)(2,1)}, bf16[4,512,1536]{2,1,0:T(8,128)(2,1)}, bf16[768,2048]{1,0:T(8,128)(2,1)}, bf16[4,256,2048]{2,1,0:T(8,12...) custom-call(bf16[256,2048]{1,0:T(8,128)(2,1)} %get-tuple-element.49.b_pair, ...), custom_call_target="tpu_custom_call" | custom-call | tf_op jit(solution)/shard_map/pallas_call | solution.py:252
  361.7 90.5 %shard_map.198 = (f32[128,2048]{1,0:T(8,128)}, bf16[512,2048]{1,0:T(8,128)(2,1)}, f32[8,2048]{1,0:T(8,128)}, f32[128,2048]{1,0:T(8,128)}, bf16[1,256,1536]{2,1,0...) custom-call(bf16[4,256,2048]{2,1,0:T(8,128)(2,1)} %get-tuple-element, ...), custom_call_target="tpu_custom_call" | custom-call | tf_op jit(solution)/shard_map/pallas_call | solution.py:252
  452.2 198.4 %shard_map.199 = (bf16[128,2048]{1,0:T(8,128)(2,1)}, f32[128,2048]{1,0:T(8,128)}, f32[24,512]{1,0:T(8,128)}, bf16[8,128,2048]{2,1,0:T(8,128)(2,1)}, bf16[8,64,51...) custom-call(bf16[512,2048]{1,0:T(8,128)(2,1)} %get-tuple-element.62., ...), custom_call_target="tpu_custom_call" | custom-call | tf_op jit(solution)/shard_map/pallas_call | solution.py:252
  650.6 0.0 copy-start.3
  650.6 1.7 convert_add_fusion
  652.3 0.0 copy-done.3
  652.3 0.2 convert_element_type.71
  652.5 2.3 broadcast_select_fusion.1
  654.8 0.0 copy-start.1
  654.8 2.4 add_bitcast_fusion
  657.3 0.0 copy-done.1
  657.3 0.0 slice-start
  657.3 0.4 convert_element_type.69
  657.7 0.0 slice-start.1
  657.7 3.7 broadcast_select_fusion
  661.4 0.0 slice-done
  661.4 0.0 slice-done.1
  661.4 0.0 copy-start
  661.4 5.4 bitcast_convert_fusion
  666.9 0.0 copy-done
  666.9 0.0 copy-start.5
  666.9 0.0 copy-start.4
  666.9 0.0 copy-start.2
  666.9 4.4 bitcast_convert_fusion.1
  671.3 0.0 copy-done.5
  671.3 0.6 slice_bitcast_fusion
  671.9 0.6 dynamic-slice_bitcast_fusion
  672.6 0.6 slice_bitcast_fusion.1
  673.2 0.0 copy-done.4
  673.2 0.8 copy.26
  674.0 0.0 copy-done.2
  674.0 1.0 copy.27
  (5 shorter events, 0.0 us)
Async XLA Ops:
  650.6 1.7 copy-start.3
  654.8 2.5 copy-start.1
  657.3 4.1 slice-start
  657.7 3.7 slice-start.1
  661.4 5.5 copy-start
  666.9 4.5 copy-start.5
  666.9 6.3 copy-start.4
  666.9 7.1 %copy-start.2 = (f32[128,2048]{1,0:T(8,128)S(1)}, f32[128,2048]{1,0:T(8,128)}, u32[]{:S(2)}) copy-start(f32[128,2048]{1,0:T(8,128)} %get-tuple-element.101) | copy-start | bytes 3145732

commit v7 on v6

--- a/solution.py
+++ b/solution.py
@@ -1491,10 +1491,11 @@
     )
 
     def settle(own, others, other):
-        total = own.astype(f32) + jnp.sum(others.astype(f32), axis=0)
-        other = other.astype(f32)
         is_own = jnp.arange(exp_dev, dtype=jnp.int32)[:, None, None] == mine
-        return jnp.where(is_own, total[None], other[None])[None]
+        total = jnp.where(is_own, own[None], other[None]).astype(f32)
+        for t in range(group - 1):
+            total += jnp.where(is_own, others[t][None], jnp.zeros((), bf16)).astype(f32)
+        return total[None]
 
     own_gate_up = lax.dynamic_index_in_dim(grad_gate_up, me_z, 0, keepdims=False)
     own_down = lax.dynamic_slice_in_dim(grad_down, me_z * d_slice, d_slice, 1)

time: 685 us -> 686 us (level)
    add x1 -> x2, other arithmetic: 1.67 us -> 9.07 us  [settle(): total += jnp.where(is_own, others[t][None], jnp.zeros((), bf16)).astype(f32)]
where the time goes in v7:
time: 686 us; the launch traced here: 677 us
  Pallas kernels  645 us (94%)
  other arithmetic  21.9 us (3%)
  local copies, waits for them, and re-layouts  8.73 us (1%)
    pallas_call x4, Pallas kernels, call(): pl.pallas_call(kernel, out_shape=outs, in_specs=in_specs or [any_spec] *...  645 us

profile of v7, /device:TPU:0, one launch (start us, length us, event | category | flops | bytes accessed | tf_op | source)
XLA Modules:
  0.0 676.5 jit_solution(5426779380958192957)
XLA Ops:
  0.7 0.7 tile.11
  1.3 0.1 tile.12
  1.4 0.7 fusion.8
  2.2 1.3 fusion.5.small
  3.5 0.8 copy.23
  4.3 0.9 convert_reduce_fusion.mask
  5.1 0.7 broadcast_in_dim.136.seg_own
  5.9 230.5 %shard_map.196 = (bf16[4,32,512]{2,1,0:T(8,128)(2,1)}, f32[512,128]{1,0:T(8,128)}, bf16[4,8,64,1280]{3,2,1,0:T(8,128)(2,1)}, bf16[512,2048]{1,0:T(8,128)(2,1)}, ...) custom-call(bf16[128,2048]{1,0:T(8,128)(2,1)} %x.7, ...), custom_call_target="tpu_custom_call" | custom-call | tf_op jit(solution)/shard_map/pallas_call | solution.py:252
  236.4 125.3 %shard_map.197 = (bf16[8,256,2048]{2,1,0:T(8,128)(2,1)}, bf16[4,512,1536]{2,1,0:T(8,128)(2,1)}, bf16[768,2048]{1,0:T(8,128)(2,1)}, bf16[4,256,2048]{2,1,0:T(8,12...) custom-call(bf16[256,2048]{1,0:T(8,128)(2,1)} %get-tuple-element.49.b_pair, ...), custom_call_target="tpu_custom_call" | custom-call | tf_op jit(solution)/shard_map/pallas_call | solution.py:252
  361.7 90.5 %shard_map.198 = (f32[128,2048]{1,0:T(8,128)}, bf16[512,2048]{1,0:T(8,128)(2,1)}, f32[8,2048]{1,0:T(8,128)}, f32[128,2048]{1,0:T(8,128)}, bf16[1,256,1536]{2,1,0...) custom-call(bf16[4,256,2048]{2,1,0:T(8,128)(2,1)} %get-tuple-element, ...), custom_call_target="tpu_custom_call" | custom-call | tf_op jit(solution)/shard_map/pallas_call | solution.py:252
  452.2 198.4 %shard_map.199 = (bf16[128,2048]{1,0:T(8,128)(2,1)}, f32[128,2048]{1,0:T(8,128)}, f32[24,512]{1,0:T(8,128)}, bf16[8,128,2048]{2,1,0:T(8,128)(2,1)}, bf16[8,64,51...) custom-call(bf16[512,2048]{1,0:T(8,128)(2,1)} %get-tuple-element.62., ...), custom_call_target="tpu_custom_call" | custom-call | tf_op jit(solution)/shard_map/pallas_call | solution.py:252
  650.6 1.2 constant_dynamic-slice_fusion
  651.8 0.0 copy-start.1
  651.8 3.8 convert_add_fusion.1
  655.6 0.0 slice-start
  655.6 1.7 dynamic-slice_bitcast_fusion
  657.2 0.0 copy-done.1
  657.2 0.0 slice-start.1
  657.3 5.3 convert_add_fusion
  662.6 0.0 slice-done
  662.6 0.0 slice-done.1
  662.6 0.0 copy-start
  662.6 5.4 bitcast_convert_fusion
  668.0 0.0 copy-done
  668.0 0.0 copy-start.4
  668.0 0.0 copy-start.3
  668.0 0.0 copy-start.2
  668.0 4.4 bitcast_convert_fusion.1
  672.5 0.0 copy-done.4
  672.5 0.6 slice_bitcast_fusion
  673.1 0.6 dynamic-slice_bitcast_fusion.1
  673.7 0.6 slice_bitcast_fusion.1
  674.3 0.0 copy-done.3
  674.3 0.8 copy.26
  675.1 0.0 copy-done.2
  675.1 1.0 copy.27
  (5 shorter events, 0.0 us)
Async XLA Ops:
  651.8 5.4 copy-start.1
  655.6 7.0 %slice-start = ((s8[5242880]{0:T(1024)(128)(4,1)}), s8[4194304]{0:T(1024)(128)(4,1)S(1)}, s32[]{:S(2)}) async-start(s8[5242880]{0:T(1024)(128)(4,1)} %bitcast.36), calls=%async_computation | async-start | bytes 8388608
  657.2 5.3 slice-start.1
  662.6 5.5 copy-start
  668.0 4.5 copy-start.4
  668.0 6.3 copy-start.3
  668.0 7.1 %copy-start.2 = (f32[128,2048]{1,0:T(8,128)S(1)}, f32[128,2048]{1,0:T(8,128)}, u32[]{:S(2)}) copy-start(f32[128,2048]{1,0:T(8,128)} %get-tuple-element.101) | copy-start | bytes 3145732
